TPU v7x, 32 devices: a whole 2x2x4 slice. The times are simulated.
32 devices in a mesh: mem: 16 (over z, y, x), lat: 2 (over core).
Axes of the slice: x: 2, y: 2, z: 4, core: 2. Of those that a mesh axis runs over, the one named last changes fastest.
Arguments:
- ensemble: bfloat16 [16, 4, 64, 8, 512], P('mem', None, 'lat')
- weights: float32 [16, 64, 8, 512], P('mem', 'lat')
- obs_cell: int32 [4, 16384], P(None, 'lat'), may hold values from 0 to 262143, as said below
- innovation: float32 [4, 16384], P(None, 'lat'), may hold values from -6 to 6
- obs_weight: float32 [4, 16384], P(None, 'lat'), may hold values from 1 to 10
- quality: int32 [4, 16384], P(None, 'lat'), may hold values 0 or 1
Outputs:
- new_weights: float32 [16, 64, 8, 512], P('mem', 'lat')
- cost: float32 [], replicated
Inputs may be any that keep to these rules, and one draw needn't show every extreme that they name: `obs_cell`: columns b * 8192 to (b + 1) * 8192 - 1 name cells in latitude rows b * 32 to (b + 1) * 32 - 1; cells may repeat.
All inputs are finite; a program needn't handle non-finite values. No bound on the sum of `quality` on one device may be relied on, other than what follows from the above.
Results may differ from a plain program's by a relative error of at most 0.0003.
Values sent between devices are 32-bit elements; how exact they have to be, the bound alone decides.
No kernel may reach another device: no remote copies, remote signals or barrier semaphores. Data moves between devices by JAX's collectives and lax.ppermute only.
A program may use at most 64 MiB of HBM per device.

v0:
```python
import math

import jax
import jax.numpy as jnp
from jax import lax
from jax.sharding import PartitionSpec as P

HALF = 8


STEP_LENGTH = 0.5
EPSILON = 1e-06


def extended(block, sides, width):
    for axis, dim in sides:
        count = lax.axis_size(axis)
        forward = [(i, i + 1) for i in range(count - 1)]
        backward = [(target, source) for source, target in forward]
        low = lax.ppermute(
            lax.slice_in_dim(block, block.shape[dim] - width, None, axis=dim), axis, forward
        )
        high = lax.ppermute(lax.slice_in_dim(block, 0, width, axis=dim), axis, backward)
        block = jnp.concatenate([low, block, high], axis=dim)
    return block


def tap_values(offset):
    sigma = HALF / 2.0
    every = jnp.arange(-HALF, HALF + 1).astype(jnp.float32)
    normal = jnp.sqrt(jnp.sum(jnp.exp(-((every / sigma) ** 2))))
    return jnp.exp(-0.5 * (offset / sigma) ** 2) / normal


def band_matrix(row_count):
    row_ids = jnp.arange(row_count)[:, None]
    col_ids = jnp.arange(row_count + 2 * HALF)[None, :]
    offset = (col_ids - row_ids - HALF).astype(jnp.float32)
    return jnp.where(jnp.abs(offset) <= HALF, tap_values(offset), 0.0)


def circulant(lon_count):
    source = jnp.arange(lon_count)[:, None]
    target = jnp.arange(lon_count)[None, :]
    offset = ((target - source + HALF) % lon_count - HALF).astype(jnp.float32)
    return jnp.where(jnp.abs(offset) <= HALF, tap_values(offset), 0.0)


def smooth(padded, row_count):
    mixed = jnp.einsum(
        "ij,mjln->miln", band_matrix(row_count), padded, precision=lax.Precision.HIGHEST
    )
    lon_count = mixed.shape[-1]
    shaped = mixed.reshape(-1, lon_count)
    result = jnp.dot(
        shaped,
        circulant(lon_count),
        precision=lax.Precision.HIGHEST,
        preferred_element_type=jnp.float32,
    )
    return result.reshape(mixed.shape)


def local(ensemble, weights, obs_cell, innovation, obs_weight, quality):
    mem_count, row_count, level_count, lon_count = weights.shape
    slot_count = ensemble.shape[1]
    members = mem_count * lax.axis_size("mem")
    norm_scale = 1.0 / math.sqrt(members - 1)
    band_cells = row_count * level_count * lon_count
    padded = extended(weights, (("lat", 1),), HALF)
    local_weights = smooth(padded, row_count)
    partial_value = ensemble[0] * local_weights[0][None]
    partial_value = partial_value.reshape(slot_count, band_cells)
    offset = obs_cell - lax.axis_index("lat") * band_cells
    keep_weight = quality.astype(jnp.float32) * obs_weight
    slot_ids = jnp.broadcast_to(jnp.arange(slot_count, dtype=jnp.int32)[:, None], obs_cell.shape)
    picked = jnp.take_along_axis(partial_value, offset, axis=1)
    observed = lax.psum(picked, "mem") * norm_scale
    resid = observed - innovation
    weighted = keep_weight * resid
    grad_increment = (
        jnp.zeros((slot_count, band_cells), jnp.float32).at[slot_ids, offset].add(weighted)
    )
    obs_term = jnp.sum(weighted * resid) / lax.axis_size("mem")
    prior_term = jnp.sum(weights * weights)
    prior_total, obs_total = lax.psum((prior_term, obs_term), ("mem", "lat"))
    grad_fields = grad_increment.reshape(slot_count, row_count, level_count, lon_count)
    back_terms = jnp.stack([jnp.sum(ensemble[0] * grad_fields, axis=0)]) * norm_scale
    padded_back = extended(back_terms, (("lat", 1),), HALF)
    grad = weights + smooth(padded_back, row_count)
    square_term = jnp.sum(grad * grad)
    grad_total = lax.psum(square_term, ("mem", "lat"))
    entries = jnp.float32(members * row_count * lax.axis_size("lat") * level_count * lon_count)
    cost = (0.5 * prior_total + 0.5 * obs_total) / entries
    length = jnp.sqrt(grad_total / entries + EPSILON)
    new_weights = weights - STEP_LENGTH * grad / length
    return (new_weights, cost)


def solution(mesh):
    placed = (
        P("mem", None, "lat", None, None),
        P("mem", "lat", None, None),
        P(None, "lat"),
        P(None, "lat"),
        P(None, "lat"),
        P(None, "lat"),
    )
    return jax.shard_map(
        local,
        mesh=mesh,
        in_specs=placed,
        out_specs=(P("mem", "lat", None, None), P()),
        check_vma=False,
    )
```

profile of v0, /device:TPU:0, one launch (start us, length us, event | category | flops | bytes accessed | tf_op | source)
XLA Modules:
  0.0 644.8 jit_solution(1959875832454271507)
XLA Ops:
  7.2 1.4 copy.13
  8.7 2.4 collective-permute-start
  11.1 1.3 collective-permute-start.1
  12.4 0.6 exponential_reduce_fusion
  13.7 1.0 or_bitcast_fusion
  14.7 2.8 reshape.78
  17.9 0.7 convolution_bitcast_fusion.3
  18.6 2.0 convolution_bitcast_fusion.2
  20.8 0.5 broadcast_multiply_fusion
  21.4 275.7 %gather_fusion = f32[32768]{0:T(1024)S(1)} fusion(f32[4,131072]{1,0:T(4,128)S(1)} %broadcast_multiply_fusion, s32[32768]{0:T(1024)S(1)} %bitcast.52), kind=kCustom, calls=%fused_computation | custom fusion | bytes 524288 | tf_op jit(solution)/shard_map/jit(take_along_axis)/gather | solution.py:77
  297.1 0.7 and_select_fusion
  297.9 107.1 %all-reduce.3.cloned.1.call-done = f32[4,8192]{1,0:T(4,128)} async-done(((f32[4,8192]{1,0:T(4,128)}), f32[4,8192]{1,0:T(4,128)}) %all-reduce.3.cloned.1.call-update) | async-done | bytes 131088 | tf_op jit(solution)/shard_map/psum | solution.py:78
  405.1 1.6 multiply_reduce_fusion.4
  406.7 172.5 %scatter_custom_fusion = f32[524288]{0:T(1024)} fusion(s32[32768]{0:T(1024)S(1)} %bitcast.54, f32[32768]{0:T(1024)S(1)} %bitcast.55, f32[]{:T(128)} %constant.28.clone.1), kind=kCustom, calls=%fused_computation.16 | custom fusion | flops 32768 | bytes 2097156
  579.1 4.0 reshape.77
  583.1 3.2 multiply_reduce_fusion
  586.5 0.3 copy.17
  586.8 1.3 collective-permute-start.2
  588.1 1.5 collective-permute-start.3
  589.6 0.7 multiply_reduce_fusion.1
  591.7 0.7 convolution_bitcast_fusion.1
  592.3 2.7 multiply_reduce_fusion.2
  595.0 39.6 %all-reduce = (f32[]{:T(128)}, f32[]{:T(128)}) all-reduce(f32[]{:T(128)} %get-tuple-element.12, f32[]{:T(128)S(6)} %mul.93), channel_id=1, replica_groups=mesh['mem'=16,'lat'=2] {'mem','lat'}, use_global_device_ids=true, to_apply=%region_5.6 | all-reduce | flops 2 | bytes 16 | tf_op jit(solution)/shard_map/psum | solution.py:92
  635.9 0.9 divide_subtract_fusion
  (39 shorter events, 0.9 us)
Async XLA Ops:
  7.2 7.5 %copy-start.3 = (bf16[1,4,32,8,512]{4,3,2,1,0:T(8,128)(2,1)S(1)}, bf16[1,4,32,8,512]{4,3,2,1,0:T(8,128)(2,1)}, u32[]{:S(2)}) copy-start(bf16[1,4,32,8,512]{4,3,2,1,0:T(8,128)(2,1)} %param.6) | copy-start | bytes 3145732
  7.2 397.9 %all-reduce.3.cloned.1.call-start = ((), (), s32[]{:S(2)}) async-start(), calls=%async_computation | async-start | bytes 262144 | tf_op jit(solution)/shard_map/psum | solution.py:78
  8.7 8.9 %copy-start.9 = (s32[2]{0:T(128)S(1)}, s32[2]{0:T(128)}, u32[]{:S(2)}) copy-start(s32[2]{0:T(128)} %constant.84) | copy-start | bytes 28
  8.7 9.2 %collective-permute-start = (f32[1,8,8,512]{3,1,2,0:T(8,128)S(1)}, f32[1,8,8,512]{3,1,2,0:T(8,128)S(1)}, u32[]{:S(2)}, u32[]{:S(2)}) collective-permute-start(f32[1,8,8,512]{3,1,2,0:T(8,128)S(1)} %get-tuple-element.10), channel_id=1, source_target_pairs={{0,1},{2,3},{4,5},{6,7},{8,9},{10,11},{12,13},{14,15},{16,17},{18,... | collective-permute-start | bytes 393224 | tf_op jit(solution)/shard_map/ppermute | solution.py:20
  11.1 6.9 %collective-permute-start.1 = (f32[1,8,8,512]{3,1,2,0:T(8,128)S(1)}, f32[1,8,8,512]{3,1,2,0:T(8,128)S(1)}, u32[]{:S(2)}, u32[]{:S(2)}) collective-permute-start(f32[1,8,8,512]{3,1,2,0:T(8,128)S(1)} %get-tuple-element.11), channel_id=1, source_target_pairs={{1,0},{3,2},{5,4},{7,6},{9,8},{11,10},{13,12},{15,14},{17,16},{19,... | collective-permute-start | bytes 393224 | tf_op jit(solution)/shard_map/ppermute | solution.py:23
  13.7 4.0 copy-start.8
  18.6 2.1 copy-start
  21.3 275.8 %copy-start.4 = (s32[4,8192]{1,0:T(4,128)S(1)}, s32[4,8192]{1,0:T(4,128)}, u32[]{:S(2)}) copy-start(s32[4,8192]{1,0:T(4,128)} %param.8) | copy-start | bytes 393220
  21.3 383.7 %copy-start.5 = (f32[4,8192]{1,0:T(4,128)S(1)}, f32[4,8192]{1,0:T(4,128)}, u32[]{:S(2)}) copy-start(f32[4,8192]{1,0:T(4,128)} %param.10) | copy-start | bytes 393220
  21.3 383.7 %copy-start.6 = (s32[4,8192]{1,0:T(4,128)S(1)}, s32[4,8192]{1,0:T(4,128)}, u32[]{:S(2)}) copy-start(s32[4,8192]{1,0:T(4,128)} %param.11) | copy-start | bytes 393220
  21.4 383.7 %copy-start.7 = (f32[4,8192]{1,0:T(4,128)S(1)}, f32[4,8192]{1,0:T(4,128)}, u32[]{:S(2)}) copy-start(f32[4,8192]{1,0:T(4,128)} %param.9) | copy-start | bytes 393220
  579.1 4.0 copy-start.1
  586.3 3.3 copy-start.2
  586.8 4.8 collective-permute-start.2
  588.1 3.5 collective-permute-start.3
Sparse Core Ops, SparseCore 0:
  298.0 107.0 all-reduce.2
where the time goes:
time: 645 us
  local copies, waits for them, and re-layouts  285 us (44%)
  other arithmetic  182 us (28%)
  waiting for transfers between devices  107 us (17%)
  blocking collectives  39.6 us (6%)
  between operations  18.8 us (3%)
  starting transfers between devices  6.46 us (1%)
    gather x2, local copies, waits for them, and re-layouts, local(): picked = jnp.take_along_axis(partial_value, offset, axis=1)  276 us
    unnamed x5, other arithmetic  174 us
    psum x1, waiting for transfers between devices, local(): observed = lax.psum(picked, 'mem') * norm_scale  107 us
    psum x1, blocking collectives, local(): grad_total = lax.psum(square_term, ('mem', 'lat'))  39.6 us
  transfers between devices with their start and end apart: 5, of which 1 were waited for; matrix products, arithmetic and copies ran while one was open for 1% of the time, Pallas kernels for 0%

commit v1 on v0

v1 whole, which is shorter than its diff:
```python
import functools
import math

import jax
import jax.numpy as jnp
import numpy as np
from jax import lax
from jax.experimental import pallas as pl
from jax.experimental.pallas import tpu as pltpu
from jax.sharding import PartitionSpec as P

HALF = 8
STEP_LENGTH = 0.5
EPSILON = 1e-06
TILE = 512
MIB = 1024 * 1024


def taps():
    sigma = HALF / 2.0
    every = np.arange(-HALF, HALF + 1).astype(np.float64)
    normal = np.sqrt(np.sum(np.exp(-((every / sigma) ** 2))))
    return np.exp(-0.5 * (every / sigma) ** 2) / normal


def circulant_parts(lon_count):
    full = np.zeros((lon_count, lon_count), np.float32)
    at = np.arange(lon_count)
    for shift_by, tap in zip(range(-HALF, HALF + 1), taps()):
        full[at, (at + shift_by) % lon_count] += np.float32(tap)
    high = full.astype(jnp.bfloat16)
    low = (full - high.astype(np.float32)).astype(jnp.bfloat16)
    return high, low


def two_parts(value):
    high = value.astype(jnp.bfloat16)
    low = (value - high.astype(jnp.float32)).astype(jnp.bfloat16)
    return high, low


def smooth_rows(low, own, high):
    tap = [float(t) for t in taps()]
    padded = jnp.concatenate([low, own, high], axis=0)
    rows = own.shape[0]
    total = padded[HALF : HALF + rows] * tap[HALF]
    for away in range(1, HALF + 1):
        pair = padded[HALF - away : HALF - away + rows] + padded[HALF + away : HALF + away + rows]
        total = total + pair * tap[HALF + away]
    return total


def smooth_lons(field, circ_high, circ_low):
    first, second = two_parts(field)
    dot = functools.partial(jnp.dot, preferred_element_type=jnp.float32)
    return dot(first, circ_high) + (dot(second, circ_high) + dot(first, circ_low))


def split_cell(cell, lon_count, lane_count):
    lon = lax.rem(cell, lon_count)
    return lax.div(cell, lon_count), lax.div(lon, lane_count), lax.rem(lon, lane_count)


def pick_kernel(low_ref, own_ref, high_ref, circ_high_ref, circ_low_ref, ens_ref, cell_ref, out_ref, local_ref, lhs_ref):
    rows, levels, lons = own_ref.shape
    slots = ens_ref.shape[0]
    keys = rows * levels
    lanes = 256
    halves = lons // lanes
    mixed = smooth_rows(low_ref[...], own_ref[...], high_ref[...]).reshape(keys, lons)
    local_ref[...] = smooth_lons(mixed, circ_high_ref[...], circ_low_ref[...])
    count = cell_ref.shape[1]
    key_ids = lax.broadcasted_iota(jnp.int32, (keys, TILE), 0)
    lane_ids = lax.broadcasted_iota(jnp.int32, (lanes, TILE), 0)
    for slot in range(slots):
        field = ens_ref[slot].reshape(keys, lons).astype(jnp.float32) * local_ref[...]
        first, second = two_parts(field.T)
        for half in range(halves):
            lhs_ref[:, pl.ds(half * keys, keys)] = first[half * lanes : (half + 1) * lanes]
            lhs_ref[:, pl.ds((halves + half) * keys, keys)] = second[half * lanes : (half + 1) * lanes]

        @pl.loop(0, count // TILE)
        def _(step):
            here = pl.ds(pl.multiple_of(step * TILE, TILE), TILE)
            key, half_of, lane = split_cell(cell_ref[pl.ds(slot, 1), here], lons, lanes)
            hots = []
            for half in range(halves):
                wanted = jnp.where(half_of == half, key, -1)
                hots.append((key_ids == wanted).astype(jnp.bfloat16))
            hot = jnp.concatenate(hots + hots, axis=0)
            found = jnp.dot(lhs_ref[...], hot, preferred_element_type=jnp.float32)
            out_ref[pl.ds(slot, 1), here] = jnp.sum(jnp.where(lane_ids == lane, found, 0.0), axis=0, keepdims=True)


def scatter_kernel(norm_scale, seen_ref, innov_ref, weight_ref, quality_ref, cell_ref, ens_ref, back_ref, cost_ref, acc_ref):
    slots, rows, levels, lons = ens_ref.shape
    keys = rows * levels
    lanes = 256
    halves = lons // lanes
    count = cell_ref.shape[1]
    key_ids = lax.broadcasted_iota(jnp.int32, (keys, TILE), 0)
    lane_ids = lax.broadcasted_iota(jnp.int32, (lanes, TILE), 0)
    resid = seen_ref[...] * norm_scale - innov_ref[...]
    keep = quality_ref[...].astype(jnp.float32) * weight_ref[...]
    cost_ref[...] = jnp.sum(keep * resid * resid).reshape(1, 1)
    for slot in range(slots):
        acc_ref[...] = jnp.zeros_like(acc_ref)

        @pl.loop(0, count // TILE)
        def _(step):
            here = pl.ds(pl.multiple_of(step * TILE, TILE), TILE)
            at = (pl.ds(slot, 1), here)
            key, half_of, lane = split_cell(cell_ref[at], lons, lanes)
            resid = seen_ref[at] * norm_scale - innov_ref[at]
            wres = quality_ref[at].astype(jnp.float32) * weight_ref[at] * resid
            first, second = two_parts(wres)
            chosen = lane_ids == lane
            placed = jnp.concatenate(
                [
                    jnp.where(chosen, first.astype(jnp.float32), 0.0).astype(jnp.bfloat16),
                    jnp.where(chosen, second.astype(jnp.float32), 0.0).astype(jnp.bfloat16),
                ],
                axis=1,
            )
            hots = []
            for half in range(halves):
                wanted = jnp.where(half_of == half, key, -1)
                hots.append((key_ids == wanted).astype(jnp.bfloat16))
            hot = jnp.concatenate(hots, axis=0)
            hot = jnp.concatenate([hot, hot], axis=1)
            acc_ref[...] += lax.dot_general(
                hot, placed, (((1,), (1,)), ((), ())), preferred_element_type=jnp.float32
            )

        grad = jnp.concatenate([acc_ref[pl.ds(h * keys, keys), :] for h in range(halves)], axis=1)
        term = ens_ref[slot].reshape(keys, lons).astype(jnp.float32) * grad
        term = term.reshape(rows, levels, lons)
        back_ref[...] = term if slot == 0 else back_ref[...] + term
    back_ref[...] *= norm_scale


def grad_kernel(low_ref, own_ref, high_ref, circ_high_ref, circ_low_ref, weights_ref, obs_cost_ref, grad_ref, sums_ref):
    rows, levels, lons = own_ref.shape
    mixed = smooth_rows(low_ref[...], own_ref[...], high_ref[...]).reshape(rows * levels, lons)
    weights = weights_ref[...].reshape(rows * levels, lons)
    grad = weights + smooth_lons(mixed, circ_high_ref[...], circ_low_ref[...])
    grad_ref[...] = grad.reshape(grad_ref.shape)
    lane = lax.broadcasted_iota(jnp.int32, sums_ref.shape, 1)
    prior = jnp.sum(weights * weights)
    square = jnp.sum(grad * grad)
    sums_ref[...] = jnp.where(lane == 0, square, jnp.where(lane == 1, prior, jnp.where(lane == 2, obs_cost_ref[...], 0.0)))


def call(body, out_shape, scratch, flops, *operands):
    vmem = pl.BlockSpec(memory_space=pltpu.VMEM)
    return pl.pallas_call(
        body,
        out_shape=out_shape,
        in_specs=[vmem] * len(operands),
        out_specs=jax.tree.map(lambda _: vmem, out_shape),
        scratch_shapes=scratch,
        compiler_params=pltpu.CompilerParams(vmem_limit_bytes=48 * MIB),
        cost_estimate=pl.CostEstimate(flops=flops, bytes_accessed=2 * MIB, transcendentals=0),
    )(*operands)


def edges(field):
    count = lax.axis_size("lat")
    forward = [(i, i + 1) for i in range(count - 1)]
    backward = [(target, source) for source, target in forward]
    low = lax.ppermute(field[-HALF:], "lat", forward)
    high = lax.ppermute(field[:HALF], "lat", backward)
    return low, high


def summed(value, axis):
    count = lax.axis_size(axis)
    if count & (count - 1):
        return lax.psum(value, axis)
    away = 1
    while away < count:
        value = value + lax.ppermute(value, axis, [(i, i ^ away) for i in range(count)])
        away *= 2
    return value


def local(ensemble, weights, obs_cell, innovation, obs_weight, quality):
    _, rows, levels, lons = weights.shape
    slots, obs = obs_cell.shape
    members = lax.axis_size("mem")
    lat_count = lax.axis_size("lat")
    norm_scale = 1.0 / math.sqrt(members - 1)
    cells = rows * levels * lons
    ens, own = ensemble[0], weights[0]
    offset = lax.rem(obs_cell, cells)
    circ_high, circ_low = (jnp.asarray(part) for part in circulant_parts(lons))
    f32 = jnp.float32
    low, high = edges(own)
    picked = call(
        pick_kernel,
        jax.ShapeDtypeStruct((slots, obs), f32),
        [pltpu.VMEM((rows * levels, lons), f32), pltpu.VMEM((256, 2 * cells // 256), jnp.bfloat16)],
        4 * slots * obs * cells,
        low, own, high, circ_high, circ_low, ens, offset,
    )
    seen = summed(picked, "mem")
    back, obs_cost = call(
        functools.partial(scatter_kernel, norm_scale),
        (jax.ShapeDtypeStruct((rows, levels, lons), f32), jax.ShapeDtypeStruct((1, 1), f32)),
        [pltpu.VMEM((cells // 256, 256), f32)],
        4 * slots * obs * cells,
        seen, innovation, obs_weight, quality, offset, ens,
    )
    back_low, back_high = edges(back)
    grad, sums = call(
        grad_kernel,
        (jax.ShapeDtypeStruct((rows, levels, lons), f32), jax.ShapeDtypeStruct((1, 128), f32)),
        [],
        10**9,
        back_low, back, back_high, circ_high, circ_low, own, obs_cost,
    )
    totals = summed(summed(sums, "lat"), "mem")
    entries = f32(members * lat_count * cells)
    cost = (0.5 * totals[0, 1] + 0.5 * totals[0, 2] / members) / entries
    length = jnp.sqrt(totals[0, 0] / entries + EPSILON)
    new_weights = own - STEP_LENGTH * grad / length
    return new_weights[None], cost


def solution(mesh):
    placed = (
        P("mem", None, "lat", None, None),
        P("mem", "lat", None, None),
        P(None, "lat"),
        P(None, "lat"),
        P(None, "lat"),
        P(None, "lat"),
    )
    return jax.shard_map(
        local,
        mesh=mesh,
        in_specs=placed,
        out_specs=(P("mem", "lat", None, None), P()),
        check_vma=False,
    )
```

time: 645 us -> 130 us (0.20)
  local copies, waits for them, and re-layouts: 285 us -> 5.06 us
  other arithmetic: 182 us -> 2.01 us
  waiting for transfers between devices: 107 us -> 26.6 us
  Pallas kernels: 0 us -> 68.1 us
  blocking collectives: 39.6 us -> 0 us
  starting transfers between devices: 6.46 us -> 24.2 us
  between operations: 18.8 us -> 4 us
    gather x2 -> x0, local copies, waits for them, and re-layouts: 276 us -> none  [local(): picked = jnp.take_along_axis(partial_value, offset, axis=1)]
    unnamed x5 -> x0, other arithmetic: 174 us -> none
    psum x1 -> x0, waiting for transfers between devices: 107 us -> none  [local(): observed = lax.psum(picked, 'mem') * norm_scale]
    pallas_call x0 -> x3, Pallas kernels: none -> 68.1 us  [call(): pl.pallas_call(body, out_shape=out_shape, in_specs=[vmem] * len(operands)...]
    psum x1 -> x0, blocking collectives: 39.6 us -> none  [local(): grad_total = lax.psum(square_term, ('mem', 'lat'))]
    ppermute x4 -> x13, waiting for transfers between devices: 0.01 us -> 26.6 us  [the longest x9 25.6 us: summed(): lax.ppermute(value, axis, [(i, i ^ away) for i in range(count)])]
    ppermute x4 -> x13, starting transfers between devices: 6.43 us -> 24.2 us  [the longest x9 15.4 us: summed(): lax.ppermute(value, axis, [(i, i ^ away) for i in range(count)])]
  transfers between devices with their start and end apart: 5 -> 13, of which waited for: 1 -> 10; matrix products, arithmetic and copies ran while one was open for 1% -> 1% of each run, Pallas kernels for 0% -> 0%
where the time goes in v1:
time: 130 us
  Pallas kernels  68.1 us (52%)
  waiting for transfers between devices  26.6 us (20%)
  starting transfers between devices  24.2 us (19%)
  local copies, waits for them, and re-layouts  5.06 us (4%)
  between operations  4 us (3%)
  other arithmetic  2.01 us (2%)
    pallas_call x3, Pallas kernels, call(): pl.pallas_call(body, out_shape=out_shape, in_specs=[vmem] * len(operands)...  68.1 us
    ppermute x9, waiting for transfers between devices, summed(): lax.ppermute(value, axis, [(i, i ^ away) for i in range(count)])  25.6 us
    ppermute x9, starting transfers between devices, summed(): lax.ppermute(value, axis, [(i, i ^ away) for i in range(count)])  15.4 us
    ppermute x2, starting transfers between devices, edges(): low = lax.ppermute(field[-HALF:], 'lat', forward)  6.08 us
    unnamed x20, local copies, waits for them, and re-layouts  3.35 us
    ppermute x2, starting transfers between devices, edges(): high = lax.ppermute(field[:HALF], 'lat', backward)  2.72 us
  transfers between devices with their start and end apart: 13, of which 10 were waited for; matrix products, arithmetic and copies ran while one was open for 1% of the time, Pallas kernels for 0%

profile of v1, /device:TPU:0, one launch (start us, length us, event | category | flops | bytes accessed | tf_op | source)
XLA Modules:
  0.0 129.9 jit_solution(11305253134086752746)
XLA Ops:
  0.6 1.0 slice_bitcast_fusion
  1.7 1.3 collective-permute-start.1
  3.0 3.0 %collective-permute-start = (f32[8,8,512]{2,1,0:T(8,128)S(1)}, f32[8,8,512]{2,1,0:T(8,128)S(1)}, u32[]{:S(2)}, u32[]{:S(2)}) collective-permute-start(f32[8,8,512]{2,1,0:T(8,128)S(1)} %get-tuple-element.13), channel_id=1, source_target_pairs={{0,1},{2,3},{4,5},{6,7},{8,9},{10,11},{12,13},{14,15},{16,17},{18,... | collective-permute-start | bytes 393224 | tf_op jit(solution)/shard_map/ppermute | solution.py:171
  7.0 1.2 copy-done.1
  10.3 34.0 %shard_map.95 = f32[4,8192]{1,0:T(4,128)S(1)} custom-call(f32[8,8,512]{2,1,0:T(8,128)S(1)} %collective-permute-done.low_ref, f32[32,8,512]{2,1,0:T(8,128)S(1)} %bitcast.11, f32[8,8,512]{2,1,0:T(8,128)S(1)} %collective-permute-done.1.high_ref, bf16[512,512]{1,0:T(8,128)(2,1)S(1)} %copy-done.8, bf16[512,512]{1,0:T(8,128)(2,1)S(1)} %copy-done.6, ...), custom_call_target="tpu_custom_call" | custom-call | flops 17179869184 | bytes 2097152 | tf_op jit(solution)/shard_map/pallas_call | solution.py:156
  44.3 3.0 %collective-permute-start.2 = (f32[4,8192]{1,0:T(4,128)S(1)}, f32[4,8192]{1,0:T(4,128)S(1)}, u32[]{:S(2)}, u32[]{:S(2)}) collective-permute-start(f32[4,8192]{1,0:T(4,128)S(1)} %shard_map.95), channel_id=1, source_target_pairs={{0,2},{2,0},{4,6},{6,4},{8,10},{10,8},{12,14},{14,12},{16,18},{18,... | collective-permute-start | bytes 393224 | tf_op jit(solution)/shard_map/ppermute | solution.py:182
  47.3 4.0 %collective-permute-done.2 = f32[4,8192]{1,0:T(4,128)S(1)} collective-permute-done((f32[4,8192]{1,0:T(4,128)S(1)}, f32[4,8192]{1,0:T(4,128)S(1)}, u32[]{:S(2)}, u32[]{:S(2)}) %collective-permute-start.2) | collective-permute-done | bytes 131104 | tf_op jit(solution)/shard_map/ppermute | solution.py:182
  51.4 1.8 %collective-permute-start.3 = (f32[4,8192]{1,0:T(4,128)S(1)}, f32[4,8192]{1,0:T(4,128)S(1)}, u32[]{:S(2)}, u32[]{:S(2)}) collective-permute-start(f32[4,8192]{1,0:T(4,128)S(1)} %add.35), channel_id=1, source_target_pairs={{0,4},{2,6},{4,0},{6,2},{8,12},{10,14},{12,8},{14,10},{16,20},{18,... | collective-permute-start | bytes 393224 | tf_op jit(solution)/shard_map/ppermute | solution.py:182
  53.2 3.5 %collective-permute-done.3 = f32[4,8192]{1,0:T(4,128)S(1)} collective-permute-done((f32[4,8192]{1,0:T(4,128)S(1)}, f32[4,8192]{1,0:T(4,128)S(1)}, u32[]{:S(2)}, u32[]{:S(2)}) %collective-permute-start.3) | collective-permute-done | bytes 131104 | tf_op jit(solution)/shard_map/ppermute | solution.py:182
  56.7 1.6 %collective-permute-start.4 = (f32[4,8192]{1,0:T(4,128)S(1)}, f32[4,8192]{1,0:T(4,128)S(1)}, u32[]{:S(2)}, u32[]{:S(2)}) collective-permute-start(f32[4,8192]{1,0:T(4,128)S(1)} %add.36), channel_id=1, source_target_pairs={{0,8},{2,10},{4,12},{6,14},{8,0},{10,2},{12,4},{14,6},{16,24},{18,... | collective-permute-start | bytes 393224 | tf_op jit(solution)/shard_map/ppermute | solution.py:182
  58.3 3.4 %collective-permute-done.4 = f32[4,8192]{1,0:T(4,128)S(1)} collective-permute-done((f32[4,8192]{1,0:T(4,128)S(1)}, f32[4,8192]{1,0:T(4,128)S(1)}, u32[]{:S(2)}, u32[]{:S(2)}) %collective-permute-start.4) | collective-permute-done | bytes 131104 | tf_op jit(solution)/shard_map/ppermute | solution.py:182
  61.8 2.7 %collective-permute-start.5 = (f32[4,8192]{1,0:T(4,128)S(1)}, f32[4,8192]{1,0:T(4,128)S(1)}, u32[]{:S(2)}, u32[]{:S(2)}) collective-permute-start(f32[4,8192]{1,0:T(4,128)S(1)} %add.37), channel_id=1, source_target_pairs={{0,16},{2,18},{4,20},{6,22},{8,24},{10,26},{12,28},{14,30},{16,0},... | collective-permute-start | bytes 393224 | tf_op jit(solution)/shard_map/ppermute | solution.py:182
  64.6 4.6 %collective-permute-done.5 = f32[4,8192]{1,0:T(4,128)S(1)} collective-permute-done((f32[4,8192]{1,0:T(4,128)S(1)}, f32[4,8192]{1,0:T(4,128)S(1)}, u32[]{:S(2)}, u32[]{:S(2)}) %collective-permute-start.5) | collective-permute-done | bytes 131104 | tf_op jit(solution)/shard_map/ppermute | solution.py:182
  69.3 32.4 %shard_map.96 = (f32[32,8,512]{2,1,0:T(8,128)S(1)}, f32[1,1]{1,0:T(1,128)}) custom-call(f32[4,8192]{1,0:T(4,128)S(1)} %add.38.seen_ref, f32[4,8192]{1,0:T(4,128)S(1)} %copy-done.3, f32[4,8192]{1,0:T(4,128)S(1)} %copy-done.4, s32[4,8192]{1,0:T(4,128)S(1)} %copy-done.5, s32[4,8192]{1,0:T(4,128)S(1)} %negate_select_fusion.cell_ref, ...), custom_call_target="tpu_custom_call" | custom-call | flops 17179869184 | bytes 2097152 | tf_op jit(solution)/shard_map/pallas_call | solution.py:156
  101.7 1.4 %collective-permute-start.7 = (f32[8,8,512]{2,1,0:T(8,128)S(1)}, f32[8,8,512]{2,1,0:T(8,128)S(1)}, u32[]{:S(2)}, u32[]{:S(2)}) collective-permute-start(f32[8,8,512]{2,1,0:T(8,128)S(1)} %get-tuple-element.10), channel_id=1, source_target_pairs={{1,0},{3,2},{5,4},{7,6},{9,8},{11,10},{13,12},{15,14},{17,16},{19,... | collective-permute-start | bytes 393224 | tf_op jit(solution)/shard_map/ppermute | solution.py:172
  103.1 3.0 %collective-permute-start.6 = (f32[8,8,512]{2,1,0:T(8,128)S(1)}, f32[8,8,512]{2,1,0:T(8,128)S(1)}, u32[]{:S(2)}, u32[]{:S(2)}) collective-permute-start(f32[8,8,512]{2,1,0:T(8,128)S(1)} %get-tuple-element.11), channel_id=1, source_target_pairs={{0,1},{2,3},{4,5},{6,7},{8,9},{10,11},{12,13},{14,15},{16,17},{18,... | collective-permute-start | bytes 393224 | tf_op jit(solution)/shard_map/ppermute | solution.py:171
  107.1 1.7 %shard_map.97 = (f32[32,8,512]{2,1,0:T(8,128)S(1)}, f32[1,128]{1,0:T(1,128)S(1)}) custom-call(f32[8,8,512]{2,1,0:T(8,128)S(1)} %collective-permute-done.6.low_ref, f32[32,8,512]{2,1,0:T(8,128)S(1)} %get-tuple-element.6.own_ref, f32[8,8,512]{2,1,0:T(8,128)S(1)} %collective-permute-done.7.high_ref, bf16[512,512]{1,0:T(8,128)(2,1)S(1)} %copy-done.9, ...), custom_call_target="tpu_custom_call" | custom-call | flops 1000000000 | bytes 2097152 | tf_op jit(solution)/shard_map/pallas_call | solution.py:156
  110.1 1.5 %collective-permute-start.9 = (f32[1,128]{1,0:T(1,128)S(1)}, f32[1,128]{1,0:T(1,128)S(1)}, u32[]{:S(2)}, u32[]{:S(2)}) collective-permute-start(f32[1,128]{1,0:T(1,128)S(1)} %add.39), channel_id=1, source_target_pairs={{0,2},{2,0},{4,6},{6,4},{8,10},{10,8},{12,14},{14,12},{16,18},{18,... | collective-permute-start | bytes 1544 | tf_op jit(solution)/shard_map/ppermute | solution.py:182
  111.6 2.1 %collective-permute-done.9 = f32[1,128]{1,0:T(1,128)S(1)} collective-permute-done((f32[1,128]{1,0:T(1,128)S(1)}, f32[1,128]{1,0:T(1,128)S(1)}, u32[]{:S(2)}, u32[]{:S(2)}) %collective-permute-start.9) | collective-permute-done | bytes 544 | tf_op jit(solution)/shard_map/ppermute | solution.py:182
  113.7 1.5 %collective-permute-start.10 = (f32[1,128]{1,0:T(1,128)S(1)}, f32[1,128]{1,0:T(1,128)S(1)}, u32[]{:S(2)}, u32[]{:S(2)}) collective-permute-start(f32[1,128]{1,0:T(1,128)S(1)} %add.40), channel_id=1, source_target_pairs={{0,4},{2,6},{4,0},{6,2},{8,12},{10,14},{12,8},{14,10},{16,20},{18,... | collective-permute-start | bytes 1544 | tf_op jit(solution)/shard_map/ppermute | solution.py:182
  115.2 2.1 %collective-permute-done.10 = f32[1,128]{1,0:T(1,128)S(1)} collective-permute-done((f32[1,128]{1,0:T(1,128)S(1)}, f32[1,128]{1,0:T(1,128)S(1)}, u32[]{:S(2)}, u32[]{:S(2)}) %collective-permute-start.10) | collective-permute-done | bytes 544 | tf_op jit(solution)/shard_map/ppermute | solution.py:182
  118.0 2.8 %collective-permute-done.11 = f32[1,128]{1,0:T(1,128)S(1)} collective-permute-done((f32[1,128]{1,0:T(1,128)S(1)}, f32[1,128]{1,0:T(1,128)S(1)}, u32[]{:S(2)}, u32[]{:S(2)}) %collective-permute-start.11) | collective-permute-done | bytes 544 | tf_op jit(solution)/shard_map/ppermute | solution.py:182
  120.8 2.1 %collective-permute-start.12 = (f32[1,128]{1,0:T(1,128)S(1)}, f32[1,128]{1,0:T(1,128)S(1)}, u32[]{:S(2)}, u32[]{:S(2)}) collective-permute-start(f32[1,128]{1,0:T(1,128)S(1)} %add.42), channel_id=1, source_target_pairs={{0,16},{2,18},{4,20},{6,22},{8,24},{10,26},{12,28},{14,30},{16,0},... | collective-permute-start | bytes 1544 | tf_op jit(solution)/shard_map/ppermute | solution.py:182
  122.9 2.3 %collective-permute-done.12 = f32[1,128]{1,0:T(1,128)S(1)} collective-permute-done((f32[1,128]{1,0:T(1,128)S(1)}, f32[1,128]{1,0:T(1,128)S(1)}, u32[]{:S(2)}, u32[]{:S(2)}) %collective-permute-start.12) | collective-permute-done | bytes 544 | tf_op jit(solution)/shard_map/ppermute | solution.py:182
  (39 shorter events, 7.8 us)
Async XLA Ops:
  0.6 6.4 %copy-start = (f32[1,32,8,512]{3,2,1,0:T(8,128)S(1)}, f32[1,32,8,512]{3,2,1,0:T(8,128)}, u32[]{:S(2)}) copy-start(f32[1,32,8,512]{3,2,1,0:T(8,128)} %param.9) | copy-start | bytes 1572868
  1.7 5.3 %collective-permute-start.1 = (f32[8,8,512]{2,1,0:T(8,128)S(1)}, f32[8,8,512]{2,1,0:T(8,128)S(1)}, u32[]{:S(2)}, u32[]{:S(2)}) collective-permute-start(f32[8,8,512]{2,1,0:T(8,128)S(1)} %get-tuple-element.12), channel_id=1, source_target_pairs={{1,0},{3,2},{5,4},{7,6},{9,8},{11,10},{13,12},{15,14},{17,16},{19,... | collective-permute-start | bytes 393224 | tf_op jit(solution)/shard_map/ppermute | solution.py:172
  3.0 4.0 %collective-permute-start = (f32[8,8,512]{2,1,0:T(8,128)S(1)}, f32[8,8,512]{2,1,0:T(8,128)S(1)}, u32[]{:S(2)}, u32[]{:S(2)}) collective-permute-start(f32[8,8,512]{2,1,0:T(8,128)S(1)} %get-tuple-element.13), channel_id=1, source_target_pairs={{0,1},{2,3},{4,5},{6,7},{8,9},{10,11},{12,13},{14,15},{16,17},{18,... | collective-permute-start | bytes 393224 | tf_op jit(solution)/shard_map/ppermute | solution.py:171
  7.0 1.2 copy-start.1
  8.3 1.0 copy-start.6
  9.3 1.0 copy-start.8
  44.3 24.9 %copy-start.2 = (bf16[1,4,32,8,512]{4,3,2,1,0:T(8,128)(2,1)S(1)}, bf16[1,4,32,8,512]{4,3,2,1,0:T(8,128)(2,1)}, u32[]{:S(2)}) copy-start(bf16[1,4,32,8,512]{4,3,2,1,0:T(8,128)(2,1)} %param.8) | copy-start | bytes 3145732
  44.3 7.0 %collective-permute-start.2 = (f32[4,8192]{1,0:T(4,128)S(1)}, f32[4,8192]{1,0:T(4,128)S(1)}, u32[]{:S(2)}, u32[]{:S(2)}) collective-permute-start(f32[4,8192]{1,0:T(4,128)S(1)} %shard_map.95), channel_id=1, source_target_pairs={{0,2},{2,0},{4,6},{6,4},{8,10},{10,8},{12,14},{14,12},{16,18},{18,... | collective-permute-start | bytes 393224 | tf_op jit(solution)/shard_map/ppermute | solution.py:182
  51.4 5.3 %collective-permute-start.3 = (f32[4,8192]{1,0:T(4,128)S(1)}, f32[4,8192]{1,0:T(4,128)S(1)}, u32[]{:S(2)}, u32[]{:S(2)}) collective-permute-start(f32[4,8192]{1,0:T(4,128)S(1)} %add.35), channel_id=1, source_target_pairs={{0,4},{2,6},{4,0},{6,2},{8,12},{10,14},{12,8},{14,10},{16,20},{18,... | collective-permute-start | bytes 393224 | tf_op jit(solution)/shard_map/ppermute | solution.py:182
  56.7 5.0 %collective-permute-start.4 = (f32[4,8192]{1,0:T(4,128)S(1)}, f32[4,8192]{1,0:T(4,128)S(1)}, u32[]{:S(2)}, u32[]{:S(2)}) collective-permute-start(f32[4,8192]{1,0:T(4,128)S(1)} %add.36), channel_id=1, source_target_pairs={{0,8},{2,10},{4,12},{6,14},{8,0},{10,2},{12,4},{14,6},{16,24},{18,... | collective-permute-start | bytes 393224 | tf_op jit(solution)/shard_map/ppermute | solution.py:182
  61.8 7.4 %copy-start.3 = (f32[4,8192]{1,0:T(4,128)S(1)}, f32[4,8192]{1,0:T(4,128)}, u32[]{:S(2)}) copy-start(f32[4,8192]{1,0:T(4,128)} %innov_ref.1) | copy-start | bytes 393220
  61.8 7.4 %copy-start.4 = (f32[4,8192]{1,0:T(4,128)S(1)}, f32[4,8192]{1,0:T(4,128)}, u32[]{:S(2)}) copy-start(f32[4,8192]{1,0:T(4,128)} %weight_ref.1) | copy-start | bytes 393220
  61.8 7.4 %copy-start.5 = (s32[4,8192]{1,0:T(4,128)S(1)}, s32[4,8192]{1,0:T(4,128)}, u32[]{:S(2)}) copy-start(s32[4,8192]{1,0:T(4,128)} %quality_ref.1) | copy-start | bytes 393220
  61.8 7.3 %collective-permute-start.5 = (f32[4,8192]{1,0:T(4,128)S(1)}, f32[4,8192]{1,0:T(4,128)S(1)}, u32[]{:S(2)}, u32[]{:S(2)}) collective-permute-start(f32[4,8192]{1,0:T(4,128)S(1)} %add.37), channel_id=1, source_target_pairs={{0,16},{2,18},{4,20},{6,22},{8,24},{10,26},{12,28},{14,30},{16,0},... | collective-permute-start | bytes 393224 | tf_op jit(solution)/shard_map/ppermute | solution.py:182
  69.2 37.9 %copy-start.9 = (bf16[512,512]{1,0:T(8,128)(2,1)S(1)}, bf16[512,512]{1,0:T(8,128)(2,1)}, u32[]{:S(2)}) copy-start(bf16[512,512]{1,0:T(8,128)(2,1)} %constant.28.clone.circ_high_ref) | copy-start | bytes 1572868
  101.6 5.5 %copy-start.7 = (bf16[512,512]{1,0:T(8,128)(2,1)S(1)}, bf16[512,512]{1,0:T(8,128)(2,1)}, u32[]{:S(2)}) copy-start(bf16[512,512]{1,0:T(8,128)(2,1)} %constant.29.clone.circ_low_ref) | copy-start | bytes 1572868
  101.7 4.5 %collective-permute-start.7 = (f32[8,8,512]{2,1,0:T(8,128)S(1)}, f32[8,8,512]{2,1,0:T(8,128)S(1)}, u32[]{:S(2)}, u32[]{:S(2)}) collective-permute-start(f32[8,8,512]{2,1,0:T(8,128)S(1)} %get-tuple-element.10), channel_id=1, source_target_pairs={{1,0},{3,2},{5,4},{7,6},{9,8},{11,10},{13,12},{15,14},{17,16},{19,... | collective-permute-start | bytes 393224 | tf_op jit(solution)/shard_map/ppermute | solution.py:172
  103.1 4.0 %collective-permute-start.6 = (f32[8,8,512]{2,1,0:T(8,128)S(1)}, f32[8,8,512]{2,1,0:T(8,128)S(1)}, u32[]{:S(2)}, u32[]{:S(2)}) collective-permute-start(f32[8,8,512]{2,1,0:T(8,128)S(1)} %get-tuple-element.11), channel_id=1, source_target_pairs={{0,1},{2,3},{4,5},{6,7},{8,9},{10,11},{12,13},{14,15},{16,17},{18,... | collective-permute-start | bytes 393224 | tf_op jit(solution)/shard_map/ppermute | solution.py:171
  108.9 1.3 collective-permute-start.8
  110.1 3.5 %collective-permute-start.9 = (f32[1,128]{1,0:T(1,128)S(1)}, f32[1,128]{1,0:T(1,128)S(1)}, u32[]{:S(2)}, u32[]{:S(2)}) collective-permute-start(f32[1,128]{1,0:T(1,128)S(1)} %add.39), channel_id=1, source_target_pairs={{0,2},{2,0},{4,6},{6,4},{8,10},{10,8},{12,14},{14,12},{16,18},{18,... | collective-permute-start | bytes 1544 | tf_op jit(solution)/shard_map/ppermute | solution.py:182
  113.7 3.5 %collective-permute-start.10 = (f32[1,128]{1,0:T(1,128)S(1)}, f32[1,128]{1,0:T(1,128)S(1)}, u32[]{:S(2)}, u32[]{:S(2)}) collective-permute-start(f32[1,128]{1,0:T(1,128)S(1)} %add.40), channel_id=1, source_target_pairs={{0,4},{2,6},{4,0},{6,2},{8,12},{10,14},{12,8},{14,10},{16,20},{18,... | collective-permute-start | bytes 1544 | tf_op jit(solution)/shard_map/ppermute | solution.py:182
  117.2 3.5 %collective-permute-start.11 = (f32[1,128]{1,0:T(1,128)S(1)}, f32[1,128]{1,0:T(1,128)S(1)}, u32[]{:S(2)}, u32[]{:S(2)}) collective-permute-start(f32[1,128]{1,0:T(1,128)S(1)} %add.41), channel_id=1, source_target_pairs={{0,8},{2,10},{4,12},{6,14},{8,0},{10,2},{12,4},{14,6},{16,24},{18,... | collective-permute-start | bytes 1544 | tf_op jit(solution)/shard_map/ppermute | solution.py:182
  120.8 4.4 %collective-permute-start.12 = (f32[1,128]{1,0:T(1,128)S(1)}, f32[1,128]{1,0:T(1,128)S(1)}, u32[]{:S(2)}, u32[]{:S(2)}) collective-permute-start(f32[1,128]{1,0:T(1,128)S(1)} %add.42), channel_id=1, source_target_pairs={{0,16},{2,18},{4,20},{6,22},{8,24},{10,26},{12,28},{14,30},{16,0},... | collective-permute-start | bytes 1544 | tf_op jit(solution)/shard_map/ppermute | solution.py:182

commit v2 on v1

v2 whole, which is shorter than its diff:
```python
import functools
import math

import jax
import jax.numpy as jnp
import numpy as np
from jax import lax
from jax.experimental import pallas as pl
from jax.experimental.pallas import tpu as pltpu
from jax.sharding import PartitionSpec as P

HALF = 8
STEP_LENGTH = 0.5
EPSILON = 1e-06
LANES = 256
WINDOW = 3
MIB = 1024 * 1024


def taps():
    sigma = HALF / 2.0
    every = np.arange(-HALF, HALF + 1).astype(np.float64)
    normal = np.sqrt(np.sum(np.exp(-((every / sigma) ** 2))))
    return np.exp(-0.5 * (every / sigma) ** 2) / normal


def circulant_parts(lon_count):
    full = np.zeros((lon_count, lon_count), np.float32)
    at = np.arange(lon_count)
    for shift_by, tap in zip(range(-HALF, HALF + 1), taps()):
        full[at, (at + shift_by) % lon_count] += np.float32(tap)
    high = full.astype(jnp.bfloat16)
    low = (full - high.astype(np.float32)).astype(jnp.bfloat16)
    return high, low


def two_parts(value):
    high = value.astype(jnp.bfloat16)
    low = (value - high.astype(jnp.float32)).astype(jnp.bfloat16)
    return high, low


def smooth_rows(low, own, high):
    tap = [float(t) for t in taps()]
    padded = jnp.concatenate([low, own, high], axis=0)
    rows = own.shape[0]
    total = padded[HALF : HALF + rows] * tap[HALF]
    for away in range(1, HALF + 1):
        pair = padded[HALF - away : HALF - away + rows] + padded[HALF + away : HALF + away + rows]
        total = total + pair * tap[HALF + away]
    return total


def smooth_lons(field, circ_high, circ_low):
    first, second = two_parts(field)
    dot = functools.partial(jnp.dot, preferred_element_type=jnp.float32)
    return dot(first, circ_high) + (dot(second, circ_high) + dot(first, circ_low))


def one_hot(ids, at):
    return (ids == at).astype(jnp.bfloat16)


def ids_of(shape, dim):
    return lax.broadcasted_iota(jnp.int32, shape, dim)


def across(left, right):
    return lax.dot_general(left, right, (((1,), (1,)), ((), ())), preferred_element_type=jnp.float32)


def permute(pos, values, tiles):
    hi_ids = ids_of((tiles, LANES), 0)
    lo_ids = ids_of((LANES, LANES), 0)
    hi, lo = lax.div(pos, LANES), lax.rem(pos, LANES)
    total = jnp.zeros((len(values) * tiles, LANES), jnp.float32)
    for at in range(tiles):
        here = slice(at * LANES, (at + 1) * LANES)
        chosen = hi_ids == hi[:, here]
        left = jnp.concatenate([jnp.where(chosen, v[:, here], 0.0) for v in values], axis=0)
        total += across(left.astype(jnp.bfloat16), one_hot(lo_ids, lo[:, here]))
    return [total[k * tiles : (k + 1) * tiles] for k in range(len(values))]


def sort_kernel(shape, cell_ref, pos_ref, key_ref, lane_ref, first_ref, last_ref, far_ref, prefix_ref):
    rows, levels, lons = shape
    slots, obs = cell_ref.shape
    tiles = obs // LANES
    row_ids = ids_of((rows, LANES), 0)
    square = (LANES, LANES)
    upper = (ids_of(square, 0) <= ids_of(square, 1)).astype(jnp.bfloat16)
    counting = jnp.concatenate([upper, jnp.ones(square, jnp.bfloat16)], axis=1)
    before = (ids_of((rows, rows), 1) < ids_of((rows, rows), 0)).astype(jnp.float32)
    for slot in range(slots):
        cell = lax.rem(cell_ref[pl.ds(slot, 1), :], rows * levels * lons)
        key, lon = lax.div(cell, lons), lax.rem(cell, lons)
        row = lax.div(key, levels)
        parts = [row[:, at * LANES : (at + 1) * LANES] for at in range(tiles)]
        hot = jnp.concatenate([one_hot(row_ids, part) for part in parts], axis=0)
        prefix_ref[...] = jnp.dot(hot, counting, preferred_element_type=jnp.float32)
        total = jnp.zeros((rows, LANES), jnp.float32)
        for at in range(tiles):
            total += prefix_ref[pl.ds(at * rows, rows), pl.ds(LANES, LANES)]
        carry = jnp.dot(before, total, precision=lax.Precision.HIGHEST, preferred_element_type=jnp.float32) - 1.0
        places = []
        for at in range(tiles):
            here = pl.ds(at * rows, rows)
            place = jnp.where(row_ids == parts[at], prefix_ref[here, pl.ds(0, LANES)] + carry, 0.0)
            places.append(jnp.sum(place, axis=0, keepdims=True))
            carry += prefix_ref[here, pl.ds(LANES, LANES)]
        pos = jnp.concatenate(places, axis=1).astype(jnp.int32)
        pos_ref[pl.ds(slot, 1), :] = pos
        lane = jnp.where(lon < LANES, lon, LANES - 1 - lon)
        keys, lanes = permute(pos, [key.astype(jnp.float32), lane.astype(jnp.float32)], tiles)
        keys = keys.astype(jnp.int32)
        here = pl.ds(slot * tiles, tiles)
        key_ref[here, :] = keys
        lane_ref[here, :] = lanes.astype(jnp.int32)
        in_row = lax.div(keys, levels)
        first = jnp.minimum(in_row[:, :1], rows - WINDOW)
        last = in_row[:, LANES - 1 :]
        far = jnp.max(last - first, axis=0, keepdims=True)
        across_lanes = lambda v: jnp.broadcast_to(v.astype(jnp.float32), (tiles, 128)).T[:1].astype(jnp.int32)
        first_ref[pl.ds(slot, 1), :] = across_lanes(first)
        last_ref[pl.ds(slot, 1), :] = across_lanes(last)
        far_ref[pl.ds(slot, 1), :] = far


def arrange_kernel(pos_ref, innov_ref, weight_ref, quality_ref, keep_ref, want_ref):
    slots, obs = pos_ref.shape
    tiles = obs // LANES
    for slot in range(slots):
        at = pl.ds(slot, 1)
        keep = quality_ref[at, :].astype(jnp.float32) * weight_ref[at, :]
        values = []
        for value in (keep, innov_ref[at, :]):
            first = value.astype(jnp.bfloat16).astype(jnp.float32)
            values += [first, value - first]
        moved = permute(pos_ref[at, :], values, tiles)
        here = pl.ds(slot * tiles, tiles)
        keep_ref[here, :] = moved[0] + moved[1]
        want_ref[here, :] = moved[2] + moved[3]


def place_of(key, lane, start, levels):
    half = lane < 0
    return key - start * levels + jnp.where(half, WINDOW * levels, 0), jnp.where(half, -1 - lane, lane)


def pick_kernel(
    low_ref, own_ref, high_ref, circ_high_ref, circ_low_ref, ens_ref, key_ref, lane_ref, first_ref, last_ref, far_ref,
    out_ref, local_ref, *part_refs,
):
    rows, levels, lons = own_ref.shape
    slots = ens_ref.shape[0]
    tiles = first_ref.shape[1]
    mixed = smooth_rows(low_ref[...], own_ref[...], high_ref[...]).reshape(rows * levels, lons)
    local_ref[...] = smooth_lons(mixed, circ_high_ref[...], circ_low_ref[...]).reshape(local_ref.shape)
    for slot in range(slots):
        field = ens_ref[slot].astype(jnp.float32) * local_ref[...]
        first = field.astype(jnp.bfloat16).astype(jnp.float32)
        part_refs[slot][...] = jnp.concatenate([first, field - first], axis=1).astype(jnp.bfloat16)
    place_ids = ids_of((2 * WINDOW * levels, LANES), 0)
    lane_ids = ids_of((LANES, LANES), 0)

    def found(slot, at, start, low_row):
        key, lane = key_ref[pl.ds(at, 1), :], lane_ref[pl.ds(at, 1), :]
        place, lane = place_of(key, lane, start, levels)
        if low_row is not None:
            place = jnp.where(lax.div(key, levels) < low_row, -1, place)
            place = jnp.where(lax.div(key, levels) >= start + WINDOW, -1, place)
        else:
            place = jnp.where(lax.div(key, levels) >= start + WINDOW, -1, place)
        part = part_refs[slot][pl.ds(start, WINDOW)].reshape(WINDOW * 2 * levels, lons)
        left = jnp.concatenate([part[:, :LANES], part[:, LANES:]], axis=0)
        both = jnp.dot(left, one_hot(lane_ids, lane), preferred_element_type=jnp.float32)
        both = both.reshape(2 * WINDOW, 2, levels, LANES)
        value = (both[:, 0] + both[:, 1]).reshape(2 * WINDOW * levels, LANES)
        return jnp.sum(jnp.where(place_ids == place, value, 0.0), axis=0, keepdims=True)

    @pl.loop(0, tiles)
    def _(tile):
        for slot in range(slots):
            at = slot * tiles + tile
            out_ref[pl.ds(at, 1), :] = found(slot, at, first_ref[slot, tile], None)

    for slot in range(slots):

        @pl.when(far_ref[slot, 0] >= WINDOW)
        def _():
            @pl.loop(0, tiles)
            def _(tile):
                at = slot * tiles + tile
                begin = first_ref[slot, tile]

                @pl.loop(1, lax.div(last_ref[slot, tile] - begin, WINDOW) + 1)
                def _(turn):
                    low_row = begin + turn * WINDOW
                    start = jnp.minimum(low_row, rows - WINDOW)
                    out_ref[pl.ds(at, 1), :] += found(slot, at, start, low_row)


def scatter_kernel(
    norm_scale, seen_ref, want_ref, keep_ref, key_ref, lane_ref, ens_ref, first_ref, last_ref, far_ref,
    back_ref, cost_ref, wres_ref, *grad_refs,
):
    slots, rows, levels, lons = ens_ref.shape
    tiles = first_ref.shape[1]
    resid = seen_ref[...] * norm_scale - want_ref[...]
    wres_ref[...] = keep_ref[...] * resid
    cost_ref[...] = jnp.sum(wres_ref[...] * resid).reshape(1, 1)
    place_ids = ids_of((2 * WINDOW * levels, LANES), 0)
    lane_ids = ids_of((LANES, LANES), 0)
    for slot in range(slots):
        grad_refs[slot][...] = jnp.zeros(grad_refs[slot].shape, jnp.float32)

    def spread(slot, at, start, low_row):
        key, lane = key_ref[pl.ds(at, 1), :], lane_ref[pl.ds(at, 1), :]
        place, lane = place_of(key, lane, start, levels)
        if low_row is not None:
            place = jnp.where(lax.div(key, levels) < low_row, -1, place)
        place = jnp.where(lax.div(key, levels) >= start + WINDOW, -1, place)
        wres = wres_ref[pl.ds(at, 1), :]
        first = wres.astype(jnp.bfloat16).astype(jnp.float32)
        chosen = place_ids == place
        left = jnp.concatenate([jnp.where(chosen, first, 0.0), jnp.where(chosen, wres - first, 0.0)], axis=0)
        both = across(left.astype(jnp.bfloat16), one_hot(lane_ids, lane))
        size = 2 * WINDOW * levels
        value = (both[:size] + both[size:]).reshape(2, WINDOW, levels, LANES)
        for half in range(2):
            grad_refs[slot][half, pl.ds(start, WINDOW)] += value[half]

    @pl.loop(0, tiles)
    def _(tile):
        for slot in range(slots):
            spread(slot, slot * tiles + tile, first_ref[slot, tile], None)

    for slot in range(slots):

        @pl.when(far_ref[slot, 0] >= WINDOW)
        def _():
            @pl.loop(0, tiles)
            def _(tile):
                begin = first_ref[slot, tile]

                @pl.loop(1, lax.div(last_ref[slot, tile] - begin, WINDOW) + 1)
                def _(turn):
                    low_row = begin + turn * WINDOW
                    spread(slot, slot * tiles + tile, jnp.minimum(low_row, rows - WINDOW), low_row)

    total = jnp.zeros((rows, levels, lons), jnp.float32)
    for slot in range(slots):
        grad = jnp.concatenate([grad_refs[slot][0], grad_refs[slot][1]], axis=2)
        total += ens_ref[slot].astype(jnp.float32) * grad
    back_ref[...] = total * norm_scale


def grad_kernel(low_ref, own_ref, high_ref, circ_high_ref, circ_low_ref, weights_ref, obs_cost_ref, grad_ref, sums_ref):
    rows, levels, lons = own_ref.shape
    mixed = smooth_rows(low_ref[...], own_ref[...], high_ref[...]).reshape(rows * levels, lons)
    weights = weights_ref[...].reshape(rows * levels, lons)
    grad = weights + smooth_lons(mixed, circ_high_ref[...], circ_low_ref[...])
    grad_ref[...] = grad.reshape(grad_ref.shape)
    lane = lax.broadcasted_iota(jnp.int32, sums_ref.shape, 1)
    prior = jnp.sum(weights * weights)
    square = jnp.sum(grad * grad)
    sums_ref[...] = jnp.where(lane == 0, square, jnp.where(lane == 1, prior, jnp.where(lane == 2, obs_cost_ref[...], 0.0)))


def call(body, out_shape, scratch, flops, *operands, scalars=()):
    vmem, smem = pl.BlockSpec(memory_space=pltpu.VMEM), pl.BlockSpec(memory_space=pltpu.SMEM)
    return pl.pallas_call(
        body,
        out_shape=out_shape,
        in_specs=[vmem] * len(operands) + [smem] * len(scalars),
        out_specs=jax.tree.map(lambda _: vmem, out_shape),
        scratch_shapes=scratch,
        compiler_params=pltpu.CompilerParams(vmem_limit_bytes=48 * MIB),
        cost_estimate=pl.CostEstimate(flops=flops, bytes_accessed=2 * MIB, transcendentals=0),
    )(*operands, *scalars)


def edges(field):
    count = lax.axis_size("lat")
    forward = [(i, i + 1) for i in range(count - 1)]
    backward = [(target, source) for source, target in forward]
    low = lax.ppermute(field[-HALF:], "lat", forward)
    high = lax.ppermute(field[:HALF], "lat", backward)
    return low, high


def summed(value, axis):
    count = lax.axis_size(axis)
    if count & (count - 1):
        return lax.psum(value, axis)
    away = 1
    while away < count:
        value = value + lax.ppermute(value, axis, [(i, i ^ away) for i in range(count)])
        away *= 2
    return value


def local(ensemble, weights, obs_cell, innovation, obs_weight, quality):
    _, rows, levels, lons = weights.shape
    slots, obs = obs_cell.shape
    members = lax.axis_size("mem")
    lat_count = lax.axis_size("lat")
    norm_scale = 1.0 / math.sqrt(members - 1)
    cells = rows * levels * lons
    ens, own = ensemble[0], weights[0]
    circ_high, circ_low = (jnp.asarray(part) for part in circulant_parts(lons))
    f32, i32 = jnp.float32, jnp.int32
    tiles = obs // LANES
    ordered = (slots * tiles, LANES)
    shape = (rows, levels, lons)
    like = jax.ShapeDtypeStruct
    low, high = edges(own)
    pos, key, lane, *bounds = call(
        functools.partial(sort_kernel, shape),
        (like((slots, obs), i32), like(ordered, i32), like(ordered, i32), like((slots, tiles), i32), like((slots, tiles), i32), like((slots, 1), i32)),
        [pltpu.VMEM((tiles * rows, 2 * LANES), f32)],
        10**9,
        obs_cell,
    )
    keep, want = call(
        arrange_kernel, (like(ordered, f32), like(ordered, f32)), [], 10**9, pos, innovation, obs_weight, quality
    )
    picked = call(
        pick_kernel,
        like(ordered, f32),
        [pltpu.VMEM(shape, f32)] + [pltpu.VMEM((rows, 2 * levels, lons), jnp.bfloat16)] * slots,
        10**9,
        low, own, high, circ_high, circ_low, ens, key, lane,
        scalars=bounds,
    )
    seen = summed(picked, "mem")
    back, obs_cost = call(
        functools.partial(scatter_kernel, norm_scale),
        (like(shape, f32), like((1, 1), f32)),
        [pltpu.VMEM(ordered, f32)] + [pltpu.VMEM((2, rows, levels, LANES), f32)] * slots,
        10**9,
        seen, want, keep, key, lane, ens,
        scalars=bounds,
    )
    back_low, back_high = edges(back)
    grad, sums = call(
        grad_kernel,
        (jax.ShapeDtypeStruct((rows, levels, lons), f32), jax.ShapeDtypeStruct((1, 128), f32)),
        [],
        10**9,
        back_low, back, back_high, circ_high, circ_low, own, obs_cost,
    )
    totals = summed(summed(sums, "lat"), "mem")
    entries = f32(members * lat_count * cells)
    cost = (0.5 * totals[0, 1] + 0.5 * totals[0, 2] / members) / entries
    length = jnp.sqrt(totals[0, 0] / entries + EPSILON)
    new_weights = own - STEP_LENGTH * grad / length
    return new_weights[None], cost


def solution(mesh):
    placed = (
        P("mem", None, "lat", None, None),
        P("mem", "lat", None, None),
        P(None, "lat"),
        P(None, "lat"),
        P(None, "lat"),
        P(None, "lat"),
    )
    return jax.shard_map(
        local,
        mesh=mesh,
        in_specs=placed,
        out_specs=(P("mem", "lat", None, None), P()),
        check_vma=False,
    )
```

time: 130 us -> 92 us (0.71)
  Pallas kernels: 68.1 us -> 38.4 us
  waiting for transfers between devices: 26.6 us -> 22 us
  local copies, waits for them, and re-layouts: 5.06 us -> 1.75 us
    pallas_call x3 -> x5, Pallas kernels: 68.1 us -> 38.4 us  [call(): pl.pallas_call(body, out_shape=out_shape, in_specs=[vmem] * len(operands)...]
    ppermute x9, waiting for transfers between devices: 25.6 us -> 21.1 us  [summed(): lax.ppermute(value, axis, [(i, i ^ away) for i in range(count)])]
    unnamed x20 -> x16, local copies, waits for them, and re-layouts: 3.35 us -> 0.05 us
  transfers between devices with their start and end apart: 13 -> 13, of which waited for: 10 -> 9; matrix products, arithmetic and copies ran while one was open for 1% -> 0% of each run, Pallas kernels for 0% -> 17%
where the time goes in v2:
time: 92 us; the launch traced here: 91.7 us
  Pallas kernels  38.4 us (42%)
  starting transfers between devices  24.5 us (27%)
  waiting for transfers between devices  22 us (24%)
  between operations  3.99 us (4%)
  local copies, waits for them, and re-layouts  1.75 us (2%)
  other arithmetic  0.99 us (1%)
    pallas_call x5, Pallas kernels, call(): pl.pallas_call(body, out_shape=out_shape, in_specs=[vmem] * len(operands)...  38.4 us
    ppermute x9, waiting for transfers between devices, summed(): lax.ppermute(value, axis, [(i, i ^ away) for i in range(count)])  21.1 us
    ppermute x9, starting transfers between devices, summed(): lax.ppermute(value, axis, [(i, i ^ away) for i in range(count)])  15.7 us
    ppermute x2, starting transfers between devices, edges(): low = lax.ppermute(field[-HALF:], 'lat', forward)  6.21 us
    ppermute x2, starting transfers between devices, edges(): high = lax.ppermute(field[:HALF], 'lat', backward)  2.58 us
  transfers between devices with their start and end apart: 13, of which 9 were waited for; matrix products, arithmetic and copies ran while one was open for 0% of the time, Pallas kernels for 17%

profile of v2, /device:TPU:0, one launch (start us, length us, event | category | flops | bytes accessed | tf_op | source)
XLA Modules:
  0.0 91.7 jit_solution(5267642743367054252)
XLA Ops:
  0.6 1.0 %slice_bitcast_fusion = (f32[8,8,512]{2,1,0:T(8,128)S(1)}, f32[8,8,512]{2,1,0:T(8,128)S(1)}) fusion(f32[1,32,8,512]{3,2,1,0:T(8,128)} %param.9), kind=kLoop, calls=%fused_computation.1 | loop fusion | bytes 524288 | tf_op jit(solution)/shard_map/slice | solution.py:288
  1.7 1.3 %collective-permute-start.1 = (f32[8,8,512]{2,1,0:T(8,128)S(1)}, f32[8,8,512]{2,1,0:T(8,128)S(1)}, u32[]{:S(2)}, u32[]{:S(2)}) collective-permute-start(f32[8,8,512]{2,1,0:T(8,128)S(1)} %get-tuple-element.28), channel_id=1, source_target_pairs={{1,0},{3,2},{5,4},{7,6},{9,8},{11,10},{13,12},{15,14},{17,16},{19,... | collective-permute-start | bytes 393224 | tf_op jit(solution)/shard_map/ppermute | solution.py:288
  3.0 3.2 %collective-permute-start = (f32[8,8,512]{2,1,0:T(8,128)S(1)}, f32[8,8,512]{2,1,0:T(8,128)S(1)}, u32[]{:S(2)}, u32[]{:S(2)}) collective-permute-start(f32[8,8,512]{2,1,0:T(8,128)S(1)} %get-tuple-element.29), channel_id=1, source_target_pairs={{0,1},{2,3},{4,5},{6,7},{8,9},{10,11},{12,13},{14,15},{16,17},{18,... | collective-permute-start | bytes 393224 | tf_op jit(solution)/shard_map/ppermute | solution.py:287
  6.2 10.0 %shard_map.95 = (s32[4,8192]{1,0:T(4,128)S(1)}, s32[128,256]{1,0:T(8,128)S(1)}, s32[128,256]{1,0:T(8,128)S(1)}, s32[4,32]{1,0:T(4,128)S(1)}, s32[4,32]{1,0:T(4,128)S(1)}, /*index=5*/s32[4,1]{1,0:T(4,128)S(1)}) custom-call(s32[4,8192]{1,0:T(4,128)S(1)} %copy-done.2), custom_call_target="tpu_custom_call" | custom-call | flops 1000000000 | bytes 2097152 | tf_op jit(solution)/shard_map/pallas_call | solution.py:272
  16.3 9.8 %shard_map.96 = f32[128,256]{1,0:T(8,128)S(1)} custom-call(f32[8,8,512]{2,1,0:T(8,128)S(1)} %collective-permute-done.low_ref, f32[32,8,512]{2,1,0:T(8,128)S(1)} %bitcast.11, f32[8,8,512]{2,1,0:T(8,128)S(1)} %collective-permute-done.1.high_ref, bf16[512,512]{1,0:T(8,128)(2,1)S(1)} %copy-done.7, bf16[512,512]{1,0:T(8,128)(2,1)S(1)} %copy-done.6, ...), custom_call_target="tpu_custom_call" | custom-call | flops 1000000000 | bytes 2097152 | tf_op jit(solution)/shard_map/pallas_call | solution.py:272
  26.1 3.0 %collective-permute-start.2 = (f32[128,256]{1,0:T(8,128)S(1)}, f32[128,256]{1,0:T(8,128)S(1)}, u32[]{:S(2)}, u32[]{:S(2)}) collective-permute-start(f32[128,256]{1,0:T(8,128)S(1)} %shard_map.96), channel_id=1, source_target_pairs={{0,2},{2,0},{4,6},{6,4},{8,10},{10,8},{12,14},{14,12},{16,18},{18,... | collective-permute-start | bytes 393224 | tf_op jit(solution)/shard_map/ppermute | solution.py:298
  29.1 3.0 %collective-permute-done.2 = f32[128,256]{1,0:T(8,128)S(1)} collective-permute-done((f32[128,256]{1,0:T(8,128)S(1)}, f32[128,256]{1,0:T(8,128)S(1)}, u32[]{:S(2)}, u32[]{:S(2)}) %collective-permute-start.2) | collective-permute-done | bytes 131104 | tf_op jit(solution)/shard_map/ppermute | solution.py:298
  32.2 2.0 %collective-permute-start.3 = (f32[128,256]{1,0:T(8,128)S(1)}, f32[128,256]{1,0:T(8,128)S(1)}, u32[]{:S(2)}, u32[]{:S(2)}) collective-permute-start(f32[128,256]{1,0:T(8,128)S(1)} %add.35), channel_id=1, source_target_pairs={{0,4},{2,6},{4,0},{6,2},{8,12},{10,14},{12,8},{14,10},{16,20},{18,... | collective-permute-start | bytes 393224 | tf_op jit(solution)/shard_map/ppermute | solution.py:298
  34.2 3.0 %collective-permute-done.3 = f32[128,256]{1,0:T(8,128)S(1)} collective-permute-done((f32[128,256]{1,0:T(8,128)S(1)}, f32[128,256]{1,0:T(8,128)S(1)}, u32[]{:S(2)}, u32[]{:S(2)}) %collective-permute-start.3) | collective-permute-done | bytes 131104 | tf_op jit(solution)/shard_map/ppermute | solution.py:298
  37.3 2.1 %collective-permute-start.4 = (f32[128,256]{1,0:T(8,128)S(1)}, f32[128,256]{1,0:T(8,128)S(1)}, u32[]{:S(2)}, u32[]{:S(2)}) collective-permute-start(f32[128,256]{1,0:T(8,128)S(1)} %add.36), channel_id=1, source_target_pairs={{0,8},{2,10},{4,12},{6,14},{8,0},{10,2},{12,4},{14,6},{16,24},{18,... | collective-permute-start | bytes 393224 | tf_op jit(solution)/shard_map/ppermute | solution.py:298
  39.3 3.0 %collective-permute-done.4 = f32[128,256]{1,0:T(8,128)S(1)} collective-permute-done((f32[128,256]{1,0:T(8,128)S(1)}, f32[128,256]{1,0:T(8,128)S(1)}, u32[]{:S(2)}, u32[]{:S(2)}) %collective-permute-start.4) | collective-permute-done | bytes 131104 | tf_op jit(solution)/shard_map/ppermute | solution.py:298
  42.3 4.4 %collective-permute-start.5 = (f32[128,256]{1,0:T(8,128)S(1)}, f32[128,256]{1,0:T(8,128)S(1)}, u32[]{:S(2)}, u32[]{:S(2)}) collective-permute-start(f32[128,256]{1,0:T(8,128)S(1)} %add.37), channel_id=1, source_target_pairs={{0,16},{2,18},{4,20},{6,22},{8,24},{10,26},{12,28},{14,30},{16,0},... | collective-permute-start | bytes 393224 | tf_op jit(solution)/shard_map/ppermute | solution.py:298
  46.7 5.8 %shard_map.97 = (f32[128,256]{1,0:T(8,128)S(1)}, f32[128,256]{1,0:T(8,128)S(1)}) custom-call(s32[4,8192]{1,0:T(4,128)S(1)} %get-tuple-element.19.pos_ref, f32[4,8192]{1,0:T(4,128)S(1)} %copy-done.3, f32[4,8192]{1,0:T(4,128)S(1)} %copy-done.4, s32[4,8192]{1,0:T(4,128)S(1)} %copy-done.5), custom_call_target="tpu_custom_call" | custom-call | flops 1000000000 | bytes 2097152 | tf_op jit(solution)/shard_map/pallas_call | solution.py:272
  52.6 11.1 %shard_map.98 = (f32[32,8,512]{2,1,0:T(8,128)S(1)}, f32[1,1]{1,0:T(1,128)}) custom-call(f32[128,256]{1,0:T(8,128)S(1)} %add.38.seen_ref, f32[128,256]{1,0:T(8,128)S(1)} %get-tuple-element.20.want_ref, f32[128,256]{1,0:T(8,128)S(1)} %get-tuple-element.21.keep_ref, s32[128,256]{1,0:T(8,128)S(1)} %get-tuple-element.14.key_ref, ...), custom_call_target="tpu_custom_call" | custom-call | flops 1000000000 | bytes 2097152 | tf_op jit(solution)/shard_map/pallas_call | solution.py:272
  63.7 1.3 %collective-permute-start.7 = (f32[8,8,512]{2,1,0:T(8,128)S(1)}, f32[8,8,512]{2,1,0:T(8,128)S(1)}, u32[]{:S(2)}, u32[]{:S(2)}) collective-permute-start(f32[8,8,512]{2,1,0:T(8,128)S(1)} %get-tuple-element.26), channel_id=1, source_target_pairs={{1,0},{3,2},{5,4},{7,6},{9,8},{11,10},{13,12},{15,14},{17,16},{19,... | collective-permute-start | bytes 393224 | tf_op jit(solution)/shard_map/ppermute | solution.py:288
  65.0 3.0 %collective-permute-start.6 = (f32[8,8,512]{2,1,0:T(8,128)S(1)}, f32[8,8,512]{2,1,0:T(8,128)S(1)}, u32[]{:S(2)}, u32[]{:S(2)}) collective-permute-start(f32[8,8,512]{2,1,0:T(8,128)S(1)} %get-tuple-element.27), channel_id=1, source_target_pairs={{0,1},{2,3},{4,5},{6,7},{8,9},{10,11},{12,13},{14,15},{16,17},{18,... | collective-permute-start | bytes 393224 | tf_op jit(solution)/shard_map/ppermute | solution.py:287
  68.0 1.0 %collective-permute-done.6.low_ref = f32[8,8,512]{2,1,0:T(8,128)S(1)} collective-permute-done((f32[8,8,512]{2,1,0:T(8,128)S(1)}, f32[8,8,512]{2,1,0:T(8,128)S(1)}, u32[]{:S(2)}, u32[]{:S(2)}) %collective-permute-start.6) | collective-permute-done | bytes 131104 | tf_op jit(solution)/shard_map/ppermute | solution.py:287
  69.0 1.7 %shard_map.99 = (f32[32,8,512]{2,1,0:T(8,128)S(1)}, f32[1,128]{1,0:T(1,128)S(1)}) custom-call(f32[8,8,512]{2,1,0:T(8,128)S(1)} %collective-permute-done.6.low_ref, f32[32,8,512]{2,1,0:T(8,128)S(1)} %get-tuple-element.22.own_ref, f32[8,8,512]{2,1,0:T(8,128)S(1)} %collective-permute-done.7.high_ref, bf16[512,512]{1,0:T(8,128)(2,1)S(1)} %copy-done.7, ...), custom_call_target="tpu_custom_call" | custom-call | flops 1000000000 | bytes 2097152 | tf_op jit(solution)/shard_map/pallas_call | solution.py:272
  72.0 1.5 %collective-permute-start.9 = (f32[1,128]{1,0:T(1,128)S(1)}, f32[1,128]{1,0:T(1,128)S(1)}, u32[]{:S(2)}, u32[]{:S(2)}) collective-permute-start(f32[1,128]{1,0:T(1,128)S(1)} %add.39), channel_id=1, source_target_pairs={{0,2},{2,0},{4,6},{6,4},{8,10},{10,8},{12,14},{14,12},{16,18},{18,... | collective-permute-start | bytes 1544 | tf_op jit(solution)/shard_map/ppermute | solution.py:298
  73.5 2.1 %collective-permute-done.9 = f32[1,128]{1,0:T(1,128)S(1)} collective-permute-done((f32[1,128]{1,0:T(1,128)S(1)}, f32[1,128]{1,0:T(1,128)S(1)}, u32[]{:S(2)}, u32[]{:S(2)}) %collective-permute-start.9) | collective-permute-done | bytes 544 | tf_op jit(solution)/shard_map/ppermute | solution.py:298
  75.5 1.5 %collective-permute-start.10 = (f32[1,128]{1,0:T(1,128)S(1)}, f32[1,128]{1,0:T(1,128)S(1)}, u32[]{:S(2)}, u32[]{:S(2)}) collective-permute-start(f32[1,128]{1,0:T(1,128)S(1)} %add.40), channel_id=1, source_target_pairs={{0,4},{2,6},{4,0},{6,2},{8,12},{10,14},{12,8},{14,10},{16,20},{18,... | collective-permute-start | bytes 1544 | tf_op jit(solution)/shard_map/ppermute | solution.py:298
  77.0 2.0 %collective-permute-done.10 = f32[1,128]{1,0:T(1,128)S(1)} collective-permute-done((f32[1,128]{1,0:T(1,128)S(1)}, f32[1,128]{1,0:T(1,128)S(1)}, u32[]{:S(2)}, u32[]{:S(2)}) %collective-permute-start.10) | collective-permute-done | bytes 544 | tf_op jit(solution)/shard_map/ppermute | solution.py:298
  79.7 2.9 %collective-permute-done.11 = f32[1,128]{1,0:T(1,128)S(1)} collective-permute-done((f32[1,128]{1,0:T(1,128)S(1)}, f32[1,128]{1,0:T(1,128)S(1)}, u32[]{:S(2)}, u32[]{:S(2)}) %collective-permute-start.11) | collective-permute-done | bytes 544 | tf_op jit(solution)/shard_map/ppermute | solution.py:298
  82.7 4.3 %collective-permute-done.12 = f32[1,128]{1,0:T(1,128)S(1)} collective-permute-done((f32[1,128]{1,0:T(1,128)S(1)}, f32[1,128]{1,0:T(1,128)S(1)}, u32[]{:S(2)}, u32[]{:S(2)}) %collective-permute-start.12) | collective-permute-done | bytes 544 | tf_op jit(solution)/shard_map/ppermute | solution.py:298
  (36 shorter events, 3.8 us)
Async XLA Ops:
  0.6 5.6 %copy-start.2 = (s32[4,8192]{1,0:T(4,128)S(1)}, s32[4,8192]{1,0:T(4,128)}, u32[]{:S(2)}) copy-start(s32[4,8192]{1,0:T(4,128)} %cell_ref.1) | copy-start | bytes 393220
  1.7 14.6 %collective-permute-start.1 = (f32[8,8,512]{2,1,0:T(8,128)S(1)}, f32[8,8,512]{2,1,0:T(8,128)S(1)}, u32[]{:S(2)}, u32[]{:S(2)}) collective-permute-start(f32[8,8,512]{2,1,0:T(8,128)S(1)} %get-tuple-element.28), channel_id=1, source_target_pairs={{1,0},{3,2},{5,4},{7,6},{9,8},{11,10},{13,12},{15,14},{17,16},{19,... | collective-permute-start | bytes 393224 | tf_op jit(solution)/shard_map/ppermute | solution.py:288
  3.0 13.3 %copy-start = (f32[1,32,8,512]{3,2,1,0:T(8,128)S(1)}, f32[1,32,8,512]{3,2,1,0:T(8,128)}, u32[]{:S(2)}) copy-start(f32[1,32,8,512]{3,2,1,0:T(8,128)} %param.9) | copy-start | bytes 1572868
  3.0 13.3 %copy-start.1 = (bf16[1,4,32,8,512]{4,3,2,1,0:T(8,128)(2,1)S(1)}, bf16[1,4,32,8,512]{4,3,2,1,0:T(8,128)(2,1)}, u32[]{:S(2)}) copy-start(bf16[1,4,32,8,512]{4,3,2,1,0:T(8,128)(2,1)} %param.8) | copy-start | bytes 3145732
  3.0 13.3 %copy-start.6 = (bf16[512,512]{1,0:T(8,128)(2,1)S(1)}, bf16[512,512]{1,0:T(8,128)(2,1)}, u32[]{:S(2)}) copy-start(bf16[512,512]{1,0:T(8,128)(2,1)} %constant.24.clone.circ_low_ref) | copy-start | bytes 1572868
  3.0 13.3 %copy-start.7 = (bf16[512,512]{1,0:T(8,128)(2,1)S(1)}, bf16[512,512]{1,0:T(8,128)(2,1)}, u32[]{:S(2)}) copy-start(bf16[512,512]{1,0:T(8,128)(2,1)} %constant.23.clone.circ_high_ref) | copy-start | bytes 1572868
  3.0 13.2 %collective-permute-start = (f32[8,8,512]{2,1,0:T(8,128)S(1)}, f32[8,8,512]{2,1,0:T(8,128)S(1)}, u32[]{:S(2)}, u32[]{:S(2)}) collective-permute-start(f32[8,8,512]{2,1,0:T(8,128)S(1)} %get-tuple-element.29), channel_id=1, source_target_pairs={{0,1},{2,3},{4,5},{6,7},{8,9},{10,11},{12,13},{14,15},{16,17},{18,... | collective-permute-start | bytes 393224 | tf_op jit(solution)/shard_map/ppermute | solution.py:287
  26.1 6.0 %collective-permute-start.2 = (f32[128,256]{1,0:T(8,128)S(1)}, f32[128,256]{1,0:T(8,128)S(1)}, u32[]{:S(2)}, u32[]{:S(2)}) collective-permute-start(f32[128,256]{1,0:T(8,128)S(1)} %shard_map.96), channel_id=1, source_target_pairs={{0,2},{2,0},{4,6},{6,4},{8,10},{10,8},{12,14},{14,12},{16,18},{18,... | collective-permute-start | bytes 393224 | tf_op jit(solution)/shard_map/ppermute | solution.py:298
  32.2 5.0 %collective-permute-start.3 = (f32[128,256]{1,0:T(8,128)S(1)}, f32[128,256]{1,0:T(8,128)S(1)}, u32[]{:S(2)}, u32[]{:S(2)}) collective-permute-start(f32[128,256]{1,0:T(8,128)S(1)} %add.35), channel_id=1, source_target_pairs={{0,4},{2,6},{4,0},{6,2},{8,12},{10,14},{12,8},{14,10},{16,20},{18,... | collective-permute-start | bytes 393224 | tf_op jit(solution)/shard_map/ppermute | solution.py:298
  37.2 9.5 %copy-start.3 = (f32[4,8192]{1,0:T(4,128)S(1)}, f32[4,8192]{1,0:T(4,128)}, u32[]{:S(2)}) copy-start(f32[4,8192]{1,0:T(4,128)} %innov_ref.1) | copy-start | bytes 393220
  37.2 9.5 %copy-start.4 = (f32[4,8192]{1,0:T(4,128)S(1)}, f32[4,8192]{1,0:T(4,128)}, u32[]{:S(2)}) copy-start(f32[4,8192]{1,0:T(4,128)} %weight_ref.1) | copy-start | bytes 393220
  37.3 9.5 %copy-start.5 = (s32[4,8192]{1,0:T(4,128)S(1)}, s32[4,8192]{1,0:T(4,128)}, u32[]{:S(2)}) copy-start(s32[4,8192]{1,0:T(4,128)} %quality_ref.1) | copy-start | bytes 393220
  37.3 5.0 %collective-permute-start.4 = (f32[128,256]{1,0:T(8,128)S(1)}, f32[128,256]{1,0:T(8,128)S(1)}, u32[]{:S(2)}, u32[]{:S(2)}) collective-permute-start(f32[128,256]{1,0:T(8,128)S(1)} %add.36), channel_id=1, source_target_pairs={{0,8},{2,10},{4,12},{6,14},{8,0},{10,2},{12,4},{14,6},{16,24},{18,... | collective-permute-start | bytes 393224 | tf_op jit(solution)/shard_map/ppermute | solution.py:298
  42.3 10.2 %collective-permute-start.5 = (f32[128,256]{1,0:T(8,128)S(1)}, f32[128,256]{1,0:T(8,128)S(1)}, u32[]{:S(2)}, u32[]{:S(2)}) collective-permute-start(f32[128,256]{1,0:T(8,128)S(1)} %add.37), channel_id=1, source_target_pairs={{0,16},{2,18},{4,20},{6,22},{8,24},{10,26},{12,28},{14,30},{16,0},... | collective-permute-start | bytes 393224 | tf_op jit(solution)/shard_map/ppermute | solution.py:298
  63.7 4.4 %collective-permute-start.7 = (f32[8,8,512]{2,1,0:T(8,128)S(1)}, f32[8,8,512]{2,1,0:T(8,128)S(1)}, u32[]{:S(2)}, u32[]{:S(2)}) collective-permute-start(f32[8,8,512]{2,1,0:T(8,128)S(1)} %get-tuple-element.26), channel_id=1, source_target_pairs={{1,0},{3,2},{5,4},{7,6},{9,8},{11,10},{13,12},{15,14},{17,16},{19,... | collective-permute-start | bytes 393224 | tf_op jit(solution)/shard_map/ppermute | solution.py:288
  65.0 4.0 %collective-permute-start.6 = (f32[8,8,512]{2,1,0:T(8,128)S(1)}, f32[8,8,512]{2,1,0:T(8,128)S(1)}, u32[]{:S(2)}, u32[]{:S(2)}) collective-permute-start(f32[8,8,512]{2,1,0:T(8,128)S(1)} %get-tuple-element.27), channel_id=1, source_target_pairs={{0,1},{2,3},{4,5},{6,7},{8,9},{10,11},{12,13},{14,15},{16,17},{18,... | collective-permute-start | bytes 393224 | tf_op jit(solution)/shard_map/ppermute | solution.py:287
  70.7 1.2 %collective-permute-start.8 = (f32[1,128]{1,0:T(1,128)S(1)}, f32[1,128]{1,0:T(1,128)S(1)}, u32[]{:S(2)}, u32[]{:S(2)}) collective-permute-start(f32[1,128]{1,0:T(1,128)S(1)} %get-tuple-element.25), channel_id=1, source_target_pairs={{0,1},{1,0},{2,3},{3,2},{4,5},{5,4},{6,7},{7,6},{8,9},{9,8},{10,11... | collective-permute-start | bytes 1544 | tf_op jit(solution)/shard_map/ppermute | solution.py:298
  72.0 3.5 %collective-permute-start.9 = (f32[1,128]{1,0:T(1,128)S(1)}, f32[1,128]{1,0:T(1,128)S(1)}, u32[]{:S(2)}, u32[]{:S(2)}) collective-permute-start(f32[1,128]{1,0:T(1,128)S(1)} %add.39), channel_id=1, source_target_pairs={{0,2},{2,0},{4,6},{6,4},{8,10},{10,8},{12,14},{14,12},{16,18},{18,... | collective-permute-start | bytes 1544 | tf_op jit(solution)/shard_map/ppermute | solution.py:298
  75.5 3.5 %collective-permute-start.10 = (f32[1,128]{1,0:T(1,128)S(1)}, f32[1,128]{1,0:T(1,128)S(1)}, u32[]{:S(2)}, u32[]{:S(2)}) collective-permute-start(f32[1,128]{1,0:T(1,128)S(1)} %add.40), channel_id=1, source_target_pairs={{0,4},{2,6},{4,0},{6,2},{8,12},{10,14},{12,8},{14,10},{16,20},{18,... | collective-permute-start | bytes 1544 | tf_op jit(solution)/shard_map/ppermute | solution.py:298
  79.1 3.5 %collective-permute-start.11 = (f32[1,128]{1,0:T(1,128)S(1)}, f32[1,128]{1,0:T(1,128)S(1)}, u32[]{:S(2)}, u32[]{:S(2)}) collective-permute-start(f32[1,128]{1,0:T(1,128)S(1)} %add.41), channel_id=1, source_target_pairs={{0,8},{2,10},{4,12},{6,14},{8,0},{10,2},{12,4},{14,6},{16,24},{18,... | collective-permute-start | bytes 1544 | tf_op jit(solution)/shard_map/ppermute | solution.py:298
  82.6 4.4 %collective-permute-start.12 = (f32[1,128]{1,0:T(1,128)S(1)}, f32[1,128]{1,0:T(1,128)S(1)}, u32[]{:S(2)}, u32[]{:S(2)}) collective-permute-start(f32[1,128]{1,0:T(1,128)S(1)} %add.42), channel_id=1, source_target_pairs={{0,16},{2,18},{4,20},{6,22},{8,24},{10,26},{12,28},{14,30},{16,0},... | collective-permute-start | bytes 1544 | tf_op jit(solution)/shard_map/ppermute | solution.py:298

commit v3 on v1

v3 whole, which is shorter than its diff:
```python
import functools
import math

import jax
import jax.numpy as jnp
import numpy as np
from jax import lax
from jax.experimental import pallas as pl
from jax.experimental.pallas import tpu as pltpu
from jax.sharding import PartitionSpec as P

HALF = 8
STEP_LENGTH = 0.5
EPSILON = 1e-06
LANES = 256
GROUP = 1024
WINDOW = 3
UNROLL = 8
MIB = 1024 * 1024


def taps():
    sigma = HALF / 2.0
    every = np.arange(-HALF, HALF + 1).astype(np.float64)
    normal = np.sqrt(np.sum(np.exp(-((every / sigma) ** 2))))
    return np.exp(-0.5 * (every / sigma) ** 2) / normal


def circulant_parts(lon_count):
    full = np.zeros((lon_count, lon_count), np.float32)
    at = np.arange(lon_count)
    for shift_by, tap in zip(range(-HALF, HALF + 1), taps()):
        full[at, (at + shift_by) % lon_count] += np.float32(tap)
    high = full.astype(jnp.bfloat16)
    low = (full - high.astype(np.float32)).astype(jnp.bfloat16)
    return high, low


def two_parts(value):
    high = value.astype(jnp.bfloat16)
    low = (value - high.astype(jnp.float32)).astype(jnp.bfloat16)
    return high, low


def smooth_rows(low, own, high):
    tap = [float(t) for t in taps()]
    padded = jnp.concatenate([low, own, high], axis=0)
    rows = own.shape[0]
    total = padded[HALF : HALF + rows] * tap[HALF]
    for away in range(1, HALF + 1):
        pair = padded[HALF - away : HALF - away + rows] + padded[HALF + away : HALF + away + rows]
        total = total + pair * tap[HALF + away]
    return total


def smooth_lons(field, circ_high, circ_low):
    first, second = two_parts(field)
    dot = functools.partial(jnp.dot, preferred_element_type=jnp.float32)
    return dot(first, circ_high) + (dot(second, circ_high) + dot(first, circ_low))


def quotient(value, by):
    if by & (by - 1):
        return lax.div(value, by), lax.rem(value, by)
    return lax.shift_right_logical(value, by.bit_length() - 1), lax.bitwise_and(value, by - 1)


def small_ids(shape):
    return lax.broadcasted_iota(jnp.int32, shape, 0).astype(jnp.bfloat16)


def one_hot(ids, at):
    return jnp.where(ids == at, jnp.bfloat16(1), jnp.bfloat16(0))


def ids_of(shape, dim):
    return lax.broadcasted_iota(jnp.int32, shape, dim)


def across(left, right):
    return lax.dot_general(left, right, (((1,), (1,)), ((), ())), preferred_element_type=jnp.float32)


def permute(pos, values, tiles):
    hi_ids, lo_ids = small_ids((tiles, GROUP)), small_ids((LANES, GROUP))
    hi, lo = (part.astype(jnp.float32).astype(jnp.bfloat16) for part in quotient(pos, LANES))
    total = jnp.zeros((len(values) * tiles, LANES), jnp.float32)
    for at in range(0, pos.shape[1], GROUP):
        here = slice(at, at + GROUP)
        chosen = hi_ids == hi[:, here]
        left = jnp.concatenate([jnp.where(chosen, v[:, here], jnp.bfloat16(0)) for v in values], axis=0)
        total += across(left, one_hot(lo_ids, lo[:, here]))
    return [total[k * tiles : (k + 1) * tiles] for k in range(len(values))]


def sort_kernel(shape, cell_ref, pos_ref, place_ref, lane_ref, first_ref, last_ref, far_ref, prefix_ref):
    rows, levels, lons = shape
    slots, obs = cell_ref.shape
    tiles = obs // LANES
    row_ids = small_ids((rows, LANES))
    square = (LANES, LANES)
    upper = (ids_of(square, 0) <= ids_of(square, 1)).astype(jnp.bfloat16)
    counting = jnp.concatenate([upper, jnp.ones((LANES, 128), jnp.bfloat16)], axis=1)
    before = (ids_of((rows, rows), 1) < ids_of((rows, rows), 0)).astype(jnp.float32)
    wide = lambda v: jnp.concatenate([v] * (LANES // 128), axis=1)
    _, cells = quotient(cell_ref[...], rows * levels * lons)
    keys, lons_of = quotient(cells, lons)
    rows_of, _ = quotient(keys, levels)
    signed = jnp.where(lons_of < LANES, lons_of, LANES - 1 - lons_of)
    keys, rows_of, signed = (v.astype(jnp.float32).astype(jnp.bfloat16) for v in (keys, rows_of, signed))
    for slot in range(slots):
        row = rows_of[slot : slot + 1]
        hots = [one_hot(row_ids, row[:, at * LANES : (at + 1) * LANES]) for at in range(tiles)]
        prefix_ref[...] = jnp.dot(jnp.concatenate(hots, axis=0), counting, preferred_element_type=jnp.float32)
        total = jnp.zeros((rows, 128), jnp.float32)
        for at in range(tiles):
            total += prefix_ref[pl.ds(at * rows, rows), pl.ds(LANES, 128)]
        carry = jnp.dot(before, total, precision=lax.Precision.HIGHEST, preferred_element_type=jnp.float32) - 1.0
        places = []
        for at in range(tiles):
            here = pl.ds(at * rows, rows)
            place = (prefix_ref[here, pl.ds(0, LANES)] + wide(carry)) * hots[at].astype(jnp.float32)
            places.append(jnp.sum(place, axis=0, keepdims=True))
            carry += prefix_ref[here, pl.ds(LANES, 128)]
        pos = jnp.concatenate(places, axis=1).astype(jnp.int32)
        pos_ref[pl.ds(slot, 1), :] = pos
        key, lane = permute(pos, [keys[slot : slot + 1], signed[slot : slot + 1]], tiles)
        key, lane = key.astype(jnp.int32), lane.astype(jnp.int32)
        row, level = quotient(key, levels)
        second = lane < 0
        here = pl.ds(slot * tiles, tiles)
        place_ref[here, :] = (2 * row + jnp.where(second, 1, 0)) * levels + level
        lane_ref[here, :] = jnp.where(second, -1 - lane, lane).astype(jnp.float32)
        first = jnp.minimum(row[:, :1], rows - WINDOW)
        last = row[:, LANES - 1 :]
        far = jnp.max(last - first, axis=0, keepdims=True)
        as_row = lambda v: jnp.broadcast_to(v.astype(jnp.float32), (tiles, 128)).T[:1].astype(jnp.int32)
        first_ref[pl.ds(slot, 1), :] = as_row(first)
        last_ref[pl.ds(slot, 1), :] = as_row(last)
        far_ref[pl.ds(slot, 1), :] = far


def arrange_kernel(pos_ref, innov_ref, weight_ref, quality_ref, keep_ref, want_ref):
    slots, obs = pos_ref.shape
    tiles = obs // LANES
    keeps = two_parts(quality_ref[...].astype(jnp.float32) * weight_ref[...])
    wants = two_parts(innov_ref[...])
    for slot in range(slots):
        at = slice(slot, slot + 1)
        moved = permute(pos_ref[at, :], [part[at] for part in keeps + wants], tiles)
        here = pl.ds(slot * tiles, tiles)
        keep_ref[here, :] = moved[0] + moved[1]
        want_ref[here, :] = moved[2] + moved[3]


def window_places(place_ref, at, start, low_row, levels):
    place = place_ref[pl.ds(at, 1), :] - start * (2 * levels)
    if low_row is None:
        return place
    return jnp.where(place < (low_row - start) * (2 * levels), -1, place)


def over_windows(tiles, slots, rows, first_ref, last_ref, far_ref, unroll, step):
    @pl.loop(0, tiles, unroll=unroll)
    def _(tile):
        for slot in range(slots):
            step(slot, tile, first_ref[slot, tile], None)

    for slot in range(slots):

        @pl.when(far_ref[slot, 0] >= WINDOW)
        def _():
            @pl.loop(0, tiles)
            def _(tile):
                begin = first_ref[slot, tile]

                @pl.loop(1, lax.div(last_ref[slot, tile] - begin, WINDOW) + 1)
                def _(turn):
                    low_row = begin + turn * WINDOW
                    step(slot, tile, jnp.minimum(low_row, rows - WINDOW), low_row)


def pick_kernel(sides, *refs):
    low, high = halo(refs[:sides])
    own_ref, circ_high_ref, circ_low_ref, ens_ref, place_ref, lane_ref, *refs = refs[sides:]
    first_ref, last_ref, far_ref, out_ref, local_ref, *part_refs = refs
    rows, levels, lons = own_ref.shape
    slots = ens_ref.shape[0]
    tiles = first_ref.shape[1]
    mixed = smooth_rows(low, own_ref[...], high).reshape(rows * levels, lons)
    local_ref[...] = smooth_lons(mixed, circ_high_ref[...], circ_low_ref[...]).reshape(local_ref.shape)
    for slot in range(slots):
        field = ens_ref[slot].astype(jnp.float32) * local_ref[...]
        first = field.astype(jnp.bfloat16).astype(jnp.float32)
        part_refs[slot][...] = jnp.concatenate([first, field - first], axis=1).astype(jnp.bfloat16)
    size = 2 * WINDOW * levels
    place_ids = ids_of((size, LANES), 0)
    lane_ids = small_ids((LANES, LANES))

    def step(slot, tile, start, low_row):
        at = slot * tiles + tile
        place = window_places(place_ref, at, start, low_row, levels)
        part = part_refs[slot][pl.ds(start, WINDOW)]
        left = jnp.stack([part[:, :, :LANES], part[:, :, LANES:]], axis=1).reshape(2 * size, LANES)
        hot = one_hot(lane_ids, lane_ref[pl.ds(at, 1), :].astype(jnp.bfloat16))
        both = jnp.dot(left, hot, preferred_element_type=jnp.float32).reshape(2 * WINDOW, 2, levels, LANES)
        value = (both[:, 0] + both[:, 1]).reshape(size, LANES)
        value = jnp.sum(jnp.where(place_ids == place, value, 0.0), axis=0, keepdims=True)
        if low_row is None:
            out_ref[pl.ds(at, 1), :] = value
        else:
            out_ref[pl.ds(at, 1), :] += value

    over_windows(tiles, slots, rows, first_ref, last_ref, far_ref, UNROLL, step)


def scatter_kernel(
    norm_scale, seen_ref, want_ref, keep_ref, place_ref, lane_ref, ens_ref, first_ref, last_ref, far_ref,
    back_ref, cost_ref, wres_ref, *grad_refs,
):
    slots, rows, levels, lons = ens_ref.shape
    tiles = first_ref.shape[1]
    resid = seen_ref[...] * norm_scale - want_ref[...]
    wres_ref[...] = keep_ref[...] * resid
    cost_ref[...] = jnp.sum(wres_ref[...] * resid).reshape(1, 1)
    size = 2 * WINDOW * levels
    place_ids = ids_of((size, LANES), 0)
    lane_ids = small_ids((LANES, LANES))
    for slot in range(slots):
        grad_refs[slot][...] = jnp.zeros(grad_refs[slot].shape, jnp.float32)

    def step(slot, tile, start, low_row):
        at = slot * tiles + tile
        place = window_places(place_ref, at, start, low_row, levels)
        wres = wres_ref[pl.ds(at, 1), :]
        first = wres.astype(jnp.bfloat16).astype(jnp.float32)
        chosen = place_ids == place
        left = jnp.concatenate([jnp.where(chosen, first, 0.0), jnp.where(chosen, wres - first, 0.0)], axis=0)
        hot = one_hot(lane_ids, lane_ref[pl.ds(at, 1), :].astype(jnp.bfloat16))
        both = across(left.astype(jnp.bfloat16), hot)
        grad_refs[slot][pl.ds(start, WINDOW)] += (both[:size] + both[size:]).reshape(WINDOW, 2, levels, LANES)

    over_windows(tiles, slots, rows, first_ref, last_ref, far_ref, UNROLL, step)
    total = jnp.zeros((rows, levels, lons), jnp.float32)
    for slot in range(slots):
        grad = jnp.concatenate([grad_refs[slot][:, 0], grad_refs[slot][:, 1]], axis=2)
        total += ens_ref[slot].astype(jnp.float32) * grad
    back_ref[...] = total * norm_scale


def grad_kernel(sides, *refs):
    low, high = halo(refs[:sides])
    own_ref, circ_high_ref, circ_low_ref, weights_ref, obs_cost_ref, grad_ref, sums_ref = refs[sides:]
    rows, levels, lons = own_ref.shape
    mixed = smooth_rows(low, own_ref[...], high).reshape(rows * levels, lons)
    weights = weights_ref[...].reshape(rows * levels, lons)
    grad = weights + smooth_lons(mixed, circ_high_ref[...], circ_low_ref[...])
    grad_ref[...] = grad.reshape(grad_ref.shape)
    lane = lax.broadcasted_iota(jnp.int32, sums_ref.shape, 1)
    prior = jnp.sum(weights * weights)
    square = jnp.sum(grad * grad)
    sums_ref[...] = jnp.where(lane == 0, square, jnp.where(lane == 1, prior, jnp.where(lane == 2, obs_cost_ref[...], 0.0)))


def update_kernel(members, entries, sums_ref, own_ref, grad_ref, new_ref, cost_ref):
    totals = jnp.sum(sums_ref[...], axis=0, keepdims=True)
    length = jnp.sqrt(totals[:, :1] / entries + EPSILON)
    new_ref[...] = own_ref[...] - grad_ref[...] * (STEP_LENGTH / length)[None]
    cost_ref[...] = (0.5 * totals[:, 1:2] + 0.5 * totals[:, 2:3] / members) / entries


def call(body, out_shape, scratch, flops, *operands, scalars=()):
    vmem, smem = pl.BlockSpec(memory_space=pltpu.VMEM), pl.BlockSpec(memory_space=pltpu.SMEM)
    return pl.pallas_call(
        body,
        out_shape=out_shape,
        in_specs=[vmem] * len(operands) + [smem] * len(scalars),
        out_specs=jax.tree.map(lambda _: vmem, out_shape),
        scratch_shapes=scratch,
        compiler_params=pltpu.CompilerParams(vmem_limit_bytes=48 * MIB),
        cost_estimate=pl.CostEstimate(flops=flops, bytes_accessed=2 * MIB, transcendentals=0),
    )(*operands, *scalars)


def edges(field):
    count = lax.axis_size("lat")
    if count == 2:
        rows = field.shape[0]
        start = (rows - HALF) * (1 - lax.axis_index("lat"))
        return swapped(lax.dynamic_slice_in_dim(field, start, HALF, 0))
    forward = [(i, i + 1) for i in range(count - 1)]
    backward = [(target, source) for source, target in forward]
    low = lax.ppermute(field[-HALF:], "lat", forward)
    high = lax.ppermute(field[:HALF], "lat", backward)
    return [low, high]


def swapped(edge):
    return [lax.ppermute(edge, "lat", [(0, 1), (1, 0)])]


def halo(refs):
    if len(refs) == 2:
        return refs[0][...], refs[1][...]
    last = lax.axis_index("lat") == 1
    return jnp.where(last, refs[0][...], 0.0), jnp.where(last, 0.0, refs[0][...])


def summed(value, axis):
    count = lax.axis_size(axis)
    if count & (count - 1):
        return lax.psum(value, axis)
    away = 1
    while away < count:
        value = value + lax.ppermute(value, axis, [(i, i ^ away) for i in range(count)])
        away *= 2
    return value


def like(shape, kind=jnp.float32):
    return jax.ShapeDtypeStruct(shape, kind)


def sort_cells(obs_cell, shape):
    slots, obs = obs_cell.shape
    tiles = obs // LANES
    whole, ordered, bound = (slots, obs), (slots * tiles, LANES), (slots, tiles)
    kinds = [like(whole, jnp.int32), like(ordered, jnp.int32), like(ordered)]
    kinds += [like(bound, jnp.int32), like(bound, jnp.int32), like((slots, 1), jnp.int32)]
    scratch = [pltpu.VMEM((tiles * shape[0], LANES + 128), jnp.float32)]
    pos, place, lane, *bounds = call(functools.partial(sort_kernel, shape), kinds, scratch, 10**9, obs_cell)
    return pos, (place, lane), bounds


def arrange(pos, innovation, obs_weight, quality):
    ordered = like((pos.size // LANES, LANES))
    return call(arrange_kernel, [ordered, ordered], [], 10**9, pos, innovation, obs_weight, quality)


def pick(sides, own, circ, ens, at, bounds):
    rows, levels, lons = own.shape
    scratch = [pltpu.VMEM(own.shape, jnp.float32)]
    scratch += [pltpu.VMEM((rows, 2 * levels, lons), jnp.bfloat16)] * ens.shape[0]
    body = functools.partial(pick_kernel, len(sides))
    return call(body, like(at[0].shape), scratch, 10**9, *sides, own, *circ, ens, *at, scalars=bounds)


def scatter(seen, want, keep, ens, at, bounds, norm_scale):
    slots, rows, levels, lons = ens.shape
    scratch = [pltpu.VMEM(seen.shape, jnp.float32)]
    scratch += [pltpu.VMEM((rows, 2, levels, LANES), jnp.float32)] * slots
    kinds = [like((rows, levels, lons)), like((1, 1))]
    body = functools.partial(scatter_kernel, norm_scale)
    return call(body, kinds, scratch, 10**9, seen, want, keep, *at, ens, scalars=bounds)


def gradient(sides, own, circ, weights, obs_cost, devices):
    kinds = [like(own.shape), like((devices, 128))]
    body = functools.partial(grad_kernel, len(sides))
    return call(body, kinds, [], 10**9, *sides, own, *circ, weights, obs_cost)


def local(ensemble, weights, obs_cell, innovation, obs_weight, quality):
    _, rows, levels, lons = weights.shape
    members, bands = lax.axis_size("mem"), lax.axis_size("lat")
    norm_scale = 1.0 / math.sqrt(members - 1)
    ens, own = ensemble[0], weights[0]
    circ = [jnp.asarray(part) for part in circulant_parts(lons)]
    sides = edges(own)
    pos, at, bounds = sort_cells(obs_cell, own.shape)
    keep, want = arrange(pos, innovation, obs_weight, quality)
    picked = pick(sides, own, circ, ens, at, bounds)
    seen = summed(picked, "mem")
    back, obs_cost = scatter(seen, want, keep, ens, at, bounds, norm_scale)
    grad, sums = gradient(edges(back), back, circ, own, obs_cost, members * bands)
    sums = lax.all_to_all(sums, ("mem", "lat"), 0, 0, tiled=True)
    body = functools.partial(update_kernel, members, float(members * bands * rows * levels * lons))
    new_weights, cost = call(body, [like(own.shape), like((1, 1))], [], 10**8, sums, own, grad)
    return new_weights[None], cost[0, 0]


def solution(mesh):
    placed = (
        P("mem", None, "lat", None, None),
        P("mem", "lat", None, None),
        P(None, "lat"),
        P(None, "lat"),
        P(None, "lat"),
        P(None, "lat"),
    )
    return jax.shard_map(
        local,
        mesh=mesh,
        in_specs=placed,
        out_specs=(P("mem", "lat", None, None), P()),
        check_vma=False,
    )
```

time: 130 us -> 64.6 us (0.50)
  Pallas kernels: 68.1 us -> 29 us
  starting transfers between devices: 24.2 us -> 9.41 us
  waiting for transfers between devices: 26.6 us -> 12.4 us
  blocking collectives: 0 us -> 11.8 us
  local copies, waits for them, and re-layouts: 5.06 us -> 1.02 us
  between operations: 4 us -> 0.79 us
  other arithmetic: 2.01 us -> 0.08 us
    pallas_call x3 -> x6, Pallas kernels: 68.1 us -> 29 us  [call(): pl.pallas_call(body, out_shape=out_shape, in_specs=[vmem] * len(operands)...]
    ppermute x9 -> x4, waiting for transfers between devices: 25.6 us -> 11 us  [summed(): lax.ppermute(value, axis, [(i, i ^ away) for i in range(count)])]
    all_to_all x0 -> x1, blocking collectives: none -> 11.8 us  [local(): sums = lax.all_to_all(sums, ('mem', 'lat'), 0, 0, tiled=True)]
    ppermute x4 -> x2, starting transfers between devices: 8.8 us -> 0.59 us  [swapped(): return [lax.ppermute(edge, 'lat', [(0, 1), (1, 0)])]]
    ppermute x9 -> x4, starting transfers between devices: 15.4 us -> 8.82 us  [summed(): lax.ppermute(value, axis, [(i, i ^ away) for i in range(count)])]
    unnamed x20 -> x16, local copies, waits for them, and re-layouts: 3.35 us -> 0.05 us
    slice x3 -> x0, local copies, waits for them, and re-layouts: 1.71 us -> none  [the longest x2 1.06 us: edges(): high = lax.ppermute(field[:HALF], 'lat', backward)]
  transfers between devices with their start and end apart: 13 -> 6, of which waited for: 10 -> 4; matrix products, arithmetic and copies ran while one was open for 1% -> 0% of each run, Pallas kernels for 0% -> 21%
where the time goes in v3:
time: 64.6 us; the launch traced here: 64.4 us
  Pallas kernels  29 us (45%)
  waiting for transfers between devices  12.4 us (19%)
  blocking collectives  11.8 us (18%)
  starting transfers between devices  9.41 us (15%)
  local copies, waits for them, and re-layouts  1.02 us (2%)
  between operations  0.79 us (1%)
    pallas_call x6, Pallas kernels, call(): pl.pallas_call(body, out_shape=out_shape, in_specs=[vmem] * len(operands)...  29 us
    all_to_all x1, blocking collectives, local(): sums = lax.all_to_all(sums, ('mem', 'lat'), 0, 0, tiled=True)  11.8 us
    ppermute x4, waiting for transfers between devices, summed(): lax.ppermute(value, axis, [(i, i ^ away) for i in range(count)])  11 us
    ppermute x4, starting transfers between devices, summed(): lax.ppermute(value, axis, [(i, i ^ away) for i in range(count)])  8.82 us
    ppermute x2, waiting for transfers between devices, swapped(): return [lax.ppermute(edge, 'lat', [(0, 1), (1, 0)])]  1.34 us
  transfers between devices with their start and end apart: 6, of which 4 were waited for; matrix products, arithmetic and copies ran while one was open for 0% of the time, Pallas kernels for 21%

profile of v3, /device:TPU:0, one launch (start us, length us, event | category | flops | bytes accessed | tf_op | source)
XLA Modules:
  0.0 64.4 jit_solution(8247327550117038361)
XLA Ops:
  0.6 1.0 %dynamic-slice_bitcast_fusion = f32[8,8,512]{2,1,0:T(8,128)S(1)} fusion(f32[1,32,8,512]{3,2,1,0:T(8,128)} %param.9, s32[]{:T(128)S(6)} %select_n.4), kind=kLoop, calls=%fused_computation | loop fusion | bytes 262148 | tf_op jit(solution)/shard_map/dynamic_slice | solution.py:290
  1.6 0.0 copy-start
  1.6 0.0 copy-start.6
  1.6 0.0 copy-start.7
  1.7 0.5 collective-permute-start
  2.2 8.1 %shard_map.95 = (s32[4,8192]{1,0:T(4,128)S(1)}, s32[128,256]{1,0:T(8,128)S(1)}, f32[128,256]{1,0:T(8,128)S(1)}, s32[4,32]{1,0:T(4,128)S(1)}, s32[4,32]{1,0:T(4,128)S(1)}, /*index=5*/s32[4,1]{1,0:T(4,128)S(1)}) custom-call(s32[4,8192]{1,0:T(4,128)S(1)} %copy-done.2), custom_call_target="tpu_custom_call" | custom-call | flops 1000000000 | bytes 2097152 | tf_op jit(solution)/shard_map/pallas_call | solution.py:274
  10.3 0.0 copy-done.1
  10.3 5.5 %shard_map.96 = f32[128,256]{1,0:T(8,128)S(1)} custom-call(f32[8,8,512]{2,1,0:T(8,128)S(1)} %collective-permute-done.refs_0_, f32[32,8,512]{2,1,0:T(8,128)S(1)} %bitcast.10, bf16[512,512]{1,0:T(8,128)(2,1)S(1)} %copy-done.7, bf16[512,512]{1,0:T(8,128)(2,1)S(1)} %copy-done.6, bf16[4,32,8,512]{3,2,1,0:T(8,128)(2,1)S(1)} %bitcast.15, ...), custom_call_target="tpu_custom_call" | custom-call | flops 1000000000 | bytes 2097152 | tf_op jit(solution)/shard_map/pallas_call | solution.py:274
  15.9 2.6 %collective-permute-start.1 = (f32[128,256]{1,0:T(8,128)S(1)}, f32[128,256]{1,0:T(8,128)S(1)}, u32[]{:S(2)}, u32[]{:S(2)}) collective-permute-start(f32[128,256]{1,0:T(8,128)S(1)} %shard_map.96), channel_id=1, source_target_pairs={{0,2},{2,0},{4,6},{6,4},{8,10},{10,8},{12,14},{14,12},{16,18},{18,... | collective-permute-start | bytes 393224 | tf_op jit(solution)/shard_map/ppermute | solution.py:315
  18.5 4.1 %collective-permute-done.1 = f32[128,256]{1,0:T(8,128)S(1)} collective-permute-done((f32[128,256]{1,0:T(8,128)S(1)}, f32[128,256]{1,0:T(8,128)S(1)}, u32[]{:S(2)}, u32[]{:S(2)}) %collective-permute-start.1) | collective-permute-done | bytes 131104 | tf_op jit(solution)/shard_map/ppermute | solution.py:315
  22.6 1.8 %collective-permute-start.2 = (f32[128,256]{1,0:T(8,128)S(1)}, f32[128,256]{1,0:T(8,128)S(1)}, u32[]{:S(2)}, u32[]{:S(2)}) collective-permute-start(f32[128,256]{1,0:T(8,128)S(1)} %add.17), channel_id=1, source_target_pairs={{0,4},{2,6},{4,0},{6,2},{8,12},{10,14},{12,8},{14,10},{16,20},{18,... | collective-permute-start | bytes 393224 | tf_op jit(solution)/shard_map/ppermute | solution.py:315
  24.5 3.5 %collective-permute-done.2 = f32[128,256]{1,0:T(8,128)S(1)} collective-permute-done((f32[128,256]{1,0:T(8,128)S(1)}, f32[128,256]{1,0:T(8,128)S(1)}, u32[]{:S(2)}, u32[]{:S(2)}) %collective-permute-start.2) | collective-permute-done | bytes 131104 | tf_op jit(solution)/shard_map/ppermute | solution.py:315
  28.0 0.0 copy-start.3
  28.1 1.7 %collective-permute-start.3 = (f32[128,256]{1,0:T(8,128)S(1)}, f32[128,256]{1,0:T(8,128)S(1)}, u32[]{:S(2)}, u32[]{:S(2)}) collective-permute-start(f32[128,256]{1,0:T(8,128)S(1)} %add.18), channel_id=1, source_target_pairs={{0,8},{2,10},{4,12},{6,14},{8,0},{10,2},{12,4},{14,6},{16,24},{18,... | collective-permute-start | bytes 393224 | tf_op jit(solution)/shard_map/ppermute | solution.py:315
  29.8 3.3 %collective-permute-done.3 = f32[128,256]{1,0:T(8,128)S(1)} collective-permute-done((f32[128,256]{1,0:T(8,128)S(1)}, f32[128,256]{1,0:T(8,128)S(1)}, u32[]{:S(2)}, u32[]{:S(2)}) %collective-permute-start.3) | collective-permute-done | bytes 131104 | tf_op jit(solution)/shard_map/ppermute | solution.py:315
  33.1 2.7 %collective-permute-start.4 = (f32[128,256]{1,0:T(8,128)S(1)}, f32[128,256]{1,0:T(8,128)S(1)}, u32[]{:S(2)}, u32[]{:S(2)}) collective-permute-start(f32[128,256]{1,0:T(8,128)S(1)} %add.19), channel_id=1, source_target_pairs={{0,16},{2,18},{4,20},{6,22},{8,24},{10,26},{12,28},{14,30},{16,0},... | collective-permute-start | bytes 393224 | tf_op jit(solution)/shard_map/ppermute | solution.py:315
  35.8 5.5 %shard_map.97 = (f32[128,256]{1,0:T(8,128)S(1)}, f32[128,256]{1,0:T(8,128)S(1)}) custom-call(s32[4,8192]{1,0:T(4,128)S(1)} %get-tuple-element.21.pos_ref, f32[4,8192]{1,0:T(4,128)S(1)} %copy-done.3, f32[4,8192]{1,0:T(4,128)S(1)} %copy-done.4, s32[4,8192]{1,0:T(4,128)S(1)} %copy-done.5), custom_call_target="tpu_custom_call" | custom-call | flops 1000000000 | bytes 2097152 | tf_op jit(solution)/shard_map/pallas_call | solution.py:274
  41.3 0.0 collective-permute-done.4
  41.4 7.1 %shard_map.98 = (f32[32,8,512]{2,1,0:T(8,128)S(1)}, f32[1,1]{1,0:T(1,128)}) custom-call(f32[128,256]{1,0:T(8,128)S(1)} %add.20.seen_ref, f32[128,256]{1,0:T(8,128)S(1)} %get-tuple-element.22.want_ref, f32[128,256]{1,0:T(8,128)S(1)} %get-tuple-element.23.keep_ref, s32[128,256]{1,0:T(8,128)S(1)} %get-tuple-element.16.refs_5_.place_ref, ...), custom_call_target="tpu_custom_call" | custom-call | flops 1000000000 | bytes 2097152 | tf_op jit(solution)/shard_map/pallas_call | solution.py:274
  48.5 0.1 collective-permute-start.5
  48.6 1.3 %collective-permute-done.5.refs_0_ = f32[8,8,512]{2,1,0:T(8,128)S(1)} collective-permute-done((f32[8,8,512]{2,1,0:T(8,128)S(1)}, f32[8,8,512]{2,1,0:T(8,128)S(1)}, u32[]{:S(2)}, u32[]{:S(2)}) %collective-permute-start.5) | collective-permute-done | bytes 131104 | tf_op jit(solution)/shard_map/ppermute | solution.py:299
  49.9 1.7 %shard_map.99 = (f32[32,8,512]{2,1,0:T(8,128)S(1)}, f32[32,128]{1,0:T(8,128)S(1)}) custom-call(f32[8,8,512]{2,1,0:T(8,128)S(1)} %collective-permute-done.5.refs_0_, f32[32,8,512]{2,1,0:T(8,128)S(1)} %get-tuple-element.24.refs_1_, bf16[512,512]{1,0:T(8,128)(2,1)S(1)} %copy-done.7, bf16[512,512]{1,0:T(8,128)(2,1)S(1)} %copy-done.6, ...), custom_call_target="tpu_custom_call" | custom-call | flops 1000000000 | bytes 2097152 | tf_op jit(solution)/shard_map/pallas_call | solution.py:274
  51.6 11.8 %all_to_all.11 = f32[32,1,128]{2,1,0:T(1,128)S(1)} all-to-all(f32[32,1,128]{2,1,0:T(1,128)S(1)} %bitcast.14), channel_id=1, replica_groups=mesh['mem'=16,'lat'=2] {'mem','lat'}, dimensions={0} | all-to-all | bytes 32768 | tf_op jit(solution)/shard_map/all_to_all | solution.py:376
  63.5 1.0 %shard_map.100 = (f32[32,8,512]{2,1,0:T(8,128)}, f32[1,1]{1,0:T(1,128)}) custom-call(f32[32,128]{1,0:T(8,128)S(1)} %bitcast.13, f32[32,8,512]{2,1,0:T(8,128)S(1)} %bitcast.12, f32[32,8,512]{2,1,0:T(8,128)S(1)} %get-tuple-element.27.grad_ref), custom_call_target="tpu_custom_call" | custom-call | flops 100000000 | bytes 2097152 | tf_op jit(solution)/shard_map/pallas_call | solution.py:274
  (17 shorter events, 0.1 us)
Async XLA Ops:
  0.6 1.5 %copy-start.2 = (s32[4,8192]{1,0:T(4,128)S(1)}, s32[4,8192]{1,0:T(4,128)}, u32[]{:S(2)}) copy-start(s32[4,8192]{1,0:T(4,128)} %cell_ref.1) | copy-start | bytes 393220
  1.6 8.7 %copy-start = (f32[1,32,8,512]{3,2,1,0:T(8,128)S(1)}, f32[1,32,8,512]{3,2,1,0:T(8,128)}, u32[]{:S(2)}) copy-start(f32[1,32,8,512]{3,2,1,0:T(8,128)} %param.9) | copy-start | bytes 1572868
  1.6 8.7 %copy-start.1 = (bf16[1,4,32,8,512]{4,3,2,1,0:T(8,128)(2,1)S(1)}, bf16[1,4,32,8,512]{4,3,2,1,0:T(8,128)(2,1)}, u32[]{:S(2)}) copy-start(bf16[1,4,32,8,512]{4,3,2,1,0:T(8,128)(2,1)} %param.8) | copy-start | bytes 3145732
  1.6 8.7 %copy-start.6 = (bf16[512,512]{1,0:T(8,128)(2,1)S(1)}, bf16[512,512]{1,0:T(8,128)(2,1)}, u32[]{:S(2)}) copy-start(bf16[512,512]{1,0:T(8,128)(2,1)} %constant.18.clone.refs_3_) | copy-start | bytes 1572868
  1.6 8.7 %copy-start.7 = (bf16[512,512]{1,0:T(8,128)(2,1)S(1)}, bf16[512,512]{1,0:T(8,128)(2,1)}, u32[]{:S(2)}) copy-start(bf16[512,512]{1,0:T(8,128)(2,1)} %constant.17.clone.refs_2_) | copy-start | bytes 1572868
  1.7 8.6 %collective-permute-start = (f32[8,8,512]{2,1,0:T(8,128)S(1)}, f32[8,8,512]{2,1,0:T(8,128)S(1)}, u32[]{:S(2)}, u32[]{:S(2)}) collective-permute-start(f32[8,8,512]{2,1,0:T(8,128)S(1)} %dynamic-slice_bitcast_fusion), channel_id=1, source_target_pairs={{0,1},{1,0},{2,3},{3,2},{4,5},{5,4},{6,7},{7,6},{8,9},{9,8},{10,11... | collective-permute-start | bytes 393224 | tf_op jit(solution)/shard_map/ppermute | solution.py:299
  15.9 6.7 %collective-permute-start.1 = (f32[128,256]{1,0:T(8,128)S(1)}, f32[128,256]{1,0:T(8,128)S(1)}, u32[]{:S(2)}, u32[]{:S(2)}) collective-permute-start(f32[128,256]{1,0:T(8,128)S(1)} %shard_map.96), channel_id=1, source_target_pairs={{0,2},{2,0},{4,6},{6,4},{8,10},{10,8},{12,14},{14,12},{16,18},{18,... | collective-permute-start | bytes 393224 | tf_op jit(solution)/shard_map/ppermute | solution.py:315
  22.6 5.4 %collective-permute-start.2 = (f32[128,256]{1,0:T(8,128)S(1)}, f32[128,256]{1,0:T(8,128)S(1)}, u32[]{:S(2)}, u32[]{:S(2)}) collective-permute-start(f32[128,256]{1,0:T(8,128)S(1)} %add.17), channel_id=1, source_target_pairs={{0,4},{2,6},{4,0},{6,2},{8,12},{10,14},{12,8},{14,10},{16,20},{18,... | collective-permute-start | bytes 393224 | tf_op jit(solution)/shard_map/ppermute | solution.py:315
  28.0 7.8 %copy-start.3 = (f32[4,8192]{1,0:T(4,128)S(1)}, f32[4,8192]{1,0:T(4,128)}, u32[]{:S(2)}) copy-start(f32[4,8192]{1,0:T(4,128)} %innov_ref.1) | copy-start | bytes 393220
  28.0 7.8 %copy-start.4 = (f32[4,8192]{1,0:T(4,128)S(1)}, f32[4,8192]{1,0:T(4,128)}, u32[]{:S(2)}) copy-start(f32[4,8192]{1,0:T(4,128)} %weight_ref.1) | copy-start | bytes 393220
  28.0 7.8 %copy-start.5 = (s32[4,8192]{1,0:T(4,128)S(1)}, s32[4,8192]{1,0:T(4,128)}, u32[]{:S(2)}) copy-start(s32[4,8192]{1,0:T(4,128)} %quality_ref.1) | copy-start | bytes 393220
  28.1 5.0 %collective-permute-start.3 = (f32[128,256]{1,0:T(8,128)S(1)}, f32[128,256]{1,0:T(8,128)S(1)}, u32[]{:S(2)}, u32[]{:S(2)}) collective-permute-start(f32[128,256]{1,0:T(8,128)S(1)} %add.18), channel_id=1, source_target_pairs={{0,8},{2,10},{4,12},{6,14},{8,0},{10,2},{12,4},{14,6},{16,24},{18,... | collective-permute-start | bytes 393224 | tf_op jit(solution)/shard_map/ppermute | solution.py:315
  33.1 8.2 %collective-permute-start.4 = (f32[128,256]{1,0:T(8,128)S(1)}, f32[128,256]{1,0:T(8,128)S(1)}, u32[]{:S(2)}, u32[]{:S(2)}) collective-permute-start(f32[128,256]{1,0:T(8,128)S(1)} %add.19), channel_id=1, source_target_pairs={{0,16},{2,18},{4,20},{6,22},{8,24},{10,26},{12,28},{14,30},{16,0},... | collective-permute-start | bytes 393224 | tf_op jit(solution)/shard_map/ppermute | solution.py:315
  48.5 1.4 %collective-permute-start.5 = (f32[8,8,512]{2,1,0:T(8,128)S(1)}, f32[8,8,512]{2,1,0:T(8,128)S(1)}, u32[]{:S(2)}, u32[]{:S(2)}) collective-permute-start(f32[8,8,512]{2,1,0:T(8,128)S(1)} %constant_dynamic-slice_fusion), channel_id=1, source_target_pairs={{0,1},{1,0},{2,3},{3,2},{4,5},{5,4},{6,7},{7,6},{8,9},{9,8},{10,11... | collective-permute-start | bytes 393224 | tf_op jit(solution)/shard_map/ppermute | solution.py:299

commit v4 on v3

--- a/solution.py
+++ b/solution.py
@@ -13,9 +13,14 @@
 STEP_LENGTH = 0.5
 EPSILON = 1e-06
 LANES = 256
+PIECE = 128
+PICK_LONS = 256
+SCATTER_LONS = 128
 GROUP = 1024
-WINDOW = 3
-UNROLL = 8
+BIN = 2
+WINDOW = 2 * BIN
+PICK_UNROLL = 16
+SCATTER_UNROLL = 16
 MIB = 1024 * 1024
 
 
@@ -81,60 +86,68 @@
     return lax.dot_general(left, right, (((1,), (1,)), ((), ())), preferred_element_type=jnp.float32)
 
 
-def permute(pos, values, tiles):
-    hi_ids, lo_ids = small_ids((tiles, GROUP)), small_ids((LANES, GROUP))
-    hi, lo = (part.astype(jnp.float32).astype(jnp.bfloat16) for part in quotient(pos, LANES))
-    total = jnp.zeros((len(values) * tiles, LANES), jnp.float32)
+def permute(pos, values, pieces):
+    hi_ids, lo_ids = small_ids((pieces, GROUP)), small_ids((PIECE, GROUP))
+    hi, lo = (part.astype(jnp.float32).astype(jnp.bfloat16) for part in quotient(pos, PIECE))
+    total = jnp.zeros((len(values) * pieces, PIECE), jnp.float32)
     for at in range(0, pos.shape[1], GROUP):
         here = slice(at, at + GROUP)
         chosen = hi_ids == hi[:, here]
         left = jnp.concatenate([jnp.where(chosen, v[:, here], jnp.bfloat16(0)) for v in values], axis=0)
         total += across(left, one_hot(lo_ids, lo[:, here]))
-    return [total[k * tiles : (k + 1) * tiles] for k in range(len(values))]
-
-
-def sort_kernel(shape, cell_ref, pos_ref, place_ref, lane_ref, first_ref, last_ref, far_ref, prefix_ref):
+    return [total[k * pieces : (k + 1) * pieces] for k in range(len(values))]
+
+
+def sort_kernel(shape, cell_ref, pos_ref, *refs):
+    *place_refs, first_ref, last_ref, far_ref, prefix_ref = refs
     rows, levels, lons = shape
     slots, obs = cell_ref.shape
-    tiles = obs // LANES
-    row_ids = small_ids((rows, LANES))
+    tiles, pieces = obs // LANES, obs // PIECE
+    bins = rows // BIN
+    bin_ids = small_ids((bins, LANES))
     square = (LANES, LANES)
     upper = (ids_of(square, 0) <= ids_of(square, 1)).astype(jnp.bfloat16)
     counting = jnp.concatenate([upper, jnp.ones((LANES, 128), jnp.bfloat16)], axis=1)
-    before = (ids_of((rows, rows), 1) < ids_of((rows, rows), 0)).astype(jnp.float32)
+    before = (ids_of((bins, bins), 1) < ids_of((bins, bins), 0)).astype(jnp.float32)
     wide = lambda v: jnp.concatenate([v] * (LANES // 128), axis=1)
     _, cells = quotient(cell_ref[...], rows * levels * lons)
     keys, lons_of = quotient(cells, lons)
-    rows_of, _ = quotient(keys, levels)
-    signed = jnp.where(lons_of < LANES, lons_of, LANES - 1 - lons_of)
-    keys, rows_of, signed = (v.astype(jnp.float32).astype(jnp.bfloat16) for v in (keys, rows_of, signed))
-    for slot in range(slots):
-        row = rows_of[slot : slot + 1]
-        hots = [one_hot(row_ids, row[:, at * LANES : (at + 1) * LANES]) for at in range(tiles)]
+    bins_of, _ = quotient(keys, levels * BIN)
+    middle = lons // 2
+    signed = jnp.where(lons_of < middle, lons_of, middle - 1 - lons_of)
+    keys, bins_of, signed = (v.astype(jnp.float32).astype(jnp.bfloat16) for v in (keys, bins_of, signed))
+    for slot in range(slots):
+        group = bins_of[slot : slot + 1]
+        hots = [one_hot(bin_ids, group[:, at * LANES : (at + 1) * LANES]) for at in range(tiles)]
         prefix_ref[...] = jnp.dot(jnp.concatenate(hots, axis=0), counting, preferred_element_type=jnp.float32)
-        total = jnp.zeros((rows, 128), jnp.float32)
+        total = jnp.zeros((bins, 128), jnp.float32)
         for at in range(tiles):
-            total += prefix_ref[pl.ds(at * rows, rows), pl.ds(LANES, 128)]
+            total += prefix_ref[pl.ds(at * bins, bins), pl.ds(LANES, 128)]
         carry = jnp.dot(before, total, precision=lax.Precision.HIGHEST, preferred_element_type=jnp.float32) - 1.0
         places = []
         for at in range(tiles):
-            here = pl.ds(at * rows, rows)
+            here = pl.ds(at * bins, bins)
             place = (prefix_ref[here, pl.ds(0, LANES)] + wide(carry)) * hots[at].astype(jnp.float32)
             places.append(jnp.sum(place, axis=0, keepdims=True))
             carry += prefix_ref[here, pl.ds(LANES, 128)]
         pos = jnp.concatenate(places, axis=1).astype(jnp.int32)
         pos_ref[pl.ds(slot, 1), :] = pos
-        key, lane = permute(pos, [keys[slot : slot + 1], signed[slot : slot + 1]], tiles)
+        key, lane = permute(pos, [keys[slot : slot + 1], signed[slot : slot + 1]], pieces)
         key, lane = key.astype(jnp.int32), lane.astype(jnp.int32)
         row, level = quotient(key, levels)
-        second = lane < 0
-        here = pl.ds(slot * tiles, tiles)
-        place_ref[here, :] = (2 * row + jnp.where(second, 1, 0)) * levels + level
-        lane_ref[here, :] = jnp.where(second, -1 - lane, lane).astype(jnp.float32)
-        first = jnp.minimum(row[:, :1], rows - WINDOW)
-        last = row[:, LANES - 1 :]
-        far = jnp.max(last - first, axis=0, keepdims=True)
-        as_row = lambda v: jnp.broadcast_to(v.astype(jnp.float32), (tiles, 128)).T[:1].astype(jnp.int32)
+        lon = jnp.where(lane < 0, middle - 1 - lane, lane)
+        here = pl.ds(slot * pieces, pieces)
+        for near, place_ref, lane_ref in zip((PICK_LONS, SCATTER_LONS), place_refs[::2], place_refs[1::2]):
+            part, lane = quotient(lon, near)
+            place_ref[here, :] = (row * (lons // near) + part) * levels + level
+            lane_ref[here, :] = lane.astype(jnp.float32)
+        group = quotient(row, BIN)[0] * BIN
+        first = jnp.minimum(group[:, :1], rows - WINDOW)
+        last = group[:, PIECE - 1 :] + BIN - 1
+        begin = jnp.concatenate([first[:1], first[:-1]], axis=0)
+        ends_tile = quotient(ids_of((pieces, 1), 0), LANES // PIECE)[1] == LANES // PIECE - 1
+        far = jnp.max(jnp.where(ends_tile, last - begin, 0), axis=0, keepdims=True)
+        as_row = lambda v: jnp.broadcast_to(v.astype(jnp.float32), (pieces, 128)).T[:1].astype(jnp.int32)
         first_ref[pl.ds(slot, 1), :] = as_row(first)
         last_ref[pl.ds(slot, 1), :] = as_row(last)
         far_ref[pl.ds(slot, 1), :] = far
@@ -142,29 +155,34 @@
 
 def arrange_kernel(pos_ref, innov_ref, weight_ref, quality_ref, keep_ref, want_ref):
     slots, obs = pos_ref.shape
-    tiles = obs // LANES
+    pieces = obs // PIECE
     keeps = two_parts(quality_ref[...].astype(jnp.float32) * weight_ref[...])
     wants = two_parts(innov_ref[...])
     for slot in range(slots):
         at = slice(slot, slot + 1)
-        moved = permute(pos_ref[at, :], [part[at] for part in keeps + wants], tiles)
-        here = pl.ds(slot * tiles, tiles)
+        moved = permute(pos_ref[at, :], [part[at] for part in keeps + wants], pieces)
+        here = pl.ds(slot * pieces, pieces)
         keep_ref[here, :] = moved[0] + moved[1]
         want_ref[here, :] = moved[2] + moved[3]
 
 
-def window_places(place_ref, at, start, low_row, levels):
-    place = place_ref[pl.ds(at, 1), :] - start * (2 * levels)
+def tile_row(ref, at):
+    parts = LANES // PIECE
+    return jnp.concatenate([ref[pl.ds(at * parts + k, 1), :] for k in range(parts)], axis=1)
+
+
+def window_places(place_ref, at, start, low_row, per_row):
+    place = tile_row(place_ref, at) - start * per_row
     if low_row is None:
         return place
-    return jnp.where(place < (low_row - start) * (2 * levels), -1, place)
+    return jnp.where(place < (low_row - start) * per_row, -1, place)
 
 
 def over_windows(tiles, slots, rows, first_ref, last_ref, far_ref, unroll, step):
     @pl.loop(0, tiles, unroll=unroll)
     def _(tile):
         for slot in range(slots):
-            step(slot, tile, first_ref[slot, tile], None)
+            step(slot, tile, first_ref[slot, tile * (LANES // PIECE)], None)
 
     for slot in range(slots):
 
@@ -172,9 +190,9 @@
         def _():
             @pl.loop(0, tiles)
             def _(tile):
-                begin = first_ref[slot, tile]
-
-                @pl.loop(1, lax.div(last_ref[slot, tile] - begin, WINDOW) + 1)
+                begin = first_ref[slot, tile * (LANES // PIECE)]
+
+                @pl.loop(1, lax.div(last_ref[slot, (tile + 1) * (LANES // PIECE) - 1] - begin, WINDOW) + 1)
                 def _(turn):
                     low_row = begin + turn * WINDOW
                     step(slot, tile, jnp.minimum(low_row, rows - WINDOW), low_row)
@@ -186,32 +204,32 @@
     first_ref, last_ref, far_ref, out_ref, local_ref, *part_refs = refs
     rows, levels, lons = own_ref.shape
     slots = ens_ref.shape[0]
-    tiles = first_ref.shape[1]
+    tiles = first_ref.shape[1] // (LANES // PIECE)
     mixed = smooth_rows(low, own_ref[...], high).reshape(rows * levels, lons)
     local_ref[...] = smooth_lons(mixed, circ_high_ref[...], circ_low_ref[...]).reshape(local_ref.shape)
     for slot in range(slots):
         field = ens_ref[slot].astype(jnp.float32) * local_ref[...]
         first = field.astype(jnp.bfloat16).astype(jnp.float32)
         part_refs[slot][...] = jnp.concatenate([first, field - first], axis=1).astype(jnp.bfloat16)
-    size = 2 * WINDOW * levels
+    parts = lons // PICK_LONS
+    size = WINDOW * parts * levels
     place_ids = ids_of((size, LANES), 0)
-    lane_ids = small_ids((LANES, LANES))
+    lane_ids = small_ids((PICK_LONS, LANES))
 
     def step(slot, tile, start, low_row):
         at = slot * tiles + tile
-        place = window_places(place_ref, at, start, low_row, levels)
+        place = window_places(place_ref, at, start, low_row, parts * levels)
         part = part_refs[slot][pl.ds(start, WINDOW)]
-        left = jnp.stack([part[:, :, :LANES], part[:, :, LANES:]], axis=1).reshape(2 * size, LANES)
-        hot = one_hot(lane_ids, lane_ref[pl.ds(at, 1), :].astype(jnp.bfloat16))
-        both = jnp.dot(left, hot, preferred_element_type=jnp.float32).reshape(2 * WINDOW, 2, levels, LANES)
+        left = jnp.stack([part[:, :, k * PICK_LONS : (k + 1) * PICK_LONS] for k in range(parts)], axis=1).reshape(2 * size, PICK_LONS)
+        hot = one_hot(lane_ids, tile_row(lane_ref, at).astype(jnp.bfloat16))
+        both = jnp.dot(left, hot, preferred_element_type=jnp.float32).reshape(WINDOW * parts, 2, levels, LANES)
         value = (both[:, 0] + both[:, 1]).reshape(size, LANES)
         value = jnp.sum(jnp.where(place_ids == place, value, 0.0), axis=0, keepdims=True)
-        if low_row is None:
-            out_ref[pl.ds(at, 1), :] = value
-        else:
-            out_ref[pl.ds(at, 1), :] += value
-
-    over_windows(tiles, slots, rows, first_ref, last_ref, far_ref, UNROLL, step)
+        for k in range(LANES // PIECE):
+            here, part = pl.ds(at * (LANES // PIECE) + k, 1), value[:, k * PIECE : (k + 1) * PIECE]
+            out_ref[here, :] = part if low_row is None else out_ref[here, :] + part
+
+    over_windows(tiles, slots, rows, first_ref, last_ref, far_ref, PICK_UNROLL, step)
 
 
 def scatter_kernel(
@@ -219,31 +237,31 @@
     back_ref, cost_ref, wres_ref, *grad_refs,
 ):
     slots, rows, levels, lons = ens_ref.shape
-    tiles = first_ref.shape[1]
+    tiles = first_ref.shape[1] // (LANES // PIECE)
     resid = seen_ref[...] * norm_scale - want_ref[...]
     wres_ref[...] = keep_ref[...] * resid
     cost_ref[...] = jnp.sum(wres_ref[...] * resid).reshape(1, 1)
-    size = 2 * WINDOW * levels
-    place_ids = ids_of((size, LANES), 0)
-    lane_ids = small_ids((LANES, LANES))
+    parts = lons // SCATTER_LONS
+    size = WINDOW * parts * levels
+    place_ids = small_ids((size, LANES))
+    lane_ids = small_ids((SCATTER_LONS, LANES))
     for slot in range(slots):
         grad_refs[slot][...] = jnp.zeros(grad_refs[slot].shape, jnp.float32)
 
     def step(slot, tile, start, low_row):
         at = slot * tiles + tile
-        place = window_places(place_ref, at, start, low_row, levels)
-        wres = wres_ref[pl.ds(at, 1), :]
-        first = wres.astype(jnp.bfloat16).astype(jnp.float32)
-        chosen = place_ids == place
-        left = jnp.concatenate([jnp.where(chosen, first, 0.0), jnp.where(chosen, wres - first, 0.0)], axis=0)
-        hot = one_hot(lane_ids, lane_ref[pl.ds(at, 1), :].astype(jnp.bfloat16))
-        both = across(left.astype(jnp.bfloat16), hot)
-        grad_refs[slot][pl.ds(start, WINDOW)] += (both[:size] + both[size:]).reshape(WINDOW, 2, levels, LANES)
-
-    over_windows(tiles, slots, rows, first_ref, last_ref, far_ref, UNROLL, step)
+        place = window_places(place_ref, at, start, low_row, parts * levels)
+        chosen = place_ids == place.astype(jnp.float32).astype(jnp.bfloat16)
+        left = [jnp.where(chosen, part, jnp.bfloat16(0)) for part in two_parts(tile_row(wres_ref, at))]
+        left = jnp.concatenate(left, axis=0)
+        hot = one_hot(lane_ids, tile_row(lane_ref, at).astype(jnp.bfloat16))
+        both = across(left, hot)
+        grad_refs[slot][pl.ds(start, WINDOW)] += (both[:size] + both[size:]).reshape(WINDOW, parts, levels, SCATTER_LONS)
+
+    over_windows(tiles, slots, rows, first_ref, last_ref, far_ref, SCATTER_UNROLL, step)
     total = jnp.zeros((rows, levels, lons), jnp.float32)
     for slot in range(slots):
-        grad = jnp.concatenate([grad_refs[slot][:, 0], grad_refs[slot][:, 1]], axis=2)
+        grad = jnp.concatenate([grad_refs[slot][:, k] for k in range(parts)], axis=2)
         total += ens_ref[slot].astype(jnp.float32) * grad
     back_ref[...] = total * norm_scale
 
@@ -324,16 +342,16 @@
 def sort_cells(obs_cell, shape):
     slots, obs = obs_cell.shape
     tiles = obs // LANES
-    whole, ordered, bound = (slots, obs), (slots * tiles, LANES), (slots, tiles)
-    kinds = [like(whole, jnp.int32), like(ordered, jnp.int32), like(ordered)]
+    whole, ordered, bound = (slots, obs), (slots * obs // PIECE, PIECE), (slots, obs // PIECE)
+    kinds = [like(whole, jnp.int32)] + [like(ordered, jnp.int32), like(ordered)] * 2
     kinds += [like(bound, jnp.int32), like(bound, jnp.int32), like((slots, 1), jnp.int32)]
-    scratch = [pltpu.VMEM((tiles * shape[0], LANES + 128), jnp.float32)]
-    pos, place, lane, *bounds = call(functools.partial(sort_kernel, shape), kinds, scratch, 10**9, obs_cell)
-    return pos, (place, lane), bounds
+    scratch = [pltpu.VMEM((tiles * shape[0] // BIN, LANES + 128), jnp.float32)]
+    pos, *ats, first, last, far = call(functools.partial(sort_kernel, shape), kinds, scratch, 10**9, obs_cell)
+    return pos, ats[:2], ats[2:], (first, last, far)
 
 
 def arrange(pos, innovation, obs_weight, quality):
-    ordered = like((pos.size // LANES, LANES))
+    ordered = like((pos.size // PIECE, PIECE))
     return call(arrange_kernel, [ordered, ordered], [], 10**9, pos, innovation, obs_weight, quality)
 
 
@@ -348,7 +366,7 @@
 def scatter(seen, want, keep, ens, at, bounds, norm_scale):
     slots, rows, levels, lons = ens.shape
     scratch = [pltpu.VMEM(seen.shape, jnp.float32)]
-    scratch += [pltpu.VMEM((rows, 2, levels, LANES), jnp.float32)] * slots
+    scratch += [pltpu.VMEM((rows, lons // SCATTER_LONS, levels, SCATTER_LONS), jnp.float32)] * slots
     kinds = [like((rows, levels, lons)), like((1, 1))]
     body = functools.partial(scatter_kernel, norm_scale)
     return call(body, kinds, scratch, 10**9, seen, want, keep, *at, ens, scalars=bounds)
@@ -367,11 +385,11 @@
     ens, own = ensemble[0], weights[0]
     circ = [jnp.asarray(part) for part in circulant_parts(lons)]
     sides = edges(own)
-    pos, at, bounds = sort_cells(obs_cell, own.shape)
+    pos, pick_at, scatter_at, bounds = sort_cells(obs_cell, own.shape)
     keep, want = arrange(pos, innovation, obs_weight, quality)
-    picked = pick(sides, own, circ, ens, at, bounds)
+    picked = pick(sides, own, circ, ens, pick_at, bounds)
     seen = summed(picked, "mem")
-    back, obs_cost = scatter(seen, want, keep, ens, at, bounds, norm_scale)
+    back, obs_cost = scatter(seen, want, keep, ens, scatter_at, bounds, norm_scale)
     grad, sums = gradient(edges(back), back, circ, own, obs_cost, members * bands)
     sums = lax.all_to_all(sums, ("mem", "lat"), 0, 0, tiled=True)
     body = functools.partial(update_kernel, members, float(members * bands * rows * levels * lons))

time: 64.6 us -> 59.6 us (0.923)
  Pallas kernels: 29 us -> 22.9 us
  blocking collectives: 11.8 us -> 12.7 us
    pallas_call x6, Pallas kernels: 29 us -> 22.9 us  [call(): pl.pallas_call(body, out_shape=out_shape, in_specs=[vmem] * len(operands)...]
    all_to_all x1, blocking collectives: 11.8 us -> 12.7 us  [local(): sums = lax.all_to_all(sums, ('mem', 'lat'), 0, 0, tiled=True)]
  transfers between devices with their start and end apart: 6 -> 6, of which waited for: 4 -> 5; matrix products, arithmetic and copies ran while one was open for 0% -> 0% of each run, Pallas kernels for 21% -> 15%
where the time goes in v4:
time: 59.6 us; the launch traced here: 59.4 us
  Pallas kernels  22.9 us (38%)
  blocking collectives  12.7 us (21%)
  waiting for transfers between devices  12.5 us (21%)
  starting transfers between devices  9.39 us (16%)
  local copies, waits for them, and re-layouts  1.02 us (2%)
  between operations  0.79 us (1%)
    pallas_call x6, Pallas kernels, call(): pl.pallas_call(body, out_shape=out_shape, in_specs=[vmem] * len(operands)...  22.9 us
    all_to_all x1, blocking collectives, local(): sums = lax.all_to_all(sums, ('mem', 'lat'), 0, 0, tiled=True)  12.7 us
    ppermute x4, waiting for transfers between devices, summed(): lax.ppermute(value, axis, [(i, i ^ away) for i in range(count)])  11.2 us
    ppermute x4, starting transfers between devices, summed(): lax.ppermute(value, axis, [(i, i ^ away) for i in range(count)])  8.8 us
    ppermute x2, waiting for transfers between devices, swapped(): return [lax.ppermute(edge, 'lat', [(0, 1), (1, 0)])]  1.34 us
  transfers between devices with their start and end apart: 6, of which 5 were waited for; matrix products, arithmetic and copies ran while one was open for 0% of the time, Pallas kernels for 15%

profile of v4, /device:TPU:0, one launch (start us, length us, event | category | flops | bytes accessed | tf_op | source)
XLA Modules:
  0.0 59.4 jit_solution(13112265932589918508)
XLA Ops:
  0.6 1.0 %dynamic-slice_bitcast_fusion = f32[8,8,512]{2,1,0:T(8,128)S(1)} fusion(f32[1,32,8,512]{3,2,1,0:T(8,128)} %param.9, s32[]{:T(128)S(6)} %select_n.4), kind=kLoop, calls=%fused_computation | loop fusion | bytes 262148 | tf_op jit(solution)/shard_map/dynamic_slice | solution.py:308
  1.6 0.0 copy-start
  1.6 0.0 copy-start.6
  1.6 0.0 copy-start.7
  1.7 0.5 collective-permute-start
  2.2 4.3 %shard_map.95 = (s32[4,8192]{1,0:T(4,128)S(1)}, s32[256,128]{1,0:T(8,128)S(1)}, f32[256,128]{1,0:T(8,128)S(1)}, s32[256,128]{1,0:T(8,128)S(1)}, f32[256,128]{1,0...) custom-call(s32[4,8192]{1,0:T(4,128)S(1)} %copy-done.2), custom_call_target="tpu_custom_call" | custom-call | flops 1000000000 | bytes 2097152 | tf_op jit(solution)/shard_map/pallas_call | solution.py:292
  6.4 0.0 copy-done
  6.5 0.0 copy-done.1
  6.5 5.3 %shard_map.96 = f32[256,128]{1,0:T(8,128)S(1)} custom-call(f32[8,8,512]{2,1,0:T(8,128)S(1)} %collective-permute-done.refs_0_, f32[32,8,512]{2,1,0:T(8,128)S(1)} %bitcast.10, bf16[512,512]{1,0:T(8,128)(2,1)S(1)} %copy-done.7, bf16[512,512]{1,0:T(8,128)(2,1)S(1)} %copy-done.6, bf16[4,32,8,512]{3,2,1,0:T(8,128)(2,1)S(1)} %bitcast.15, ...), custom_call_target="tpu_custom_call" | custom-call | flops 1000000000 | bytes 2097152 | tf_op jit(solution)/shard_map/pallas_call | solution.py:292
  11.8 2.6 %collective-permute-start.1 = (f32[256,128]{1,0:T(8,128)S(1)}, f32[256,128]{1,0:T(8,128)S(1)}, u32[]{:S(2)}, u32[]{:S(2)}) collective-permute-start(f32[256,128]{1,0:T(8,128)S(1)} %shard_map.96), channel_id=1, source_target_pairs={{0,2},{2,0},{4,6},{6,4},{8,10},{10,8},{12,14},{14,12},{16,18},{18,... | collective-permute-start | bytes 393224 | tf_op jit(solution)/shard_map/ppermute | solution.py:333
  14.4 4.1 %collective-permute-done.1 = f32[256,128]{1,0:T(8,128)S(1)} collective-permute-done((f32[256,128]{1,0:T(8,128)S(1)}, f32[256,128]{1,0:T(8,128)S(1)}, u32[]{:S(2)}, u32[]{:S(2)}) %collective-permute-start.1) | collective-permute-done | bytes 131104 | tf_op jit(solution)/shard_map/ppermute | solution.py:333
  18.6 1.8 %collective-permute-start.2 = (f32[256,128]{1,0:T(8,128)S(1)}, f32[256,128]{1,0:T(8,128)S(1)}, u32[]{:S(2)}, u32[]{:S(2)}) collective-permute-start(f32[256,128]{1,0:T(8,128)S(1)} %add.17), channel_id=1, source_target_pairs={{0,4},{2,6},{4,0},{6,2},{8,12},{10,14},{12,8},{14,10},{16,20},{18,... | collective-permute-start | bytes 393224 | tf_op jit(solution)/shard_map/ppermute | solution.py:333
  20.4 3.5 %collective-permute-done.2 = f32[256,128]{1,0:T(8,128)S(1)} collective-permute-done((f32[256,128]{1,0:T(8,128)S(1)}, f32[256,128]{1,0:T(8,128)S(1)}, u32[]{:S(2)}, u32[]{:S(2)}) %collective-permute-start.2) | collective-permute-done | bytes 131104 | tf_op jit(solution)/shard_map/ppermute | solution.py:333
  24.0 1.7 %collective-permute-start.3 = (f32[256,128]{1,0:T(8,128)S(1)}, f32[256,128]{1,0:T(8,128)S(1)}, u32[]{:S(2)}, u32[]{:S(2)}) collective-permute-start(f32[256,128]{1,0:T(8,128)S(1)} %add.18), channel_id=1, source_target_pairs={{0,8},{2,10},{4,12},{6,14},{8,0},{10,2},{12,4},{14,6},{16,24},{18,... | collective-permute-start | bytes 393224 | tf_op jit(solution)/shard_map/ppermute | solution.py:333
  25.7 3.3 %collective-permute-done.3 = f32[256,128]{1,0:T(8,128)S(1)} collective-permute-done((f32[256,128]{1,0:T(8,128)S(1)}, f32[256,128]{1,0:T(8,128)S(1)}, u32[]{:S(2)}, u32[]{:S(2)}) %collective-permute-start.3) | collective-permute-done | bytes 131104 | tf_op jit(solution)/shard_map/ppermute | solution.py:333
  29.0 2.7 %collective-permute-start.4 = (f32[256,128]{1,0:T(8,128)S(1)}, f32[256,128]{1,0:T(8,128)S(1)}, u32[]{:S(2)}, u32[]{:S(2)}) collective-permute-start(f32[256,128]{1,0:T(8,128)S(1)} %add.19), channel_id=1, source_target_pairs={{0,16},{2,18},{4,20},{6,22},{8,24},{10,26},{12,28},{14,30},{16,0},... | collective-permute-start | bytes 393224 | tf_op jit(solution)/shard_map/ppermute | solution.py:333
  31.8 4.5 %shard_map.97 = (f32[256,128]{1,0:T(8,128)S(1)}, f32[256,128]{1,0:T(8,128)S(1)}) custom-call(s32[4,8192]{1,0:T(4,128)S(1)} %get-tuple-element.23.pos_ref, f32[4,8192]{1,0:T(4,128)S(1)} %copy-done.3, f32[4,8192]{1,0:T(4,128)S(1)} %copy-done.4, s32[4,8192]{1,0:T(4,128)S(1)} %copy-done.5), custom_call_target="tpu_custom_call" | custom-call | flops 1000000000 | bytes 2097152 | tf_op jit(solution)/shard_map/pallas_call | solution.py:292
  36.2 0.2 collective-permute-done.4
  36.4 6.1 %shard_map.98 = (f32[32,8,512]{2,1,0:T(8,128)S(1)}, f32[1,1]{1,0:T(1,128)}) custom-call(f32[256,128]{1,0:T(8,128)S(1)} %add.20.seen_ref, f32[256,128]{1,0:T(8,128)S(1)} %get-tuple-element.24.want_ref, f32[256,128]{1,0:T(8,128)S(1)} %get-tuple-element.25.keep_ref, s32[256,128]{1,0:T(8,128)S(1)} %get-tuple-element.26.place_ref, ...), custom_call_target="tpu_custom_call" | custom-call | flops 1000000000 | bytes 2097152 | tf_op jit(solution)/shard_map/pallas_call | solution.py:292
  42.6 0.1 collective-permute-start.5
  42.6 1.3 %collective-permute-done.5.refs_0_ = f32[8,8,512]{2,1,0:T(8,128)S(1)} collective-permute-done((f32[8,8,512]{2,1,0:T(8,128)S(1)}, f32[8,8,512]{2,1,0:T(8,128)S(1)}, u32[]{:S(2)}, u32[]{:S(2)}) %collective-permute-start.5) | collective-permute-done | bytes 131104 | tf_op jit(solution)/shard_map/ppermute | solution.py:317
  44.0 1.7 %shard_map.99 = (f32[32,8,512]{2,1,0:T(8,128)S(1)}, f32[32,128]{1,0:T(8,128)S(1)}) custom-call(f32[8,8,512]{2,1,0:T(8,128)S(1)} %collective-permute-done.5.refs_0_, f32[32,8,512]{2,1,0:T(8,128)S(1)} %get-tuple-element.28.refs_1_, bf16[512,512]{1,0:T(8,128)(2,1)S(1)} %copy-done.7, bf16[512,512]{1,0:T(8,128)(2,1)S(1)} %copy-done.6, ...), custom_call_target="tpu_custom_call" | custom-call | flops 1000000000 | bytes 2097152 | tf_op jit(solution)/shard_map/pallas_call | solution.py:292
  45.7 12.7 %all_to_all.11 = f32[32,1,128]{2,1,0:T(1,128)S(1)} all-to-all(f32[32,1,128]{2,1,0:T(1,128)S(1)} %bitcast.14), channel_id=1, replica_groups=mesh['mem'=16,'lat'=2] {'mem','lat'}, dimensions={0} | all-to-all | bytes 32768 | tf_op jit(solution)/shard_map/all_to_all | solution.py:394
  58.4 1.0 %shard_map.100 = (f32[32,8,512]{2,1,0:T(8,128)}, f32[1,1]{1,0:T(1,128)}) custom-call(f32[32,128]{1,0:T(8,128)S(1)} %bitcast.13, f32[32,8,512]{2,1,0:T(8,128)S(1)} %bitcast.12, f32[32,8,512]{2,1,0:T(8,128)S(1)} %get-tuple-element.31.grad_ref), custom_call_target="tpu_custom_call" | custom-call | flops 100000000 | bytes 2097152 | tf_op jit(solution)/shard_map/pallas_call | solution.py:292
  (17 shorter events, 0.1 us)
Async XLA Ops:
  0.6 1.5 %copy-start.2 = (s32[4,8192]{1,0:T(4,128)S(1)}, s32[4,8192]{1,0:T(4,128)}, u32[]{:S(2)}) copy-start(s32[4,8192]{1,0:T(4,128)} %cell_ref.1) | copy-start | bytes 393220
  1.6 4.9 %copy-start = (f32[1,32,8,512]{3,2,1,0:T(8,128)S(1)}, f32[1,32,8,512]{3,2,1,0:T(8,128)}, u32[]{:S(2)}) copy-start(f32[1,32,8,512]{3,2,1,0:T(8,128)} %param.9) | copy-start | bytes 1572868
  1.6 4.9 %copy-start.1 = (bf16[1,4,32,8,512]{4,3,2,1,0:T(8,128)(2,1)S(1)}, bf16[1,4,32,8,512]{4,3,2,1,0:T(8,128)(2,1)}, u32[]{:S(2)}) copy-start(bf16[1,4,32,8,512]{4,3,2,1,0:T(8,128)(2,1)} %param.8) | copy-start | bytes 3145732
  1.6 4.9 %copy-start.6 = (bf16[512,512]{1,0:T(8,128)(2,1)S(1)}, bf16[512,512]{1,0:T(8,128)(2,1)}, u32[]{:S(2)}) copy-start(bf16[512,512]{1,0:T(8,128)(2,1)} %constant.18.clone.refs_3_) | copy-start | bytes 1572868
  1.6 4.9 %copy-start.7 = (bf16[512,512]{1,0:T(8,128)(2,1)S(1)}, bf16[512,512]{1,0:T(8,128)(2,1)}, u32[]{:S(2)}) copy-start(bf16[512,512]{1,0:T(8,128)(2,1)} %constant.17.clone.refs_2_) | copy-start | bytes 1572868
  1.7 4.8 %collective-permute-start = (f32[8,8,512]{2,1,0:T(8,128)S(1)}, f32[8,8,512]{2,1,0:T(8,128)S(1)}, u32[]{:S(2)}, u32[]{:S(2)}) collective-permute-start(f32[8,8,512]{2,1,0:T(8,128)S(1)} %dynamic-slice_bitcast_fusion), channel_id=1, source_target_pairs={{0,1},{1,0},{2,3},{3,2},{4,5},{5,4},{6,7},{7,6},{8,9},{9,8},{10,11... | collective-permute-start | bytes 393224 | tf_op jit(solution)/shard_map/ppermute | solution.py:317
  11.8 6.7 %collective-permute-start.1 = (f32[256,128]{1,0:T(8,128)S(1)}, f32[256,128]{1,0:T(8,128)S(1)}, u32[]{:S(2)}, u32[]{:S(2)}) collective-permute-start(f32[256,128]{1,0:T(8,128)S(1)} %shard_map.96), channel_id=1, source_target_pairs={{0,2},{2,0},{4,6},{6,4},{8,10},{10,8},{12,14},{14,12},{16,18},{18,... | collective-permute-start | bytes 393224 | tf_op jit(solution)/shard_map/ppermute | solution.py:333
  18.6 5.4 %collective-permute-start.2 = (f32[256,128]{1,0:T(8,128)S(1)}, f32[256,128]{1,0:T(8,128)S(1)}, u32[]{:S(2)}, u32[]{:S(2)}) collective-permute-start(f32[256,128]{1,0:T(8,128)S(1)} %add.17), channel_id=1, source_target_pairs={{0,4},{2,6},{4,0},{6,2},{8,12},{10,14},{12,8},{14,10},{16,20},{18,... | collective-permute-start | bytes 393224 | tf_op jit(solution)/shard_map/ppermute | solution.py:333
  24.0 7.8 %copy-start.3 = (f32[4,8192]{1,0:T(4,128)S(1)}, f32[4,8192]{1,0:T(4,128)}, u32[]{:S(2)}) copy-start(f32[4,8192]{1,0:T(4,128)} %innov_ref.1) | copy-start | bytes 393220
  24.0 7.8 %copy-start.4 = (f32[4,8192]{1,0:T(4,128)S(1)}, f32[4,8192]{1,0:T(4,128)}, u32[]{:S(2)}) copy-start(f32[4,8192]{1,0:T(4,128)} %weight_ref.1) | copy-start | bytes 393220
  24.0 7.8 %copy-start.5 = (s32[4,8192]{1,0:T(4,128)S(1)}, s32[4,8192]{1,0:T(4,128)}, u32[]{:S(2)}) copy-start(s32[4,8192]{1,0:T(4,128)} %quality_ref.1) | copy-start | bytes 393220
  24.0 5.0 %collective-permute-start.3 = (f32[256,128]{1,0:T(8,128)S(1)}, f32[256,128]{1,0:T(8,128)S(1)}, u32[]{:S(2)}, u32[]{:S(2)}) collective-permute-start(f32[256,128]{1,0:T(8,128)S(1)} %add.18), channel_id=1, source_target_pairs={{0,8},{2,10},{4,12},{6,14},{8,0},{10,2},{12,4},{14,6},{16,24},{18,... | collective-permute-start | bytes 393224 | tf_op jit(solution)/shard_map/ppermute | solution.py:333
  29.0 7.3 %collective-permute-start.4 = (f32[256,128]{1,0:T(8,128)S(1)}, f32[256,128]{1,0:T(8,128)S(1)}, u32[]{:S(2)}, u32[]{:S(2)}) collective-permute-start(f32[256,128]{1,0:T(8,128)S(1)} %add.19), channel_id=1, source_target_pairs={{0,16},{2,18},{4,20},{6,22},{8,24},{10,26},{12,28},{14,30},{16,0},... | collective-permute-start | bytes 393224 | tf_op jit(solution)/shard_map/ppermute | solution.py:333
  42.6 1.4 %collective-permute-start.5 = (f32[8,8,512]{2,1,0:T(8,128)S(1)}, f32[8,8,512]{2,1,0:T(8,128)S(1)}, u32[]{:S(2)}, u32[]{:S(2)}) collective-permute-start(f32[8,8,512]{2,1,0:T(8,128)S(1)} %constant_dynamic-slice_fusion), channel_id=1, source_target_pairs={{0,1},{1,0},{2,3},{3,2},{4,5},{5,4},{6,7},{7,6},{8,9},{9,8},{10,11... | collective-permute-start | bytes 393224 | tf_op jit(solution)/shard_map/ppermute | solution.py:317

commit v5 on v4

--- a/solution.py
+++ b/solution.py
@@ -21,6 +21,8 @@
 WINDOW = 2 * BIN
 PICK_UNROLL = 16
 SCATTER_UNROLL = 16
+GROUPS = 2
+COST = 10**9
 MIB = 1024 * 1024
 
 
@@ -98,10 +100,10 @@
     return [total[k * pieces : (k + 1) * pieces] for k in range(len(values))]
 
 
-def sort_kernel(shape, cell_ref, pos_ref, *refs):
-    *place_refs, first_ref, last_ref, far_ref, prefix_ref = refs
+def sort_kernel(shape, groups, cell_ref, pos_ref, *refs):
+    *refs, prefix_ref = refs
     rows, levels, lons = shape
-    slots, obs = cell_ref.shape
+    _, obs = cell_ref.shape
     tiles, pieces = obs // LANES, obs // PIECE
     bins = rows // BIN
     bin_ids = small_ids((bins, LANES))
@@ -116,9 +118,12 @@
     middle = lons // 2
     signed = jnp.where(lons_of < middle, lons_of, middle - 1 - lons_of)
     keys, bins_of, signed = (v.astype(jnp.float32).astype(jnp.bfloat16) for v in (keys, bins_of, signed))
-    for slot in range(slots):
-        group = bins_of[slot : slot + 1]
-        hots = [one_hot(bin_ids, group[:, at * LANES : (at + 1) * LANES]) for at in range(tiles)]
+    outs = len(refs) // len(groups)
+    for slot, (group, mine) in enumerate([(g, m) for m, g in enumerate(groups) for _ in g]):
+        *place_refs, first_ref, last_ref, far_ref = refs[mine * outs : (mine + 1) * outs]
+        turn = slot - group[0]
+        in_bin = bins_of[slot : slot + 1]
+        hots = [one_hot(bin_ids, in_bin[:, at * LANES : (at + 1) * LANES]) for at in range(tiles)]
         prefix_ref[...] = jnp.dot(jnp.concatenate(hots, axis=0), counting, preferred_element_type=jnp.float32)
         total = jnp.zeros((bins, 128), jnp.float32)
         for at in range(tiles):
@@ -136,32 +141,32 @@
         key, lane = key.astype(jnp.int32), lane.astype(jnp.int32)
         row, level = quotient(key, levels)
         lon = jnp.where(lane < 0, middle - 1 - lane, lane)
-        here = pl.ds(slot * pieces, pieces)
+        here = pl.ds(turn * pieces, pieces)
         for near, place_ref, lane_ref in zip((PICK_LONS, SCATTER_LONS), place_refs[::2], place_refs[1::2]):
             part, lane = quotient(lon, near)
             place_ref[here, :] = (row * (lons // near) + part) * levels + level
             lane_ref[here, :] = lane.astype(jnp.float32)
-        group = quotient(row, BIN)[0] * BIN
-        first = jnp.minimum(group[:, :1], rows - WINDOW)
-        last = group[:, PIECE - 1 :] + BIN - 1
+        begin_row = quotient(row, BIN)[0] * BIN
+        first = jnp.minimum(begin_row[:, :1], rows - WINDOW)
+        last = begin_row[:, PIECE - 1 :] + BIN - 1
         begin = jnp.concatenate([first[:1], first[:-1]], axis=0)
         ends_tile = quotient(ids_of((pieces, 1), 0), LANES // PIECE)[1] == LANES // PIECE - 1
         far = jnp.max(jnp.where(ends_tile, last - begin, 0), axis=0, keepdims=True)
         as_row = lambda v: jnp.broadcast_to(v.astype(jnp.float32), (pieces, 128)).T[:1].astype(jnp.int32)
-        first_ref[pl.ds(slot, 1), :] = as_row(first)
-        last_ref[pl.ds(slot, 1), :] = as_row(last)
-        far_ref[pl.ds(slot, 1), :] = far
-
-
-def arrange_kernel(pos_ref, innov_ref, weight_ref, quality_ref, keep_ref, want_ref):
-    slots, obs = pos_ref.shape
-    pieces = obs // PIECE
-    keeps = two_parts(quality_ref[...].astype(jnp.float32) * weight_ref[...])
-    wants = two_parts(innov_ref[...])
-    for slot in range(slots):
-        at = slice(slot, slot + 1)
-        moved = permute(pos_ref[at, :], [part[at] for part in keeps + wants], pieces)
-        here = pl.ds(slot * pieces, pieces)
+        first_ref[pl.ds(turn, 1), :] = as_row(first)
+        last_ref[pl.ds(turn, 1), :] = as_row(last)
+        far_ref[pl.ds(turn, 1), :] = far
+
+
+def arrange_kernel(group, pos_ref, innov_ref, weight_ref, quality_ref, keep_ref, want_ref):
+    pieces = pos_ref.shape[1] // PIECE
+    mine = slice(group[0], group[-1] + 1)
+    keeps = two_parts(quality_ref[mine, :].astype(jnp.float32) * weight_ref[mine, :])
+    wants = two_parts(innov_ref[mine, :])
+    for turn, slot in enumerate(group):
+        at = slice(turn, turn + 1)
+        moved = permute(pos_ref[slot : slot + 1, :], [part[at] for part in keeps + wants], pieces)
+        here = pl.ds(turn * pieces, pieces)
         keep_ref[here, :] = moved[0] + moved[1]
         want_ref[here, :] = moved[2] + moved[3]
 
@@ -198,17 +203,21 @@
                     step(slot, tile, jnp.minimum(low_row, rows - WINDOW), low_row)
 
 
-def pick_kernel(sides, *refs):
-    low, high = halo(refs[:sides])
-    own_ref, circ_high_ref, circ_low_ref, ens_ref, place_ref, lane_ref, *refs = refs[sides:]
-    first_ref, last_ref, far_ref, out_ref, local_ref, *part_refs = refs
+def pick_kernel(group, sides, own_ref, circ_high_ref, circ_low_ref, *refs):
+    if sides:
+        low, high = halo(refs[:sides])
+        refs = refs[sides:]
+    ens_ref, place_ref, lane_ref, first_ref, last_ref, far_ref, out_ref, *part_refs = refs
     rows, levels, lons = own_ref.shape
-    slots = ens_ref.shape[0]
+    slots = len(group)
     tiles = first_ref.shape[1] // (LANES // PIECE)
-    mixed = smooth_rows(low, own_ref[...], high).reshape(rows * levels, lons)
-    local_ref[...] = smooth_lons(mixed, circ_high_ref[...], circ_low_ref[...]).reshape(local_ref.shape)
+    local_ref = own_ref
+    if sides:
+        local_ref, *part_refs = part_refs
+        mixed = smooth_rows(low, own_ref[...], high).reshape(rows * levels, lons)
+        local_ref[...] = smooth_lons(mixed, circ_high_ref[...], circ_low_ref[...]).reshape(local_ref.shape)
     for slot in range(slots):
-        field = ens_ref[slot].astype(jnp.float32) * local_ref[...]
+        field = ens_ref[group[slot]].astype(jnp.float32) * local_ref[...]
         first = field.astype(jnp.bfloat16).astype(jnp.float32)
         part_refs[slot][...] = jnp.concatenate([first, field - first], axis=1).astype(jnp.bfloat16)
     parts = lons // PICK_LONS
@@ -232,15 +241,16 @@
     over_windows(tiles, slots, rows, first_ref, last_ref, far_ref, PICK_UNROLL, step)
 
 
-def scatter_kernel(
-    norm_scale, seen_ref, want_ref, keep_ref, place_ref, lane_ref, ens_ref, first_ref, last_ref, far_ref,
-    back_ref, cost_ref, wres_ref, *grad_refs,
-):
-    slots, rows, levels, lons = ens_ref.shape
+def scatter_kernel(group, norm_scale, earlier, seen_ref, want_ref, keep_ref, place_ref, lane_ref, ens_ref, *refs):
+    before_refs, refs = refs[:earlier], refs[earlier:]
+    first_ref, last_ref, far_ref, back_ref, cost_ref, wres_ref, *grad_refs = refs
+    slots = len(group)
+    _, rows, levels, lons = ens_ref.shape
     tiles = first_ref.shape[1] // (LANES // PIECE)
     resid = seen_ref[...] * norm_scale - want_ref[...]
     wres_ref[...] = keep_ref[...] * resid
-    cost_ref[...] = jnp.sum(wres_ref[...] * resid).reshape(1, 1)
+    cost = jnp.sum(wres_ref[...] * resid).reshape(1, 1)
+    cost_ref[...] = cost + before_refs[1][...] if earlier else cost
     parts = lons // SCATTER_LONS
     size = WINDOW * parts * levels
     place_ids = small_ids((size, LANES))
@@ -262,8 +272,9 @@
     total = jnp.zeros((rows, levels, lons), jnp.float32)
     for slot in range(slots):
         grad = jnp.concatenate([grad_refs[slot][:, k] for k in range(parts)], axis=2)
-        total += ens_ref[slot].astype(jnp.float32) * grad
-    back_ref[...] = total * norm_scale
+        total += ens_ref[group[slot]].astype(jnp.float32) * grad
+    total = total * norm_scale
+    back_ref[...] = total + before_refs[0][...] if earlier else total
 
 
 def grad_kernel(sides, *refs):
@@ -305,7 +316,8 @@
     if count == 2:
         rows = field.shape[0]
         start = (rows - HALF) * (1 - lax.axis_index("lat"))
-        return swapped(lax.dynamic_slice_in_dim(field, start, HALF, 0))
+        edge = lax.dynamic_slice_in_dim(field, start, HALF, 0)
+        return [lax.ppermute(edge, "lat", [(0, 1), (1, 0)])]
     forward = [(i, i + 1) for i in range(count - 1)]
     backward = [(target, source) for source, target in forward]
     low = lax.ppermute(field[-HALF:], "lat", forward)
@@ -313,10 +325,6 @@
     return [low, high]
 
 
-def swapped(edge):
-    return [lax.ppermute(edge, "lat", [(0, 1), (1, 0)])]
-
-
 def halo(refs):
     if len(refs) == 2:
         return refs[0][...], refs[1][...]
@@ -324,14 +332,13 @@
     return jnp.where(last, refs[0][...], 0.0), jnp.where(last, 0.0, refs[0][...])
 
 
-def summed(value, axis):
+def summed(value, axis, turn=0):
     count = lax.axis_size(axis)
     if count & (count - 1):
         return lax.psum(value, axis)
-    away = 1
-    while away < count:
+    aways = [1 << k for k in range(count.bit_length() - 1)]
+    for away in aways[turn:] + aways[:turn]:
         value = value + lax.ppermute(value, axis, [(i, i ^ away) for i in range(count)])
-        away *= 2
     return value
 
 
@@ -339,43 +346,46 @@
     return jax.ShapeDtypeStruct(shape, kind)
 
 
-def sort_cells(obs_cell, shape):
+def sort_cells(obs_cell, shape, groups):
     slots, obs = obs_cell.shape
-    tiles = obs // LANES
-    whole, ordered, bound = (slots, obs), (slots * obs // PIECE, PIECE), (slots, obs // PIECE)
-    kinds = [like(whole, jnp.int32)] + [like(ordered, jnp.int32), like(ordered)] * 2
-    kinds += [like(bound, jnp.int32), like(bound, jnp.int32), like((slots, 1), jnp.int32)]
-    scratch = [pltpu.VMEM((tiles * shape[0] // BIN, LANES + 128), jnp.float32)]
-    pos, *ats, first, last, far = call(functools.partial(sort_kernel, shape), kinds, scratch, 10**9, obs_cell)
-    return pos, ats[:2], ats[2:], (first, last, far)
-
-
-def arrange(pos, innovation, obs_weight, quality):
-    ordered = like((pos.size // PIECE, PIECE))
-    return call(arrange_kernel, [ordered, ordered], [], 10**9, pos, innovation, obs_weight, quality)
-
-
-def pick(sides, own, circ, ens, at, bounds):
+    kinds = [like((slots, obs), jnp.int32)]
+    for group in groups:
+        ordered, bound = (len(group) * obs // PIECE, PIECE), (len(group), obs // PIECE)
+        kinds += [like(ordered, jnp.int32), like(ordered)] * 2
+        kinds += [like(bound, jnp.int32), like(bound, jnp.int32), like((len(group), 1), jnp.int32)]
+    scratch = [pltpu.VMEM((obs // LANES * shape[0] // BIN, LANES + 128), jnp.float32)]
+    pos, *outs = call(functools.partial(sort_kernel, shape, groups), kinds, scratch, COST, obs_cell)
+    outs = [outs[k : k + 7] for k in range(0, len(outs), 7)]
+    return pos, [(out[:2], out[2:4], out[4:]) for out in outs]
+
+
+def arrange(pos, innovation, obs_weight, quality, group):
+    ordered = like((len(group) * pos.shape[1] // PIECE, PIECE))
+    body = functools.partial(arrange_kernel, group)
+    return call(body, [ordered, ordered], [], COST, pos, innovation, obs_weight, quality)
+
+
+def pick(sides, own, circ, ens, at, bounds, group):
     rows, levels, lons = own.shape
-    scratch = [pltpu.VMEM(own.shape, jnp.float32)]
-    scratch += [pltpu.VMEM((rows, 2 * levels, lons), jnp.bfloat16)] * ens.shape[0]
-    body = functools.partial(pick_kernel, len(sides))
-    return call(body, like(at[0].shape), scratch, 10**9, *sides, own, *circ, ens, *at, scalars=bounds)
-
-
-def scatter(seen, want, keep, ens, at, bounds, norm_scale):
-    slots, rows, levels, lons = ens.shape
+    kinds = [like(at[0].shape)] + [like(own.shape)] * (len(sides) > 0)
+    scratch = [pltpu.VMEM((rows, 2 * levels, lons), jnp.bfloat16)] * len(group)
+    body = functools.partial(pick_kernel, group, len(sides))
+    return call(body, kinds, scratch, COST, own, *circ, *sides, ens, *at, scalars=bounds)
+
+
+def scatter(seen, want, keep, ens, at, bounds, norm_scale, group, earlier):
+    _, rows, levels, lons = ens.shape
     scratch = [pltpu.VMEM(seen.shape, jnp.float32)]
-    scratch += [pltpu.VMEM((rows, lons // SCATTER_LONS, levels, SCATTER_LONS), jnp.float32)] * slots
+    scratch += [pltpu.VMEM((rows, lons // SCATTER_LONS, levels, SCATTER_LONS), jnp.float32)] * len(group)
     kinds = [like((rows, levels, lons)), like((1, 1))]
-    body = functools.partial(scatter_kernel, norm_scale)
-    return call(body, kinds, scratch, 10**9, seen, want, keep, *at, ens, scalars=bounds)
+    body = functools.partial(scatter_kernel, group, norm_scale, len(earlier))
+    return call(body, kinds, scratch, COST, seen, want, keep, *at, ens, *earlier, scalars=bounds)
 
 
 def gradient(sides, own, circ, weights, obs_cost, devices):
     kinds = [like(own.shape), like((devices, 128))]
     body = functools.partial(grad_kernel, len(sides))
-    return call(body, kinds, [], 10**9, *sides, own, *circ, weights, obs_cost)
+    return call(body, kinds, [], COST, *sides, own, *circ, weights, obs_cost)
 
 
 def local(ensemble, weights, obs_cell, innovation, obs_weight, quality):
@@ -384,12 +394,23 @@
     norm_scale = 1.0 / math.sqrt(members - 1)
     ens, own = ensemble[0], weights[0]
     circ = [jnp.asarray(part) for part in circulant_parts(lons)]
+    slots = obs_cell.shape[0]
+    size = slots // GROUPS
+    groups = [range(k, k + size) for k in range(0, slots, size)]
     sides = edges(own)
-    pos, pick_at, scatter_at, bounds = sort_cells(obs_cell, own.shape)
-    keep, want = arrange(pos, innovation, obs_weight, quality)
-    picked = pick(sides, own, circ, ens, pick_at, bounds)
-    seen = summed(picked, "mem")
-    back, obs_cost = scatter(seen, want, keep, ens, scatter_at, bounds, norm_scale)
+    pos, ordered = sort_cells(obs_cell, own.shape, groups)
+    arranged = [arrange(pos, innovation, obs_weight, quality, group) for group in groups]
+    local_weights, seen = None, []
+    for turn, (group, (pick_at, _, bounds)) in enumerate(zip(groups, ordered)):
+        if turn == 0:
+            picked, local_weights = pick(sides, own, circ, ens, pick_at, bounds, group)
+        else:
+            (picked,) = pick([], local_weights, circ, ens, pick_at, bounds, group)
+        seen.append(summed(picked, "mem", 2 * turn))
+    sofar = []
+    for group, total, (keep, want), (_, scatter_at, bounds) in zip(groups, seen, arranged, ordered):
+        sofar = scatter(total, want, keep, ens, scatter_at, bounds, norm_scale, group, sofar)
+    back, obs_cost = sofar
     grad, sums = gradient(edges(back), back, circ, own, obs_cost, members * bands)
     sums = lax.all_to_all(sums, ("mem", "lat"), 0, 0, tiled=True)
     body = functools.partial(update_kernel, members, float(members * bands * rows * levels * lons))

time: 59.6 us -> 56.7 us (0.951)
  waiting for transfers between devices: 12.5 us -> 2.47 us
  starting transfers between devices: 9.39 us -> 14.4 us
  Pallas kernels: 22.9 us -> 25.7 us
  blocking collectives: 12.7 us -> 12 us
    ppermute x4 -> x8, waiting for transfers between devices: 11.2 us -> 1.13 us  [summed(): lax.ppermute(value, axis, [(i, i ^ away) for i in range(count)])]
    ppermute x4 -> x8, starting transfers between devices: 8.8 us -> 13.8 us  [summed(): lax.ppermute(value, axis, [(i, i ^ away) for i in range(count)])]
    pallas_call x6 -> x9, Pallas kernels: 22.9 us -> 25.7 us  [call(): pl.pallas_call(body, out_shape=out_shape, in_specs=[vmem] * len(operands)...]
    all_to_all x1, blocking collectives: 12.7 us -> 12 us  [local(): sums = lax.all_to_all(sums, ('mem', 'lat'), 0, 0, tiled=True)]
  transfers between devices with their start and end apart: 6 -> 10, of which waited for: 5 -> 2; matrix products, arithmetic and copies ran while one was open for 0% -> 0% of each run, Pallas kernels for 15% -> 27%
where the time goes in v5:
time: 56.7 us; the launch traced here: 56.5 us
  Pallas kernels  25.7 us (45%)
  starting transfers between devices  14.4 us (25%)
  blocking collectives  12 us (21%)
  waiting for transfers between devices  2.47 us (4%)
  local copies, waits for them, and re-layouts  1.02 us (2%)
  between operations  0.83 us (1%)
    pallas_call x9, Pallas kernels, call(): pl.pallas_call(body, out_shape=out_shape, in_specs=[vmem] * len(operands)...  25.7 us
    ppermute x8, starting transfers between devices, summed(): lax.ppermute(value, axis, [(i, i ^ away) for i in range(count)])  13.8 us
    all_to_all x1, blocking collectives, local(): sums = lax.all_to_all(sums, ('mem', 'lat'), 0, 0, tiled=True)  12 us
    ppermute x2, waiting for transfers between devices, edges(): return [lax.ppermute(edge, 'lat', [(0, 1), (1, 0)])]  1.34 us
  transfers between devices with their start and end apart: 10, of which 2 were waited for; matrix products, arithmetic and copies ran while one was open for 0% of the time, Pallas kernels for 27%

profile of v5, /device:TPU:0, one launch (start us, length us, event | category | flops | bytes accessed | tf_op | source)
XLA Modules:
  0.0 56.5 jit_solution(8202957733844945019)
XLA Ops:
  0.6 1.0 %dynamic-slice_bitcast_fusion = f32[8,8,512]{2,1,0:T(8,128)S(1)} fusion(f32[1,32,8,512]{3,2,1,0:T(8,128)} %param.9, s32[]{:T(128)S(6)} %select_n.4), kind=kLoop, calls=%fused_computation | loop fusion | bytes 262148 | tf_op jit(solution)/shard_map/dynamic_slice | solution.py:319
  1.7 0.5 collective-permute-start
  2.2 4.3 %shard_map.95 = (s32[4,8192]{1,0:T(4,128)S(1)}, s32[128,128]{1,0:T(8,128)S(1)}, f32[128,128]{1,0:T(8,128)S(1)}, s32[128,128]{1,0:T(8,128)S(1)}, f32[128,128]{1,0...) custom-call(s32[4,8192]{1,0:T(4,128)S(1)} %copy-done.2), custom_call_target="tpu_custom_call" | custom-call | flops 1000000000 | bytes 2097152 | tf_op jit(solution)/shard_map/pallas_call | solution.py:303
  6.5 3.3 %shard_map.96 = (f32[128,128]{1,0:T(8,128)S(1)}, f32[32,8,512]{2,1,0:T(8,128)S(1)}) custom-call(f32[32,8,512]{2,1,0:T(8,128)S(1)} %bitcast.10, bf16[512,512]{1,0:T(8,128)(2,1)S(1)} %copy-done.6, bf16[512,512]{1,0:T(8,128)(2,1)S(1)} %copy-done.7, f32[8,8,512]{2,1,0:T(8,128)S(1)} %collective-permute-done.refs_0_, bf16[4,32,8,512]{3,2,1,0:T(8,128)(2,1)S(1)} %bitcast.15, ...), custom_call_target="tpu_custom_call" | custom-call | flops 1000000000 | bytes 2097152 | tf_op jit(solution)/shard_map/pallas_call | solution.py:303
  9.8 2.6 %collective-permute-start.5 = (f32[128,128]{1,0:T(8,128)S(1)}, f32[128,128]{1,0:T(8,128)S(1)}, u32[]{:S(2)}, u32[]{:S(2)}) collective-permute-start(f32[128,128]{1,0:T(8,128)S(1)} %get-tuple-element.47), channel_id=1, source_target_pairs={{0,2},{2,0},{4,6},{6,4},{8,10},{10,8},{12,14},{14,12},{16,18},{18,... | collective-permute-start | bytes 196616 | tf_op jit(solution)/shard_map/ppermute | solution.py:341
  12.4 2.7 %shard_map.97 = f32[128,128]{1,0:T(8,128)S(1)} custom-call(f32[32,8,512]{2,1,0:T(8,128)S(1)} %get-tuple-element.36.own_ref, bf16[512,512]{1,0:T(8,128)(2,1)S(1)} %copy-done.6, bf16[512,512]{1,0:T(8,128)(2,1)S(1)} %copy-done.7, bf16[4,32,8,512]{3,2,1,0:T(8,128)(2,1)S(1)} %bitcast.16, s32[128,128]{1,0:T(8,128)S(1)} %get-tuple-element.37.refs_1_, ...), custom_call_target="tpu_custom_call" | custom-call | flops 1000000000 | bytes 2097152 | tf_op jit(solution)/shard_map/pallas_call | solution.py:303
  15.1 1.6 %collective-permute-start.1 = (f32[128,128]{1,0:T(8,128)S(1)}, f32[128,128]{1,0:T(8,128)S(1)}, u32[]{:S(2)}, u32[]{:S(2)}) collective-permute-start(f32[128,128]{1,0:T(8,128)S(1)} %shard_map.97), channel_id=1, source_target_pairs={{0,8},{2,10},{4,12},{6,14},{8,0},{10,2},{12,4},{14,6},{16,24},{18,... | collective-permute-start | bytes 196616 | tf_op jit(solution)/shard_map/ppermute | solution.py:341
  16.7 1.6 %collective-permute-start.6 = (f32[128,128]{1,0:T(8,128)S(1)}, f32[128,128]{1,0:T(8,128)S(1)}, u32[]{:S(2)}, u32[]{:S(2)}) collective-permute-start(f32[128,128]{1,0:T(8,128)S(1)} %add.33), channel_id=1, source_target_pairs={{0,4},{2,6},{4,0},{6,2},{8,12},{10,14},{12,8},{14,10},{16,20},{18,... | collective-permute-start | bytes 196616 | tf_op jit(solution)/shard_map/ppermute | solution.py:341
  18.3 1.1 %collective-permute-done.1 = f32[128,128]{1,0:T(8,128)S(1)} collective-permute-done((f32[128,128]{1,0:T(8,128)S(1)}, f32[128,128]{1,0:T(8,128)S(1)}, u32[]{:S(2)}, u32[]{:S(2)}) %collective-permute-start.1) | collective-permute-done | bytes 65568 | tf_op jit(solution)/shard_map/ppermute | solution.py:341
  19.4 2.7 %collective-permute-start.2 = (f32[128,128]{1,0:T(8,128)S(1)}, f32[128,128]{1,0:T(8,128)S(1)}, u32[]{:S(2)}, u32[]{:S(2)}) collective-permute-start(f32[128,128]{1,0:T(8,128)S(1)} %add.29), channel_id=1, source_target_pairs={{0,16},{2,18},{4,20},{6,22},{8,24},{10,26},{12,28},{14,30},{16,0},... | collective-permute-start | bytes 196616 | tf_op jit(solution)/shard_map/ppermute | solution.py:341
  22.1 1.6 %collective-permute-start.7 = (f32[128,128]{1,0:T(8,128)S(1)}, f32[128,128]{1,0:T(8,128)S(1)}, u32[]{:S(2)}, u32[]{:S(2)}) collective-permute-start(f32[128,128]{1,0:T(8,128)S(1)} %add.34), channel_id=1, source_target_pairs={{0,8},{2,10},{4,12},{6,14},{8,0},{10,2},{12,4},{14,6},{16,24},{18,... | collective-permute-start | bytes 196616 | tf_op jit(solution)/shard_map/ppermute | solution.py:341
  23.7 2.3 %shard_map.98 = (f32[128,128]{1,0:T(8,128)S(1)}, f32[128,128]{1,0:T(8,128)S(1)}) custom-call(s32[4,8192]{1,0:T(4,128)S(1)} %get-tuple-element.42.pos_ref, f32[4,8192]{1,0:T(4,128)S(1)} %copy-done.3, f32[4,8192]{1,0:T(4,128)S(1)} %copy-done.4, s32[4,8192]{1,0:T(4,128)S(1)} %copy-done.5), custom_call_target="tpu_custom_call" | custom-call | flops 1000000000 | bytes 2097152 | tf_op jit(solution)/shard_map/pallas_call | solution.py:303
  26.0 0.0 collective-permute-done.2
  26.1 0.6 %collective-permute-start.3 = (f32[128,128]{1,0:T(8,128)S(1)}, f32[128,128]{1,0:T(8,128)S(1)}, u32[]{:S(2)}, u32[]{:S(2)}) collective-permute-start(f32[128,128]{1,0:T(8,128)S(1)} %add.30), channel_id=1, source_target_pairs={{0,2},{2,0},{4,6},{6,4},{8,10},{10,8},{12,14},{14,12},{16,18},{18,... | collective-permute-start | bytes 196616 | tf_op jit(solution)/shard_map/ppermute | solution.py:341
  26.7 1.5 %collective-permute-start.8 = (f32[128,128]{1,0:T(8,128)S(1)}, f32[128,128]{1,0:T(8,128)S(1)}, u32[]{:S(2)}, u32[]{:S(2)}) collective-permute-start(f32[128,128]{1,0:T(8,128)S(1)} %add.35), channel_id=1, source_target_pairs={{0,16},{2,18},{4,20},{6,22},{8,24},{10,26},{12,28},{14,30},{16,0},... | collective-permute-start | bytes 196616 | tf_op jit(solution)/shard_map/ppermute | solution.py:341
  28.2 2.3 %shard_map.99 = (f32[128,128]{1,0:T(8,128)S(1)}, f32[128,128]{1,0:T(8,128)S(1)}) custom-call(s32[4,8192]{1,0:T(4,128)S(1)} %get-tuple-element.42.pos_ref, f32[4,8192]{1,0:T(4,128)S(1)} %copy-done.3, f32[4,8192]{1,0:T(4,128)S(1)} %copy-done.4, s32[4,8192]{1,0:T(4,128)S(1)} %copy-done.5), custom_call_target="tpu_custom_call" | custom-call | flops 1000000000 | bytes 2097152 | tf_op jit(solution)/shard_map/pallas_call | solution.py:303
  30.5 1.6 %collective-permute-start.4 = (f32[128,128]{1,0:T(8,128)S(1)}, f32[128,128]{1,0:T(8,128)S(1)}, u32[]{:S(2)}, u32[]{:S(2)}) collective-permute-start(f32[128,128]{1,0:T(8,128)S(1)} %add.31), channel_id=1, source_target_pairs={{0,4},{2,6},{4,0},{6,2},{8,12},{10,14},{12,8},{14,10},{16,20},{18,... | collective-permute-start | bytes 196616 | tf_op jit(solution)/shard_map/ppermute | solution.py:341
  32.1 3.8 %shard_map.100 = (f32[32,8,512]{2,1,0:T(8,128)S(1)}, f32[1,1]{1,0:T(1,128)}) custom-call(f32[128,128]{1,0:T(8,128)S(1)} %add.36.seen_ref, f32[128,128]{1,0:T(8,128)S(1)} %get-tuple-element.48.want_ref, f32[128,128]{1,0:T(8,128)S(1)} %get-tuple-element.49.keep_ref, s32[128,128]{1,0:T(8,128)S(1)} %get-tuple-element.50.place_ref, ...), custom_call_target="tpu_custom_call" | custom-call | flops 1000000000 | bytes 2097152 | tf_op jit(solution)/shard_map/pallas_call | solution.py:303
  35.9 4.4 %shard_map.101 = (f32[32,8,512]{2,1,0:T(8,128)S(1)}, f32[1,1]{1,0:T(1,128)}) custom-call(f32[128,128]{1,0:T(8,128)S(1)} %add.32.seen_ref, f32[128,128]{1,0:T(8,128)S(1)} %get-tuple-element.43.want_ref, f32[128,128]{1,0:T(8,128)S(1)} %get-tuple-element.44.keep_ref, s32[128,128]{1,0:T(8,128)S(1)} %get-tuple-element.45.place_ref, ...), custom_call_target="tpu_custom_call" | custom-call | flops 1000000000 | bytes 2097152 | tf_op jit(solution)/shard_map/pallas_call | solution.py:303
  40.3 0.1 collective-permute-start.9
  40.4 1.3 %collective-permute-done.9.refs_0_ = f32[8,8,512]{2,1,0:T(8,128)S(1)} collective-permute-done((f32[8,8,512]{2,1,0:T(8,128)S(1)}, f32[8,8,512]{2,1,0:T(8,128)S(1)}, u32[]{:S(2)}, u32[]{:S(2)}) %collective-permute-start.9) | collective-permute-done | bytes 131104 | tf_op jit(solution)/shard_map/ppermute | solution.py:320
  41.8 1.7 %shard_map.102 = (f32[32,8,512]{2,1,0:T(8,128)S(1)}, f32[32,128]{1,0:T(8,128)S(1)}) custom-call(f32[8,8,512]{2,1,0:T(8,128)S(1)} %collective-permute-done.9.refs_0_, f32[32,8,512]{2,1,0:T(8,128)S(1)} %get-tuple-element.54.refs_1_, bf16[512,512]{1,0:T(8,128)(2,1)S(1)} %copy-done.6, bf16[512,512]{1,0:T(8,128)(2,1)S(1)} %copy-done.7, ...), custom_call_target="tpu_custom_call" | custom-call | flops 1000000000 | bytes 2097152 | tf_op jit(solution)/shard_map/pallas_call | solution.py:303
  43.5 12.0 %all_to_all.11 = f32[32,1,128]{2,1,0:T(1,128)S(1)} all-to-all(f32[32,1,128]{2,1,0:T(1,128)S(1)} %bitcast.14), channel_id=1, replica_groups=mesh['mem'=16,'lat'=2] {'mem','lat'}, dimensions={0} | all-to-all | bytes 32768 | tf_op jit(solution)/shard_map/all_to_all | solution.py:415
  55.5 1.0 %shard_map.103 = (f32[32,8,512]{2,1,0:T(8,128)}, f32[1,1]{1,0:T(1,128)}) custom-call(f32[32,128]{1,0:T(8,128)S(1)} %bitcast.13, f32[32,8,512]{2,1,0:T(8,128)S(1)} %bitcast.12, f32[32,8,512]{2,1,0:T(8,128)S(1)} %get-tuple-element.57.grad_ref), custom_call_target="tpu_custom_call" | custom-call | flops 100000000 | bytes 2097152 | tf_op jit(solution)/shard_map/pallas_call | solution.py:303
  (32 shorter events, 0.2 us)
Async XLA Ops:
  0.6 1.5 %copy-start.2 = (s32[4,8192]{1,0:T(4,128)S(1)}, s32[4,8192]{1,0:T(4,128)}, u32[]{:S(2)}) copy-start(s32[4,8192]{1,0:T(4,128)} %cell_ref.1) | copy-start | bytes 393220
  1.6 4.9 %copy-start = (f32[1,32,8,512]{3,2,1,0:T(8,128)S(1)}, f32[1,32,8,512]{3,2,1,0:T(8,128)}, u32[]{:S(2)}) copy-start(f32[1,32,8,512]{3,2,1,0:T(8,128)} %param.9) | copy-start | bytes 1572868
  1.6 4.9 %copy-start.1 = (bf16[1,4,32,8,512]{4,3,2,1,0:T(8,128)(2,1)S(1)}, bf16[1,4,32,8,512]{4,3,2,1,0:T(8,128)(2,1)}, u32[]{:S(2)}) copy-start(bf16[1,4,32,8,512]{4,3,2,1,0:T(8,128)(2,1)} %param.8) | copy-start | bytes 3145732
  1.6 4.9 %copy-start.6 = (bf16[512,512]{1,0:T(8,128)(2,1)S(1)}, bf16[512,512]{1,0:T(8,128)(2,1)}, u32[]{:S(2)}) copy-start(bf16[512,512]{1,0:T(8,128)(2,1)} %constant.17.clone.circ_high_ref.refs_2_) | copy-start | bytes 1572868
  1.6 4.9 %copy-start.7 = (bf16[512,512]{1,0:T(8,128)(2,1)S(1)}, bf16[512,512]{1,0:T(8,128)(2,1)}, u32[]{:S(2)}) copy-start(bf16[512,512]{1,0:T(8,128)(2,1)} %constant.18.clone.circ_low_ref.refs_3_) | copy-start | bytes 1572868
  1.7 4.8 %collective-permute-start = (f32[8,8,512]{2,1,0:T(8,128)S(1)}, f32[8,8,512]{2,1,0:T(8,128)S(1)}, u32[]{:S(2)}, u32[]{:S(2)}) collective-permute-start(f32[8,8,512]{2,1,0:T(8,128)S(1)} %dynamic-slice_bitcast_fusion), channel_id=1, source_target_pairs={{0,1},{1,0},{2,3},{3,2},{4,5},{5,4},{6,7},{7,6},{8,9},{9,8},{10,11... | collective-permute-start | bytes 393224 | tf_op jit(solution)/shard_map/ppermute | solution.py:320
  9.8 6.9 %collective-permute-start.5 = (f32[128,128]{1,0:T(8,128)S(1)}, f32[128,128]{1,0:T(8,128)S(1)}, u32[]{:S(2)}, u32[]{:S(2)}) collective-permute-start(f32[128,128]{1,0:T(8,128)S(1)} %get-tuple-element.47), channel_id=1, source_target_pairs={{0,2},{2,0},{4,6},{6,4},{8,10},{10,8},{12,14},{14,12},{16,18},{18,... | collective-permute-start | bytes 196616 | tf_op jit(solution)/shard_map/ppermute | solution.py:341
  15.1 4.3 %collective-permute-start.1 = (f32[128,128]{1,0:T(8,128)S(1)}, f32[128,128]{1,0:T(8,128)S(1)}, u32[]{:S(2)}, u32[]{:S(2)}) collective-permute-start(f32[128,128]{1,0:T(8,128)S(1)} %shard_map.97), channel_id=1, source_target_pairs={{0,8},{2,10},{4,12},{6,14},{8,0},{10,2},{12,4},{14,6},{16,24},{18,... | collective-permute-start | bytes 196616 | tf_op jit(solution)/shard_map/ppermute | solution.py:341
  16.7 5.4 %collective-permute-start.6 = (f32[128,128]{1,0:T(8,128)S(1)}, f32[128,128]{1,0:T(8,128)S(1)}, u32[]{:S(2)}, u32[]{:S(2)}) collective-permute-start(f32[128,128]{1,0:T(8,128)S(1)} %add.33), channel_id=1, source_target_pairs={{0,4},{2,6},{4,0},{6,2},{8,12},{10,14},{12,8},{14,10},{16,20},{18,... | collective-permute-start | bytes 196616 | tf_op jit(solution)/shard_map/ppermute | solution.py:341
  19.4 4.3 %copy-start.4 = (f32[4,8192]{1,0:T(4,128)S(1)}, f32[4,8192]{1,0:T(4,128)}, u32[]{:S(2)}) copy-start(f32[4,8192]{1,0:T(4,128)} %weight_ref.3) | copy-start | bytes 393220
  19.4 4.3 %copy-start.5 = (s32[4,8192]{1,0:T(4,128)S(1)}, s32[4,8192]{1,0:T(4,128)}, u32[]{:S(2)}) copy-start(s32[4,8192]{1,0:T(4,128)} %quality_ref.3) | copy-start | bytes 393220
  19.4 4.3 %copy-start.3 = (f32[4,8192]{1,0:T(4,128)S(1)}, f32[4,8192]{1,0:T(4,128)}, u32[]{:S(2)}) copy-start(f32[4,8192]{1,0:T(4,128)} %innov_ref.3) | copy-start | bytes 393220
  19.4 6.6 %collective-permute-start.2 = (f32[128,128]{1,0:T(8,128)S(1)}, f32[128,128]{1,0:T(8,128)S(1)}, u32[]{:S(2)}, u32[]{:S(2)}) collective-permute-start(f32[128,128]{1,0:T(8,128)S(1)} %add.29), channel_id=1, source_target_pairs={{0,16},{2,18},{4,20},{6,22},{8,24},{10,26},{12,28},{14,30},{16,0},... | collective-permute-start | bytes 196616 | tf_op jit(solution)/shard_map/ppermute | solution.py:341
  22.1 4.6 %collective-permute-start.7 = (f32[128,128]{1,0:T(8,128)S(1)}, f32[128,128]{1,0:T(8,128)S(1)}, u32[]{:S(2)}, u32[]{:S(2)}) collective-permute-start(f32[128,128]{1,0:T(8,128)S(1)} %add.34), channel_id=1, source_target_pairs={{0,8},{2,10},{4,12},{6,14},{8,0},{10,2},{12,4},{14,6},{16,24},{18,... | collective-permute-start | bytes 196616 | tf_op jit(solution)/shard_map/ppermute | solution.py:341
  26.1 4.4 %collective-permute-start.3 = (f32[128,128]{1,0:T(8,128)S(1)}, f32[128,128]{1,0:T(8,128)S(1)}, u32[]{:S(2)}, u32[]{:S(2)}) collective-permute-start(f32[128,128]{1,0:T(8,128)S(1)} %add.30), channel_id=1, source_target_pairs={{0,2},{2,0},{4,6},{6,4},{8,10},{10,8},{12,14},{14,12},{16,18},{18,... | collective-permute-start | bytes 196616 | tf_op jit(solution)/shard_map/ppermute | solution.py:341
  26.7 5.4 %collective-permute-start.8 = (f32[128,128]{1,0:T(8,128)S(1)}, f32[128,128]{1,0:T(8,128)S(1)}, u32[]{:S(2)}, u32[]{:S(2)}) collective-permute-start(f32[128,128]{1,0:T(8,128)S(1)} %add.35), channel_id=1, source_target_pairs={{0,16},{2,18},{4,20},{6,22},{8,24},{10,26},{12,28},{14,30},{16,0},... | collective-permute-start | bytes 196616 | tf_op jit(solution)/shard_map/ppermute | solution.py:341
  30.5 5.4 %collective-permute-start.4 = (f32[128,128]{1,0:T(8,128)S(1)}, f32[128,128]{1,0:T(8,128)S(1)}, u32[]{:S(2)}, u32[]{:S(2)}) collective-permute-start(f32[128,128]{1,0:T(8,128)S(1)} %add.31), channel_id=1, source_target_pairs={{0,4},{2,6},{4,0},{6,2},{8,12},{10,14},{12,8},{14,10},{16,20},{18,... | collective-permute-start | bytes 196616 | tf_op jit(solution)/shard_map/ppermute | solution.py:341
  40.3 1.4 %collective-permute-start.9 = (f32[8,8,512]{2,1,0:T(8,128)S(1)}, f32[8,8,512]{2,1,0:T(8,128)S(1)}, u32[]{:S(2)}, u32[]{:S(2)}) collective-permute-start(f32[8,8,512]{2,1,0:T(8,128)S(1)} %constant_dynamic-slice_fusion), channel_id=1, source_target_pairs={{0,1},{1,0},{2,3},{3,2},{4,5},{5,4},{6,7},{7,6},{8,9},{9,8},{10,11... | collective-permute-start | bytes 393224 | tf_op jit(solution)/shard_map/ppermute | solution.py:320

commit v6 on v5

--- a/solution.py
+++ b/solution.py
@@ -120,7 +120,7 @@
     keys, bins_of, signed = (v.astype(jnp.float32).astype(jnp.bfloat16) for v in (keys, bins_of, signed))
     outs = len(refs) // len(groups)
     for slot, (group, mine) in enumerate([(g, m) for m, g in enumerate(groups) for _ in g]):
-        *place_refs, first_ref, last_ref, far_ref = refs[mine * outs : (mine + 1) * outs]
+        *place_refs, bounds_ref = refs[mine * outs : (mine + 1) * outs]
         turn = slot - group[0]
         in_bin = bins_of[slot : slot + 1]
         hots = [one_hot(bin_ids, in_bin[:, at * LANES : (at + 1) * LANES]) for at in range(tiles)]
@@ -152,10 +152,10 @@
         begin = jnp.concatenate([first[:1], first[:-1]], axis=0)
         ends_tile = quotient(ids_of((pieces, 1), 0), LANES // PIECE)[1] == LANES // PIECE - 1
         far = jnp.max(jnp.where(ends_tile, last - begin, 0), axis=0, keepdims=True)
-        as_row = lambda v: jnp.broadcast_to(v.astype(jnp.float32), (pieces, 128)).T[:1].astype(jnp.int32)
-        first_ref[pl.ds(turn, 1), :] = as_row(first)
-        last_ref[pl.ds(turn, 1), :] = as_row(last)
-        far_ref[pl.ds(turn, 1), :] = far
+        spread = [jnp.broadcast_to(v.astype(jnp.float32), (pieces, 128)).T[:1].astype(jnp.int32) for v in (first, last)]
+        spread.append(jnp.broadcast_to(far, (1, pieces)))
+        for kind, v in enumerate(spread):
+            bounds_ref[pl.ds(kind * len(group) + turn, 1), pl.ds(0, pieces)] = v
 
 
 def arrange_kernel(group, pos_ref, innov_ref, weight_ref, quality_ref, keep_ref, want_ref):
@@ -183,21 +183,24 @@
     return jnp.where(place < (low_row - start) * per_row, -1, place)
 
 
-def over_windows(tiles, slots, rows, first_ref, last_ref, far_ref, unroll, step):
+def over_windows(tiles, slots, rows, bounds_ref, unroll, step):
+    parts = LANES // PIECE
+
     @pl.loop(0, tiles, unroll=unroll)
     def _(tile):
         for slot in range(slots):
-            step(slot, tile, first_ref[slot, tile * (LANES // PIECE)], None)
+            step(slot, tile, bounds_ref[slot, tile * parts], None)
 
     for slot in range(slots):
 
-        @pl.when(far_ref[slot, 0] >= WINDOW)
+        @pl.when(bounds_ref[2 * slots + slot, 0] >= WINDOW)
         def _():
             @pl.loop(0, tiles)
             def _(tile):
-                begin = first_ref[slot, tile * (LANES // PIECE)]
-
-                @pl.loop(1, lax.div(last_ref[slot, (tile + 1) * (LANES // PIECE) - 1] - begin, WINDOW) + 1)
+                begin = bounds_ref[slot, tile * parts]
+                end = bounds_ref[slots + slot, (tile + 1) * parts - 1]
+
+                @pl.loop(1, lax.div(end - begin, WINDOW) + 1)
                 def _(turn):
                     low_row = begin + turn * WINDOW
                     step(slot, tile, jnp.minimum(low_row, rows - WINDOW), low_row)
@@ -207,10 +210,12 @@
     if sides:
         low, high = halo(refs[:sides])
         refs = refs[sides:]
-    ens_ref, place_ref, lane_ref, first_ref, last_ref, far_ref, out_ref, *part_refs = refs
+    ens_ref, place_ref, lane_ref, bounds_in_ref, out_ref, *part_refs, bounds_ref, sem = refs
+    bounds_copy = pltpu.make_async_copy(bounds_in_ref, bounds_ref, sem)
+    bounds_copy.start()
     rows, levels, lons = own_ref.shape
     slots = len(group)
-    tiles = first_ref.shape[1] // (LANES // PIECE)
+    tiles = place_ref.shape[0] * PIECE // (slots * LANES)
     local_ref = own_ref
     if sides:
         local_ref, *part_refs = part_refs
@@ -238,18 +243,21 @@
             here, part = pl.ds(at * (LANES // PIECE) + k, 1), value[:, k * PIECE : (k + 1) * PIECE]
             out_ref[here, :] = part if low_row is None else out_ref[here, :] + part
 
-    over_windows(tiles, slots, rows, first_ref, last_ref, far_ref, PICK_UNROLL, step)
+    bounds_copy.wait()
+    over_windows(tiles, slots, rows, bounds_ref, PICK_UNROLL, step)
 
 
 def scatter_kernel(group, norm_scale, earlier, seen_ref, want_ref, keep_ref, place_ref, lane_ref, ens_ref, *refs):
     before_refs, refs = refs[:earlier], refs[earlier:]
-    first_ref, last_ref, far_ref, back_ref, cost_ref, wres_ref, *grad_refs = refs
+    bounds_in_ref, back_ref, cost_ref, wres_ref, *grad_refs, bounds_ref, sem = refs
+    bounds_copy = pltpu.make_async_copy(bounds_in_ref, bounds_ref, sem)
+    bounds_copy.start()
     slots = len(group)
     _, rows, levels, lons = ens_ref.shape
-    tiles = first_ref.shape[1] // (LANES // PIECE)
+    tiles = place_ref.shape[0] * PIECE // (slots * LANES)
     resid = seen_ref[...] * norm_scale - want_ref[...]
     wres_ref[...] = keep_ref[...] * resid
-    cost = jnp.sum(wres_ref[...] * resid).reshape(1, 1)
+    cost = jnp.sum((wres_ref[...] * resid).reshape(-1, *cost_ref.shape), axis=0)
     cost_ref[...] = cost + before_refs[1][...] if earlier else cost
     parts = lons // SCATTER_LONS
     size = WINDOW * parts * levels
@@ -268,7 +276,8 @@
         both = across(left, hot)
         grad_refs[slot][pl.ds(start, WINDOW)] += (both[:size] + both[size:]).reshape(WINDOW, parts, levels, SCATTER_LONS)
 
-    over_windows(tiles, slots, rows, first_ref, last_ref, far_ref, SCATTER_UNROLL, step)
+    bounds_copy.wait()
+    over_windows(tiles, slots, rows, bounds_ref, SCATTER_UNROLL, step)
     total = jnp.zeros((rows, levels, lons), jnp.float32)
     for slot in range(slots):
         grad = jnp.concatenate([grad_refs[slot][:, k] for k in range(parts)], axis=2)
@@ -288,7 +297,8 @@
     lane = lax.broadcasted_iota(jnp.int32, sums_ref.shape, 1)
     prior = jnp.sum(weights * weights)
     square = jnp.sum(grad * grad)
-    sums_ref[...] = jnp.where(lane == 0, square, jnp.where(lane == 1, prior, jnp.where(lane == 2, obs_cost_ref[...], 0.0)))
+    obs_cost = jnp.sum(obs_cost_ref[...])
+    sums_ref[...] = jnp.where(lane == 0, square, jnp.where(lane == 1, prior, jnp.where(lane == 2, obs_cost, 0.0)))
 
 
 def update_kernel(members, entries, sums_ref, own_ref, grad_ref, new_ref, cost_ref):
@@ -298,17 +308,17 @@
     cost_ref[...] = (0.5 * totals[:, 1:2] + 0.5 * totals[:, 2:3] / members) / entries
 
 
-def call(body, out_shape, scratch, flops, *operands, scalars=()):
-    vmem, smem = pl.BlockSpec(memory_space=pltpu.VMEM), pl.BlockSpec(memory_space=pltpu.SMEM)
+def call(body, out_shape, scratch, flops, *operands):
+    vmem = pl.BlockSpec(memory_space=pltpu.VMEM)
     return pl.pallas_call(
         body,
         out_shape=out_shape,
-        in_specs=[vmem] * len(operands) + [smem] * len(scalars),
+        in_specs=[vmem] * len(operands),
         out_specs=jax.tree.map(lambda _: vmem, out_shape),
         scratch_shapes=scratch,
         compiler_params=pltpu.CompilerParams(vmem_limit_bytes=48 * MIB),
         cost_estimate=pl.CostEstimate(flops=flops, bytes_accessed=2 * MIB, transcendentals=0),
-    )(*operands, *scalars)
+    )(*operands)
 
 
 def edges(field):
@@ -350,13 +360,13 @@
     slots, obs = obs_cell.shape
     kinds = [like((slots, obs), jnp.int32)]
     for group in groups:
-        ordered, bound = (len(group) * obs // PIECE, PIECE), (len(group), obs // PIECE)
+        ordered = (len(group) * obs // PIECE, PIECE)
         kinds += [like(ordered, jnp.int32), like(ordered)] * 2
-        kinds += [like(bound, jnp.int32), like(bound, jnp.int32), like((len(group), 1), jnp.int32)]
+        kinds += [like((-(-3 * len(group) // 8) * 8, -(-(obs // PIECE) // 128) * 128), jnp.int32)]
     scratch = [pltpu.VMEM((obs // LANES * shape[0] // BIN, LANES + 128), jnp.float32)]
     pos, *outs = call(functools.partial(sort_kernel, shape, groups), kinds, scratch, COST, obs_cell)
-    outs = [outs[k : k + 7] for k in range(0, len(outs), 7)]
-    return pos, [(out[:2], out[2:4], out[4:]) for out in outs]
+    outs = [outs[k : k + 5] for k in range(0, len(outs), 5)]
+    return pos, [(out[:2], out[2:4], out[4]) for out in outs]
 
 
 def arrange(pos, innovation, obs_weight, quality, group):
@@ -369,17 +379,19 @@
     rows, levels, lons = own.shape
     kinds = [like(at[0].shape)] + [like(own.shape)] * (len(sides) > 0)
     scratch = [pltpu.VMEM((rows, 2 * levels, lons), jnp.bfloat16)] * len(group)
+    scratch += [pltpu.SMEM(bounds.shape, jnp.int32), pltpu.SemaphoreType.DMA]
     body = functools.partial(pick_kernel, group, len(sides))
-    return call(body, kinds, scratch, COST, own, *circ, *sides, ens, *at, scalars=bounds)
+    return call(body, kinds, scratch, COST, own, *circ, *sides, ens, *at, bounds)
 
 
 def scatter(seen, want, keep, ens, at, bounds, norm_scale, group, earlier):
     _, rows, levels, lons = ens.shape
     scratch = [pltpu.VMEM(seen.shape, jnp.float32)]
     scratch += [pltpu.VMEM((rows, lons // SCATTER_LONS, levels, SCATTER_LONS), jnp.float32)] * len(group)
-    kinds = [like((rows, levels, lons)), like((1, 1))]
+    kinds = [like((rows, levels, lons)), like((8, 128))]
+    scratch += [pltpu.SMEM(bounds.shape, jnp.int32), pltpu.SemaphoreType.DMA]
     body = functools.partial(scatter_kernel, group, norm_scale, len(earlier))
-    return call(body, kinds, scratch, COST, seen, want, keep, *at, ens, *earlier, scalars=bounds)
+    return call(body, kinds, scratch, COST, seen, want, keep, *at, ens, *earlier, bounds)
 
 
 def gradient(sides, own, circ, weights, obs_cost, devices):

time: 56.7 us -> 53.7 us (0.947)
  Pallas kernels: 25.7 us -> 22.7 us
    pallas_call x9, Pallas kernels: 25.7 us -> 22.7 us  [call(): pl.pallas_call(body, out_shape=out_shape, in_specs=[vmem] * len(operands)...]
where the time goes in v6:
time: 53.7 us; the launch traced here: 53.6 us
  Pallas kernels  22.7 us (42%)
  starting transfers between devices  14.4 us (27%)
  blocking collectives  12 us (22%)
  waiting for transfers between devices  2.47 us (5%)
  local copies, waits for them, and re-layouts  1.03 us (2%)
  between operations  0.87 us (2%)
    pallas_call x9, Pallas kernels, call(): pl.pallas_call(body, out_shape=out_shape, in_specs=[vmem] * len(operands)...  22.7 us
    ppermute x8, starting transfers between devices, summed(): lax.ppermute(value, axis, [(i, i ^ away) for i in range(count)])  13.8 us
    all_to_all x1, blocking collectives, local(): sums = lax.all_to_all(sums, ('mem', 'lat'), 0, 0, tiled=True)  12 us
    ppermute x2, waiting for transfers between devices, edges(): return [lax.ppermute(edge, 'lat', [(0, 1), (1, 0)])]  1.34 us
    ppermute x8, waiting for transfers between devices, summed(): lax.ppermute(value, axis, [(i, i ^ away) for i in range(count)])  1.13 us
  transfers between devices with their start and end apart: 10, of which 2 were waited for; matrix products, arithmetic and copies ran while one was open for 0% of the time, Pallas kernels for 27%

profile of v6, /device:TPU:0, one launch (start us, length us, event | category | flops | bytes accessed | tf_op | source)
XLA Modules:
  0.0 53.6 jit_solution(15657185668672096636)
XLA Ops:
  0.6 1.0 %dynamic-slice_bitcast_fusion = f32[8,8,512]{2,1,0:T(8,128)S(1)} fusion(f32[1,32,8,512]{3,2,1,0:T(8,128)} %param.9, s32[]{:T(128)S(6)} %select_n.4), kind=kLoop, calls=%fused_computation | loop fusion | bytes 262148 | tf_op jit(solution)/shard_map/dynamic_slice | solution.py:329
  1.7 0.5 collective-permute-start
  2.2 4.3 %shard_map.95 = (s32[4,8192]{1,0:T(4,128)S(1)}, s32[128,128]{1,0:T(8,128)S(1)}, f32[128,128]{1,0:T(8,128)S(1)}, s32[128,128]{1,0:T(8,128)S(1)}, f32[128,128]{1,0...) custom-call(s32[4,8192]{1,0:T(4,128)S(1)} %copy-done.2), custom_call_target="tpu_custom_call" | custom-call | flops 1000000000 | bytes 2097152 | tf_op jit(solution)/shard_map/pallas_call | solution.py:313
  6.5 2.7 %shard_map.96 = (f32[128,128]{1,0:T(8,128)S(1)}, f32[32,8,512]{2,1,0:T(8,128)S(1)}) custom-call(f32[32,8,512]{2,1,0:T(8,128)S(1)} %bitcast.10, bf16[512,512]{1,0:T(8,128)(2,1)S(1)} %copy-done.6, bf16[512,512]{1,0:T(8,128)(2,1)S(1)} %copy-done.7, f32[8,8,512]{2,1,0:T(8,128)S(1)} %collective-permute-done.refs_0_, bf16[4,32,8,512]{3,2,1,0:T(8,128)(2,1)S(1)} %bitcast.15, ...), custom_call_target="tpu_custom_call" | custom-call | flops 1000000000 | bytes 2097152 | tf_op jit(solution)/shard_map/pallas_call | solution.py:313
  9.2 2.6 %collective-permute-start.5 = (f32[128,128]{1,0:T(8,128)S(1)}, f32[128,128]{1,0:T(8,128)S(1)}, u32[]{:S(2)}, u32[]{:S(2)}) collective-permute-start(f32[128,128]{1,0:T(8,128)S(1)} %get-tuple-element.39), channel_id=1, source_target_pairs={{0,2},{2,0},{4,6},{6,4},{8,10},{10,8},{12,14},{14,12},{16,18},{18,... | collective-permute-start | bytes 196616 | tf_op jit(solution)/shard_map/ppermute | solution.py:351
  11.8 2.5 %shard_map.97 = f32[128,128]{1,0:T(8,128)S(1)} custom-call(f32[32,8,512]{2,1,0:T(8,128)S(1)} %get-tuple-element.30.own_ref, bf16[512,512]{1,0:T(8,128)(2,1)S(1)} %copy-done.6, bf16[512,512]{1,0:T(8,128)(2,1)S(1)} %copy-done.7, bf16[4,32,8,512]{3,2,1,0:T(8,128)(2,1)S(1)} %bitcast.16, s32[128,128]{1,0:T(8,128)S(1)} %get-tuple-element.31.refs_1_, ...), custom_call_target="tpu_custom_call" | custom-call | flops 1000000000 | bytes 2097152 | tf_op jit(solution)/shard_map/pallas_call | solution.py:313
  14.3 1.6 %collective-permute-start.1 = (f32[128,128]{1,0:T(8,128)S(1)}, f32[128,128]{1,0:T(8,128)S(1)}, u32[]{:S(2)}, u32[]{:S(2)}) collective-permute-start(f32[128,128]{1,0:T(8,128)S(1)} %shard_map.97), channel_id=1, source_target_pairs={{0,8},{2,10},{4,12},{6,14},{8,0},{10,2},{12,4},{14,6},{16,24},{18,... | collective-permute-start | bytes 196616 | tf_op jit(solution)/shard_map/ppermute | solution.py:351
  16.0 1.6 %collective-permute-start.6 = (f32[128,128]{1,0:T(8,128)S(1)}, f32[128,128]{1,0:T(8,128)S(1)}, u32[]{:S(2)}, u32[]{:S(2)}) collective-permute-start(f32[128,128]{1,0:T(8,128)S(1)} %add.33), channel_id=1, source_target_pairs={{0,4},{2,6},{4,0},{6,2},{8,12},{10,14},{12,8},{14,10},{16,20},{18,... | collective-permute-start | bytes 196616 | tf_op jit(solution)/shard_map/ppermute | solution.py:351
  17.5 1.1 %collective-permute-done.1 = f32[128,128]{1,0:T(8,128)S(1)} collective-permute-done((f32[128,128]{1,0:T(8,128)S(1)}, f32[128,128]{1,0:T(8,128)S(1)}, u32[]{:S(2)}, u32[]{:S(2)}) %collective-permute-start.1) | collective-permute-done | bytes 65568 | tf_op jit(solution)/shard_map/ppermute | solution.py:351
  18.7 2.7 %collective-permute-start.2 = (f32[128,128]{1,0:T(8,128)S(1)}, f32[128,128]{1,0:T(8,128)S(1)}, u32[]{:S(2)}, u32[]{:S(2)}) collective-permute-start(f32[128,128]{1,0:T(8,128)S(1)} %add.29), channel_id=1, source_target_pairs={{0,16},{2,18},{4,20},{6,22},{8,24},{10,26},{12,28},{14,30},{16,0},... | collective-permute-start | bytes 196616 | tf_op jit(solution)/shard_map/ppermute | solution.py:351
  21.3 1.6 %collective-permute-start.7 = (f32[128,128]{1,0:T(8,128)S(1)}, f32[128,128]{1,0:T(8,128)S(1)}, u32[]{:S(2)}, u32[]{:S(2)}) collective-permute-start(f32[128,128]{1,0:T(8,128)S(1)} %add.34), channel_id=1, source_target_pairs={{0,8},{2,10},{4,12},{6,14},{8,0},{10,2},{12,4},{14,6},{16,24},{18,... | collective-permute-start | bytes 196616 | tf_op jit(solution)/shard_map/ppermute | solution.py:351
  23.0 2.3 %shard_map.98 = (f32[128,128]{1,0:T(8,128)S(1)}, f32[128,128]{1,0:T(8,128)S(1)}) custom-call(s32[4,8192]{1,0:T(4,128)S(1)} %get-tuple-element.34.pos_ref, f32[4,8192]{1,0:T(4,128)S(1)} %copy-done.3, f32[4,8192]{1,0:T(4,128)S(1)} %copy-done.4, s32[4,8192]{1,0:T(4,128)S(1)} %copy-done.5), custom_call_target="tpu_custom_call" | custom-call | flops 1000000000 | bytes 2097152 | tf_op jit(solution)/shard_map/pallas_call | solution.py:313
  25.3 0.0 collective-permute-done.2
  25.3 0.6 %collective-permute-start.3 = (f32[128,128]{1,0:T(8,128)S(1)}, f32[128,128]{1,0:T(8,128)S(1)}, u32[]{:S(2)}, u32[]{:S(2)}) collective-permute-start(f32[128,128]{1,0:T(8,128)S(1)} %add.30), channel_id=1, source_target_pairs={{0,2},{2,0},{4,6},{6,4},{8,10},{10,8},{12,14},{14,12},{16,18},{18,... | collective-permute-start | bytes 196616 | tf_op jit(solution)/shard_map/ppermute | solution.py:351
  26.0 1.5 %collective-permute-start.8 = (f32[128,128]{1,0:T(8,128)S(1)}, f32[128,128]{1,0:T(8,128)S(1)}, u32[]{:S(2)}, u32[]{:S(2)}) collective-permute-start(f32[128,128]{1,0:T(8,128)S(1)} %add.35), channel_id=1, source_target_pairs={{0,16},{2,18},{4,20},{6,22},{8,24},{10,26},{12,28},{14,30},{16,0},... | collective-permute-start | bytes 196616 | tf_op jit(solution)/shard_map/ppermute | solution.py:351
  27.4 2.3 %shard_map.99 = (f32[128,128]{1,0:T(8,128)S(1)}, f32[128,128]{1,0:T(8,128)S(1)}) custom-call(s32[4,8192]{1,0:T(4,128)S(1)} %get-tuple-element.34.pos_ref, f32[4,8192]{1,0:T(4,128)S(1)} %copy-done.3, f32[4,8192]{1,0:T(4,128)S(1)} %copy-done.4, s32[4,8192]{1,0:T(4,128)S(1)} %copy-done.5), custom_call_target="tpu_custom_call" | custom-call | flops 1000000000 | bytes 2097152 | tf_op jit(solution)/shard_map/pallas_call | solution.py:313
  29.8 1.6 %collective-permute-start.4 = (f32[128,128]{1,0:T(8,128)S(1)}, f32[128,128]{1,0:T(8,128)S(1)}, u32[]{:S(2)}, u32[]{:S(2)}) collective-permute-start(f32[128,128]{1,0:T(8,128)S(1)} %add.31), channel_id=1, source_target_pairs={{0,4},{2,6},{4,0},{6,2},{8,12},{10,14},{12,8},{14,10},{16,20},{18,... | collective-permute-start | bytes 196616 | tf_op jit(solution)/shard_map/ppermute | solution.py:351
  31.4 3.3 %shard_map.100 = (f32[32,8,512]{2,1,0:T(8,128)S(1)}, f32[8,128]{1,0:T(8,128)S(1)}) custom-call(f32[128,128]{1,0:T(8,128)S(1)} %add.36.seen_ref, f32[128,128]{1,0:T(8,128)S(1)} %get-tuple-element.40.want_ref, f32[128,128]{1,0:T(8,128)S(1)} %get-tuple-element.41.keep_ref, s32[128,128]{1,0:T(8,128)S(1)} %get-tuple-element.42.place_ref, ...), custom_call_target="tpu_custom_call" | custom-call | flops 1000000000 | bytes 2097152 | tf_op jit(solution)/shard_map/pallas_call | solution.py:313
  34.7 3.3 %shard_map.101 = (f32[32,8,512]{2,1,0:T(8,128)S(1)}, f32[8,128]{1,0:T(8,128)S(1)}) custom-call(f32[128,128]{1,0:T(8,128)S(1)} %add.32.seen_ref, f32[128,128]{1,0:T(8,128)S(1)} %get-tuple-element.35.want_ref, f32[128,128]{1,0:T(8,128)S(1)} %get-tuple-element.36.keep_ref, s32[128,128]{1,0:T(8,128)S(1)} %get-tuple-element.37.place_ref, ...), custom_call_target="tpu_custom_call" | custom-call | flops 1000000000 | bytes 2097152 | tf_op jit(solution)/shard_map/pallas_call | solution.py:313
  38.1 0.1 collective-permute-start.9
  38.1 1.3 %collective-permute-done.9.refs_0_ = f32[8,8,512]{2,1,0:T(8,128)S(1)} collective-permute-done((f32[8,8,512]{2,1,0:T(8,128)S(1)}, f32[8,8,512]{2,1,0:T(8,128)S(1)}, u32[]{:S(2)}, u32[]{:S(2)}) %collective-permute-start.9) | collective-permute-done | bytes 131104 | tf_op jit(solution)/shard_map/ppermute | solution.py:330
  39.5 1.1 %shard_map.102 = (f32[32,8,512]{2,1,0:T(8,128)S(1)}, f32[32,128]{1,0:T(8,128)S(1)}) custom-call(f32[8,8,512]{2,1,0:T(8,128)S(1)} %collective-permute-done.9.refs_0_, f32[32,8,512]{2,1,0:T(8,128)S(1)} %get-tuple-element.46.refs_1_, bf16[512,512]{1,0:T(8,128)(2,1)S(1)} %copy-done.6, bf16[512,512]{1,0:T(8,128)(2,1)S(1)} %copy-done.7, ...), custom_call_target="tpu_custom_call" | custom-call | flops 1000000000 | bytes 2097152 | tf_op jit(solution)/shard_map/pallas_call | solution.py:313
  40.6 12.0 %all_to_all.11 = f32[32,1,128]{2,1,0:T(1,128)S(1)} all-to-all(f32[32,1,128]{2,1,0:T(1,128)S(1)} %bitcast.14), channel_id=1, replica_groups=mesh['mem'=16,'lat'=2] {'mem','lat'}, dimensions={0} | all-to-all | bytes 32768 | tf_op jit(solution)/shard_map/all_to_all | solution.py:427
  52.6 1.0 %shard_map.103 = (f32[32,8,512]{2,1,0:T(8,128)}, f32[1,1]{1,0:T(1,128)}) custom-call(f32[32,128]{1,0:T(8,128)S(1)} %bitcast.13, f32[32,8,512]{2,1,0:T(8,128)S(1)} %bitcast.12, f32[32,8,512]{2,1,0:T(8,128)S(1)} %get-tuple-element.49.grad_ref), custom_call_target="tpu_custom_call" | custom-call | flops 100000000 | bytes 2097152 | tf_op jit(solution)/shard_map/pallas_call | solution.py:313
  (32 shorter events, 0.2 us)
Async XLA Ops:
  0.6 1.5 %copy-start.2 = (s32[4,8192]{1,0:T(4,128)S(1)}, s32[4,8192]{1,0:T(4,128)}, u32[]{:S(2)}) copy-start(s32[4,8192]{1,0:T(4,128)} %cell_ref.1) | copy-start | bytes 393220
  1.6 4.8 %copy-start = (f32[1,32,8,512]{3,2,1,0:T(8,128)S(1)}, f32[1,32,8,512]{3,2,1,0:T(8,128)}, u32[]{:S(2)}) copy-start(f32[1,32,8,512]{3,2,1,0:T(8,128)} %param.9) | copy-start | bytes 1572868
  1.6 4.9 %copy-start.1 = (bf16[1,4,32,8,512]{4,3,2,1,0:T(8,128)(2,1)S(1)}, bf16[1,4,32,8,512]{4,3,2,1,0:T(8,128)(2,1)}, u32[]{:S(2)}) copy-start(bf16[1,4,32,8,512]{4,3,2,1,0:T(8,128)(2,1)} %param.8) | copy-start | bytes 3145732
  1.6 4.9 %copy-start.6 = (bf16[512,512]{1,0:T(8,128)(2,1)S(1)}, bf16[512,512]{1,0:T(8,128)(2,1)}, u32[]{:S(2)}) copy-start(bf16[512,512]{1,0:T(8,128)(2,1)} %constant.17.clone.circ_high_ref.refs_2_) | copy-start | bytes 1572868
  1.6 4.8 %copy-start.7 = (bf16[512,512]{1,0:T(8,128)(2,1)S(1)}, bf16[512,512]{1,0:T(8,128)(2,1)}, u32[]{:S(2)}) copy-start(bf16[512,512]{1,0:T(8,128)(2,1)} %constant.18.clone.circ_low_ref.refs_3_) | copy-start | bytes 1572868
  1.7 4.8 %collective-permute-start = (f32[8,8,512]{2,1,0:T(8,128)S(1)}, f32[8,8,512]{2,1,0:T(8,128)S(1)}, u32[]{:S(2)}, u32[]{:S(2)}) collective-permute-start(f32[8,8,512]{2,1,0:T(8,128)S(1)} %dynamic-slice_bitcast_fusion), channel_id=1, source_target_pairs={{0,1},{1,0},{2,3},{3,2},{4,5},{5,4},{6,7},{7,6},{8,9},{9,8},{10,11... | collective-permute-start | bytes 393224 | tf_op jit(solution)/shard_map/ppermute | solution.py:330
  9.2 6.7 %collective-permute-start.5 = (f32[128,128]{1,0:T(8,128)S(1)}, f32[128,128]{1,0:T(8,128)S(1)}, u32[]{:S(2)}, u32[]{:S(2)}) collective-permute-start(f32[128,128]{1,0:T(8,128)S(1)} %get-tuple-element.39), channel_id=1, source_target_pairs={{0,2},{2,0},{4,6},{6,4},{8,10},{10,8},{12,14},{14,12},{16,18},{18,... | collective-permute-start | bytes 196616 | tf_op jit(solution)/shard_map/ppermute | solution.py:351
  14.3 4.3 %collective-permute-start.1 = (f32[128,128]{1,0:T(8,128)S(1)}, f32[128,128]{1,0:T(8,128)S(1)}, u32[]{:S(2)}, u32[]{:S(2)}) collective-permute-start(f32[128,128]{1,0:T(8,128)S(1)} %shard_map.97), channel_id=1, source_target_pairs={{0,8},{2,10},{4,12},{6,14},{8,0},{10,2},{12,4},{14,6},{16,24},{18,... | collective-permute-start | bytes 196616 | tf_op jit(solution)/shard_map/ppermute | solution.py:351
  16.0 5.4 %collective-permute-start.6 = (f32[128,128]{1,0:T(8,128)S(1)}, f32[128,128]{1,0:T(8,128)S(1)}, u32[]{:S(2)}, u32[]{:S(2)}) collective-permute-start(f32[128,128]{1,0:T(8,128)S(1)} %add.33), channel_id=1, source_target_pairs={{0,4},{2,6},{4,0},{6,2},{8,12},{10,14},{12,8},{14,10},{16,20},{18,... | collective-permute-start | bytes 196616 | tf_op jit(solution)/shard_map/ppermute | solution.py:351
  18.6 4.3 %copy-start.4 = (f32[4,8192]{1,0:T(4,128)S(1)}, f32[4,8192]{1,0:T(4,128)}, u32[]{:S(2)}) copy-start(f32[4,8192]{1,0:T(4,128)} %weight_ref.3) | copy-start | bytes 393220
  18.6 4.3 %copy-start.5 = (s32[4,8192]{1,0:T(4,128)S(1)}, s32[4,8192]{1,0:T(4,128)}, u32[]{:S(2)}) copy-start(s32[4,8192]{1,0:T(4,128)} %quality_ref.3) | copy-start | bytes 393220
  18.7 4.3 %copy-start.3 = (f32[4,8192]{1,0:T(4,128)S(1)}, f32[4,8192]{1,0:T(4,128)}, u32[]{:S(2)}) copy-start(f32[4,8192]{1,0:T(4,128)} %innov_ref.3) | copy-start | bytes 393220
  18.7 6.6 %collective-permute-start.2 = (f32[128,128]{1,0:T(8,128)S(1)}, f32[128,128]{1,0:T(8,128)S(1)}, u32[]{:S(2)}, u32[]{:S(2)}) collective-permute-start(f32[128,128]{1,0:T(8,128)S(1)} %add.29), channel_id=1, source_target_pairs={{0,16},{2,18},{4,20},{6,22},{8,24},{10,26},{12,28},{14,30},{16,0},... | collective-permute-start | bytes 196616 | tf_op jit(solution)/shard_map/ppermute | solution.py:351
  21.3 4.6 %collective-permute-start.7 = (f32[128,128]{1,0:T(8,128)S(1)}, f32[128,128]{1,0:T(8,128)S(1)}, u32[]{:S(2)}, u32[]{:S(2)}) collective-permute-start(f32[128,128]{1,0:T(8,128)S(1)} %add.34), channel_id=1, source_target_pairs={{0,8},{2,10},{4,12},{6,14},{8,0},{10,2},{12,4},{14,6},{16,24},{18,... | collective-permute-start | bytes 196616 | tf_op jit(solution)/shard_map/ppermute | solution.py:351
  25.3 4.4 %collective-permute-start.3 = (f32[128,128]{1,0:T(8,128)S(1)}, f32[128,128]{1,0:T(8,128)S(1)}, u32[]{:S(2)}, u32[]{:S(2)}) collective-permute-start(f32[128,128]{1,0:T(8,128)S(1)} %add.30), channel_id=1, source_target_pairs={{0,2},{2,0},{4,6},{6,4},{8,10},{10,8},{12,14},{14,12},{16,18},{18,... | collective-permute-start | bytes 196616 | tf_op jit(solution)/shard_map/ppermute | solution.py:351
  26.0 5.4 %collective-permute-start.8 = (f32[128,128]{1,0:T(8,128)S(1)}, f32[128,128]{1,0:T(8,128)S(1)}, u32[]{:S(2)}, u32[]{:S(2)}) collective-permute-start(f32[128,128]{1,0:T(8,128)S(1)} %add.35), channel_id=1, source_target_pairs={{0,16},{2,18},{4,20},{6,22},{8,24},{10,26},{12,28},{14,30},{16,0},... | collective-permute-start | bytes 196616 | tf_op jit(solution)/shard_map/ppermute | solution.py:351
  29.8 4.9 %collective-permute-start.4 = (f32[128,128]{1,0:T(8,128)S(1)}, f32[128,128]{1,0:T(8,128)S(1)}, u32[]{:S(2)}, u32[]{:S(2)}) collective-permute-start(f32[128,128]{1,0:T(8,128)S(1)} %add.31), channel_id=1, source_target_pairs={{0,4},{2,6},{4,0},{6,2},{8,12},{10,14},{12,8},{14,10},{16,20},{18,... | collective-permute-start | bytes 196616 | tf_op jit(solution)/shard_map/ppermute | solution.py:351
  38.1 1.4 %collective-permute-start.9 = (f32[8,8,512]{2,1,0:T(8,128)S(1)}, f32[8,8,512]{2,1,0:T(8,128)S(1)}, u32[]{:S(2)}, u32[]{:S(2)}) collective-permute-start(f32[8,8,512]{2,1,0:T(8,128)S(1)} %constant_dynamic-slice_fusion), channel_id=1, source_target_pairs={{0,1},{1,0},{2,3},{3,2},{4,5},{5,4},{6,7},{7,6},{8,9},{9,8},{10,11... | collective-permute-start | bytes 393224 | tf_op jit(solution)/shard_map/ppermute | solution.py:330

commit v7 on v6

--- a/solution.py
+++ b/solution.py
@@ -19,8 +19,6 @@
 GROUP = 1024
 BIN = 2
 WINDOW = 2 * BIN
-PICK_UNROLL = 16
-SCATTER_UNROLL = 16
 GROUPS = 2
 COST = 10**9
 MIB = 1024 * 1024
@@ -183,22 +181,23 @@
     return jnp.where(place < (low_row - start) * per_row, -1, place)
 
 
-def over_windows(tiles, slots, rows, bounds_ref, unroll, step):
+def over_windows(tiles, slots, rows, bounds_ref, scalar_ref, sem, step):
     parts = LANES // PIECE
-
-    @pl.loop(0, tiles, unroll=unroll)
-    def _(tile):
+    bounds = bounds_ref[...]
+    for tile in range(tiles):
         for slot in range(slots):
-            step(slot, tile, bounds_ref[slot, tile * parts], None)
+            step(slot, tile, bounds[slot, tile * parts], None)
 
     for slot in range(slots):
 
-        @pl.when(bounds_ref[2 * slots + slot, 0] >= WINDOW)
+        @pl.when(bounds[2 * slots + slot, 0] >= WINDOW)
         def _():
+            pltpu.async_copy(bounds_ref, scalar_ref, sem).wait()
+
             @pl.loop(0, tiles)
             def _(tile):
-                begin = bounds_ref[slot, tile * parts]
-                end = bounds_ref[slots + slot, (tile + 1) * parts - 1]
+                begin = scalar_ref[slot, tile * parts]
+                end = scalar_ref[slots + slot, (tile + 1) * parts - 1]
 
                 @pl.loop(1, lax.div(end - begin, WINDOW) + 1)
                 def _(turn):
@@ -210,9 +209,7 @@
     if sides:
         low, high = halo(refs[:sides])
         refs = refs[sides:]
-    ens_ref, place_ref, lane_ref, bounds_in_ref, out_ref, *part_refs, bounds_ref, sem = refs
-    bounds_copy = pltpu.make_async_copy(bounds_in_ref, bounds_ref, sem)
-    bounds_copy.start()
+    ens_ref, place_ref, lane_ref, bounds_ref, out_ref, *part_refs, scalar_ref, sem = refs
     rows, levels, lons = own_ref.shape
     slots = len(group)
     tiles = place_ref.shape[0] * PIECE // (slots * LANES)
@@ -243,15 +240,12 @@
             here, part = pl.ds(at * (LANES // PIECE) + k, 1), value[:, k * PIECE : (k + 1) * PIECE]
             out_ref[here, :] = part if low_row is None else out_ref[here, :] + part
 
-    bounds_copy.wait()
-    over_windows(tiles, slots, rows, bounds_ref, PICK_UNROLL, step)
+    over_windows(tiles, slots, rows, bounds_ref, scalar_ref, sem, step)
 
 
 def scatter_kernel(group, norm_scale, earlier, seen_ref, want_ref, keep_ref, place_ref, lane_ref, ens_ref, *refs):
     before_refs, refs = refs[:earlier], refs[earlier:]
-    bounds_in_ref, back_ref, cost_ref, wres_ref, *grad_refs, bounds_ref, sem = refs
-    bounds_copy = pltpu.make_async_copy(bounds_in_ref, bounds_ref, sem)
-    bounds_copy.start()
+    bounds_ref, back_ref, cost_ref, wres_ref, *grad_refs, scalar_ref, sem = refs
     slots = len(group)
     _, rows, levels, lons = ens_ref.shape
     tiles = place_ref.shape[0] * PIECE // (slots * LANES)
@@ -276,8 +270,7 @@
         both = across(left, hot)
         grad_refs[slot][pl.ds(start, WINDOW)] += (both[:size] + both[size:]).reshape(WINDOW, parts, levels, SCATTER_LONS)
 
-    bounds_copy.wait()
-    over_windows(tiles, slots, rows, bounds_ref, SCATTER_UNROLL, step)
+    over_windows(tiles, slots, rows, bounds_ref, scalar_ref, sem, step)
     total = jnp.zeros((rows, levels, lons), jnp.float32)
     for slot in range(slots):
         grad = jnp.concatenate([grad_refs[slot][:, k] for k in range(parts)], axis=2)

time: 53.7 us -> 52.8 us (0.983)
  Pallas kernels: 22.7 us -> 21.8 us
    pallas_call x9, Pallas kernels: 22.7 us -> 21.8 us  [call(): pl.pallas_call(body, out_shape=out_shape, in_specs=[vmem] * len(operands)...]
where the time goes in v7:
time: 52.8 us; the launch traced here: 52.6 us
  Pallas kernels  21.8 us (41%)
  starting transfers between devices  14.5 us (27%)
  blocking collectives  11.9 us (23%)
  waiting for transfers between devices  2.47 us (5%)
  local copies, waits for them, and re-layouts  1.03 us (2%)
  between operations  0.87 us (2%)
    pallas_call x9, Pallas kernels, call(): pl.pallas_call(body, out_shape=out_shape, in_specs=[vmem] * len(operands)...  21.8 us
    ppermute x8, starting transfers between devices, summed(): lax.ppermute(value, axis, [(i, i ^ away) for i in range(count)])  13.9 us
    all_to_all x1, blocking collectives, local(): sums = lax.all_to_all(sums, ('mem', 'lat'), 0, 0, tiled=True)  11.9 us
    ppermute x2, waiting for transfers between devices, edges(): return [lax.ppermute(edge, 'lat', [(0, 1), (1, 0)])]  1.34 us
    ppermute x8, waiting for transfers between devices, summed(): lax.ppermute(value, axis, [(i, i ^ away) for i in range(count)])  1.13 us
  transfers between devices with their start and end apart: 10, of which 2 were waited for; matrix products, arithmetic and copies ran while one was open for 0% of the time, Pallas kernels for 27%

profile of v7, /device:TPU:0, one launch (start us, length us, event | category | flops | bytes accessed | tf_op | source)
XLA Modules:
  0.0 52.6 jit_solution(1552139399707415303)
XLA Ops:
  0.6 1.0 %dynamic-slice_bitcast_fusion = f32[8,8,512]{2,1,0:T(8,128)S(1)} fusion(f32[1,32,8,512]{3,2,1,0:T(8,128)} %param.9, s32[]{:T(128)S(6)} %select_n.4), kind=kLoop, calls=%fused_computation | loop fusion | bytes 262148 | tf_op jit(solution)/shard_map/dynamic_slice | solution.py:322
  1.7 0.5 collective-permute-start
  2.2 4.3 %shard_map.95 = (s32[4,8192]{1,0:T(4,128)S(1)}, s32[128,128]{1,0:T(8,128)S(1)}, f32[128,128]{1,0:T(8,128)S(1)}, s32[128,128]{1,0:T(8,128)S(1)}, f32[128,128]{1,0...) custom-call(s32[4,8192]{1,0:T(4,128)S(1)} %copy-done.2), custom_call_target="tpu_custom_call" | custom-call | flops 1000000000 | bytes 2097152 | tf_op jit(solution)/shard_map/pallas_call | solution.py:306
  6.5 2.7 %shard_map.96 = (f32[128,128]{1,0:T(8,128)S(1)}, f32[32,8,512]{2,1,0:T(8,128)S(1)}) custom-call(f32[32,8,512]{2,1,0:T(8,128)S(1)} %bitcast.10, bf16[512,512]{1,0:T(8,128)(2,1)S(1)} %copy-done.6, bf16[512,512]{1,0:T(8,128)(2,1)S(1)} %copy-done.7, f32[8,8,512]{2,1,0:T(8,128)S(1)} %collective-permute-done.refs_0_, bf16[4,32,8,512]{3,2,1,0:T(8,128)(2,1)S(1)} %bitcast.15, ...), custom_call_target="tpu_custom_call" | custom-call | flops 1000000000 | bytes 2097152 | tf_op jit(solution)/shard_map/pallas_call | solution.py:306
  9.2 2.6 %collective-permute-start.5 = (f32[128,128]{1,0:T(8,128)S(1)}, f32[128,128]{1,0:T(8,128)S(1)}, u32[]{:S(2)}, u32[]{:S(2)}) collective-permute-start(f32[128,128]{1,0:T(8,128)S(1)} %get-tuple-element.39), channel_id=1, source_target_pairs={{0,2},{2,0},{4,6},{6,4},{8,10},{10,8},{12,14},{14,12},{16,18},{18,... | collective-permute-start | bytes 196616 | tf_op jit(solution)/shard_map/ppermute | solution.py:344
  11.8 2.3 %shard_map.97 = f32[128,128]{1,0:T(8,128)S(1)} custom-call(f32[32,8,512]{2,1,0:T(8,128)S(1)} %get-tuple-element.30.own_ref, bf16[512,512]{1,0:T(8,128)(2,1)S(1)} %copy-done.6, bf16[512,512]{1,0:T(8,128)(2,1)S(1)} %copy-done.7, bf16[4,32,8,512]{3,2,1,0:T(8,128)(2,1)S(1)} %bitcast.16, s32[128,128]{1,0:T(8,128)S(1)} %get-tuple-element.31.refs_1_, ...), custom_call_target="tpu_custom_call" | custom-call | flops 1000000000 | bytes 2097152 | tf_op jit(solution)/shard_map/pallas_call | solution.py:306
  14.1 1.6 %collective-permute-start.1 = (f32[128,128]{1,0:T(8,128)S(1)}, f32[128,128]{1,0:T(8,128)S(1)}, u32[]{:S(2)}, u32[]{:S(2)}) collective-permute-start(f32[128,128]{1,0:T(8,128)S(1)} %shard_map.97), channel_id=1, source_target_pairs={{0,8},{2,10},{4,12},{6,14},{8,0},{10,2},{12,4},{14,6},{16,24},{18,... | collective-permute-start | bytes 196616 | tf_op jit(solution)/shard_map/ppermute | solution.py:344
  15.7 1.6 %collective-permute-start.6 = (f32[128,128]{1,0:T(8,128)S(1)}, f32[128,128]{1,0:T(8,128)S(1)}, u32[]{:S(2)}, u32[]{:S(2)}) collective-permute-start(f32[128,128]{1,0:T(8,128)S(1)} %add.33), channel_id=1, source_target_pairs={{0,4},{2,6},{4,0},{6,2},{8,12},{10,14},{12,8},{14,10},{16,20},{18,... | collective-permute-start | bytes 196616 | tf_op jit(solution)/shard_map/ppermute | solution.py:344
  17.3 1.1 %collective-permute-done.1 = f32[128,128]{1,0:T(8,128)S(1)} collective-permute-done((f32[128,128]{1,0:T(8,128)S(1)}, f32[128,128]{1,0:T(8,128)S(1)}, u32[]{:S(2)}, u32[]{:S(2)}) %collective-permute-start.1) | collective-permute-done | bytes 65568 | tf_op jit(solution)/shard_map/ppermute | solution.py:344
  18.4 2.7 %collective-permute-start.2 = (f32[128,128]{1,0:T(8,128)S(1)}, f32[128,128]{1,0:T(8,128)S(1)}, u32[]{:S(2)}, u32[]{:S(2)}) collective-permute-start(f32[128,128]{1,0:T(8,128)S(1)} %add.29), channel_id=1, source_target_pairs={{0,16},{2,18},{4,20},{6,22},{8,24},{10,26},{12,28},{14,30},{16,0},... | collective-permute-start | bytes 196616 | tf_op jit(solution)/shard_map/ppermute | solution.py:344
  21.1 1.6 %collective-permute-start.7 = (f32[128,128]{1,0:T(8,128)S(1)}, f32[128,128]{1,0:T(8,128)S(1)}, u32[]{:S(2)}, u32[]{:S(2)}) collective-permute-start(f32[128,128]{1,0:T(8,128)S(1)} %add.34), channel_id=1, source_target_pairs={{0,8},{2,10},{4,12},{6,14},{8,0},{10,2},{12,4},{14,6},{16,24},{18,... | collective-permute-start | bytes 196616 | tf_op jit(solution)/shard_map/ppermute | solution.py:344
  22.8 2.3 %shard_map.98 = (f32[128,128]{1,0:T(8,128)S(1)}, f32[128,128]{1,0:T(8,128)S(1)}) custom-call(s32[4,8192]{1,0:T(4,128)S(1)} %get-tuple-element.34.pos_ref, f32[4,8192]{1,0:T(4,128)S(1)} %copy-done.3, f32[4,8192]{1,0:T(4,128)S(1)} %copy-done.4, s32[4,8192]{1,0:T(4,128)S(1)} %copy-done.5), custom_call_target="tpu_custom_call" | custom-call | flops 1000000000 | bytes 2097152 | tf_op jit(solution)/shard_map/pallas_call | solution.py:306
  25.1 0.6 %collective-permute-start.3 = (f32[128,128]{1,0:T(8,128)S(1)}, f32[128,128]{1,0:T(8,128)S(1)}, u32[]{:S(2)}, u32[]{:S(2)}) collective-permute-start(f32[128,128]{1,0:T(8,128)S(1)} %add.30), channel_id=1, source_target_pairs={{0,2},{2,0},{4,6},{6,4},{8,10},{10,8},{12,14},{14,12},{16,18},{18,... | collective-permute-start | bytes 196616 | tf_op jit(solution)/shard_map/ppermute | solution.py:344
  25.7 1.6 %collective-permute-start.8 = (f32[128,128]{1,0:T(8,128)S(1)}, f32[128,128]{1,0:T(8,128)S(1)}, u32[]{:S(2)}, u32[]{:S(2)}) collective-permute-start(f32[128,128]{1,0:T(8,128)S(1)} %add.35), channel_id=1, source_target_pairs={{0,16},{2,18},{4,20},{6,22},{8,24},{10,26},{12,28},{14,30},{16,0},... | collective-permute-start | bytes 196616 | tf_op jit(solution)/shard_map/ppermute | solution.py:344
  27.4 2.3 %shard_map.99 = (f32[128,128]{1,0:T(8,128)S(1)}, f32[128,128]{1,0:T(8,128)S(1)}) custom-call(s32[4,8192]{1,0:T(4,128)S(1)} %get-tuple-element.34.pos_ref, f32[4,8192]{1,0:T(4,128)S(1)} %copy-done.3, f32[4,8192]{1,0:T(4,128)S(1)} %copy-done.4, s32[4,8192]{1,0:T(4,128)S(1)} %copy-done.5), custom_call_target="tpu_custom_call" | custom-call | flops 1000000000 | bytes 2097152 | tf_op jit(solution)/shard_map/pallas_call | solution.py:306
  29.7 0.0 collective-permute-done.3
  29.7 1.6 %collective-permute-start.4 = (f32[128,128]{1,0:T(8,128)S(1)}, f32[128,128]{1,0:T(8,128)S(1)}, u32[]{:S(2)}, u32[]{:S(2)}) collective-permute-start(f32[128,128]{1,0:T(8,128)S(1)} %add.31), channel_id=1, source_target_pairs={{0,4},{2,6},{4,0},{6,2},{8,12},{10,14},{12,8},{14,10},{16,20},{18,... | collective-permute-start | bytes 196616 | tf_op jit(solution)/shard_map/ppermute | solution.py:344
  31.3 2.9 %shard_map.100 = (f32[32,8,512]{2,1,0:T(8,128)S(1)}, f32[8,128]{1,0:T(8,128)S(1)}) custom-call(f32[128,128]{1,0:T(8,128)S(1)} %add.36.seen_ref, f32[128,128]{1,0:T(8,128)S(1)} %get-tuple-element.40.want_ref, f32[128,128]{1,0:T(8,128)S(1)} %get-tuple-element.41.keep_ref, s32[128,128]{1,0:T(8,128)S(1)} %get-tuple-element.42.place_ref, ...), custom_call_target="tpu_custom_call" | custom-call | flops 1000000000 | bytes 2097152 | tf_op jit(solution)/shard_map/pallas_call | solution.py:306
  34.2 2.9 %shard_map.101 = (f32[32,8,512]{2,1,0:T(8,128)S(1)}, f32[8,128]{1,0:T(8,128)S(1)}) custom-call(f32[128,128]{1,0:T(8,128)S(1)} %add.32.seen_ref, f32[128,128]{1,0:T(8,128)S(1)} %get-tuple-element.35.want_ref, f32[128,128]{1,0:T(8,128)S(1)} %get-tuple-element.36.keep_ref, s32[128,128]{1,0:T(8,128)S(1)} %get-tuple-element.37.place_ref, ...), custom_call_target="tpu_custom_call" | custom-call | flops 1000000000 | bytes 2097152 | tf_op jit(solution)/shard_map/pallas_call | solution.py:306
  37.2 0.1 collective-permute-start.9
  37.3 1.3 %collective-permute-done.9.refs_0_ = f32[8,8,512]{2,1,0:T(8,128)S(1)} collective-permute-done((f32[8,8,512]{2,1,0:T(8,128)S(1)}, f32[8,8,512]{2,1,0:T(8,128)S(1)}, u32[]{:S(2)}, u32[]{:S(2)}) %collective-permute-start.9) | collective-permute-done | bytes 131104 | tf_op jit(solution)/shard_map/ppermute | solution.py:323
  38.6 1.1 %shard_map.102 = (f32[32,8,512]{2,1,0:T(8,128)S(1)}, f32[32,128]{1,0:T(8,128)S(1)}) custom-call(f32[8,8,512]{2,1,0:T(8,128)S(1)} %collective-permute-done.9.refs_0_, f32[32,8,512]{2,1,0:T(8,128)S(1)} %get-tuple-element.46.refs_1_, bf16[512,512]{1,0:T(8,128)(2,1)S(1)} %copy-done.6, bf16[512,512]{1,0:T(8,128)(2,1)S(1)} %copy-done.7, ...), custom_call_target="tpu_custom_call" | custom-call | flops 1000000000 | bytes 2097152 | tf_op jit(solution)/shard_map/pallas_call | solution.py:306
  39.7 11.9 %all_to_all.11 = f32[32,1,128]{2,1,0:T(1,128)S(1)} all-to-all(f32[32,1,128]{2,1,0:T(1,128)S(1)} %bitcast.14), channel_id=1, replica_groups=mesh['mem'=16,'lat'=2] {'mem','lat'}, dimensions={0} | all-to-all | bytes 32768 | tf_op jit(solution)/shard_map/all_to_all | solution.py:420
  51.6 1.0 %shard_map.103 = (f32[32,8,512]{2,1,0:T(8,128)}, f32[1,1]{1,0:T(1,128)}) custom-call(f32[32,128]{1,0:T(8,128)S(1)} %bitcast.13, f32[32,8,512]{2,1,0:T(8,128)S(1)} %bitcast.12, f32[32,8,512]{2,1,0:T(8,128)S(1)} %get-tuple-element.49.grad_ref), custom_call_target="tpu_custom_call" | custom-call | flops 100000000 | bytes 2097152 | tf_op jit(solution)/shard_map/pallas_call | solution.py:306
  (32 shorter events, 0.2 us)
Async XLA Ops:
  0.6 1.5 %copy-start.2 = (s32[4,8192]{1,0:T(4,128)S(1)}, s32[4,8192]{1,0:T(4,128)}, u32[]{:S(2)}) copy-start(s32[4,8192]{1,0:T(4,128)} %cell_ref.1) | copy-start | bytes 393220
  1.6 4.8 %copy-start = (f32[1,32,8,512]{3,2,1,0:T(8,128)S(1)}, f32[1,32,8,512]{3,2,1,0:T(8,128)}, u32[]{:S(2)}) copy-start(f32[1,32,8,512]{3,2,1,0:T(8,128)} %param.9) | copy-start | bytes 1572868
  1.6 4.9 %copy-start.1 = (bf16[1,4,32,8,512]{4,3,2,1,0:T(8,128)(2,1)S(1)}, bf16[1,4,32,8,512]{4,3,2,1,0:T(8,128)(2,1)}, u32[]{:S(2)}) copy-start(bf16[1,4,32,8,512]{4,3,2,1,0:T(8,128)(2,1)} %param.8) | copy-start | bytes 3145732
  1.6 4.9 %copy-start.6 = (bf16[512,512]{1,0:T(8,128)(2,1)S(1)}, bf16[512,512]{1,0:T(8,128)(2,1)}, u32[]{:S(2)}) copy-start(bf16[512,512]{1,0:T(8,128)(2,1)} %constant.17.clone.circ_high_ref.refs_2_) | copy-start | bytes 1572868
  1.6 4.8 %copy-start.7 = (bf16[512,512]{1,0:T(8,128)(2,1)S(1)}, bf16[512,512]{1,0:T(8,128)(2,1)}, u32[]{:S(2)}) copy-start(bf16[512,512]{1,0:T(8,128)(2,1)} %constant.18.clone.circ_low_ref.refs_3_) | copy-start | bytes 1572868
  1.7 4.8 %collective-permute-start = (f32[8,8,512]{2,1,0:T(8,128)S(1)}, f32[8,8,512]{2,1,0:T(8,128)S(1)}, u32[]{:S(2)}, u32[]{:S(2)}) collective-permute-start(f32[8,8,512]{2,1,0:T(8,128)S(1)} %dynamic-slice_bitcast_fusion), channel_id=1, source_target_pairs={{0,1},{1,0},{2,3},{3,2},{4,5},{5,4},{6,7},{7,6},{8,9},{9,8},{10,11... | collective-permute-start | bytes 393224 | tf_op jit(solution)/shard_map/ppermute | solution.py:323
  9.2 6.5 %collective-permute-start.5 = (f32[128,128]{1,0:T(8,128)S(1)}, f32[128,128]{1,0:T(8,128)S(1)}, u32[]{:S(2)}, u32[]{:S(2)}) collective-permute-start(f32[128,128]{1,0:T(8,128)S(1)} %get-tuple-element.39), channel_id=1, source_target_pairs={{0,2},{2,0},{4,6},{6,4},{8,10},{10,8},{12,14},{14,12},{16,18},{18,... | collective-permute-start | bytes 196616 | tf_op jit(solution)/shard_map/ppermute | solution.py:344
  14.1 4.3 %collective-permute-start.1 = (f32[128,128]{1,0:T(8,128)S(1)}, f32[128,128]{1,0:T(8,128)S(1)}, u32[]{:S(2)}, u32[]{:S(2)}) collective-permute-start(f32[128,128]{1,0:T(8,128)S(1)} %shard_map.97), channel_id=1, source_target_pairs={{0,8},{2,10},{4,12},{6,14},{8,0},{10,2},{12,4},{14,6},{16,24},{18,... | collective-permute-start | bytes 196616 | tf_op jit(solution)/shard_map/ppermute | solution.py:344
  15.7 5.4 %collective-permute-start.6 = (f32[128,128]{1,0:T(8,128)S(1)}, f32[128,128]{1,0:T(8,128)S(1)}, u32[]{:S(2)}, u32[]{:S(2)}) collective-permute-start(f32[128,128]{1,0:T(8,128)S(1)} %add.33), channel_id=1, source_target_pairs={{0,4},{2,6},{4,0},{6,2},{8,12},{10,14},{12,8},{14,10},{16,20},{18,... | collective-permute-start | bytes 196616 | tf_op jit(solution)/shard_map/ppermute | solution.py:344
  18.4 4.4 %copy-start.4 = (f32[4,8192]{1,0:T(4,128)S(1)}, f32[4,8192]{1,0:T(4,128)}, u32[]{:S(2)}) copy-start(f32[4,8192]{1,0:T(4,128)} %weight_ref.3) | copy-start | bytes 393220
  18.4 4.4 %copy-start.5 = (s32[4,8192]{1,0:T(4,128)S(1)}, s32[4,8192]{1,0:T(4,128)}, u32[]{:S(2)}) copy-start(s32[4,8192]{1,0:T(4,128)} %quality_ref.3) | copy-start | bytes 393220
  18.4 4.3 %copy-start.3 = (f32[4,8192]{1,0:T(4,128)S(1)}, f32[4,8192]{1,0:T(4,128)}, u32[]{:S(2)}) copy-start(f32[4,8192]{1,0:T(4,128)} %innov_ref.3) | copy-start | bytes 393220
  18.4 6.7 %collective-permute-start.2 = (f32[128,128]{1,0:T(8,128)S(1)}, f32[128,128]{1,0:T(8,128)S(1)}, u32[]{:S(2)}, u32[]{:S(2)}) collective-permute-start(f32[128,128]{1,0:T(8,128)S(1)} %add.29), channel_id=1, source_target_pairs={{0,16},{2,18},{4,20},{6,22},{8,24},{10,26},{12,28},{14,30},{16,0},... | collective-permute-start | bytes 196616 | tf_op jit(solution)/shard_map/ppermute | solution.py:344
  21.1 4.6 %collective-permute-start.7 = (f32[128,128]{1,0:T(8,128)S(1)}, f32[128,128]{1,0:T(8,128)S(1)}, u32[]{:S(2)}, u32[]{:S(2)}) collective-permute-start(f32[128,128]{1,0:T(8,128)S(1)} %add.34), channel_id=1, source_target_pairs={{0,8},{2,10},{4,12},{6,14},{8,0},{10,2},{12,4},{14,6},{16,24},{18,... | collective-permute-start | bytes 196616 | tf_op jit(solution)/shard_map/ppermute | solution.py:344
  25.1 4.5 %collective-permute-start.3 = (f32[128,128]{1,0:T(8,128)S(1)}, f32[128,128]{1,0:T(8,128)S(1)}, u32[]{:S(2)}, u32[]{:S(2)}) collective-permute-start(f32[128,128]{1,0:T(8,128)S(1)} %add.30), channel_id=1, source_target_pairs={{0,2},{2,0},{4,6},{6,4},{8,10},{10,8},{12,14},{14,12},{16,18},{18,... | collective-permute-start | bytes 196616 | tf_op jit(solution)/shard_map/ppermute | solution.py:344
  25.7 5.5 %collective-permute-start.8 = (f32[128,128]{1,0:T(8,128)S(1)}, f32[128,128]{1,0:T(8,128)S(1)}, u32[]{:S(2)}, u32[]{:S(2)}) collective-permute-start(f32[128,128]{1,0:T(8,128)S(1)} %add.35), channel_id=1, source_target_pairs={{0,16},{2,18},{4,20},{6,22},{8,24},{10,26},{12,28},{14,30},{16,0},... | collective-permute-start | bytes 196616 | tf_op jit(solution)/shard_map/ppermute | solution.py:344
  29.7 4.5 %collective-permute-start.4 = (f32[128,128]{1,0:T(8,128)S(1)}, f32[128,128]{1,0:T(8,128)S(1)}, u32[]{:S(2)}, u32[]{:S(2)}) collective-permute-start(f32[128,128]{1,0:T(8,128)S(1)} %add.31), channel_id=1, source_target_pairs={{0,4},{2,6},{4,0},{6,2},{8,12},{10,14},{12,8},{14,10},{16,20},{18,... | collective-permute-start | bytes 196616 | tf_op jit(solution)/shard_map/ppermute | solution.py:344
  37.2 1.4 %collective-permute-start.9 = (f32[8,8,512]{2,1,0:T(8,128)S(1)}, f32[8,8,512]{2,1,0:T(8,128)S(1)}, u32[]{:S(2)}, u32[]{:S(2)}) collective-permute-start(f32[8,8,512]{2,1,0:T(8,128)S(1)} %constant_dynamic-slice_fusion), channel_id=1, source_target_pairs={{0,1},{1,0},{2,3},{3,2},{4,5},{5,4},{6,7},{7,6},{8,9},{9,8},{10,11... | collective-permute-start | bytes 393224 | tf_op jit(solution)/shard_map/ppermute | solution.py:323

commit v8 on v7

--- a/solution.py
+++ b/solution.py
@@ -17,8 +17,8 @@
 PICK_LONS = 256
 SCATTER_LONS = 128
 GROUP = 1024
-BIN = 2
-WINDOW = 2 * BIN
+BIN = 1
+WINDOW = 3
 GROUPS = 2
 COST = 10**9
 MIB = 1024 * 1024
@@ -99,16 +99,17 @@
 
 
 def sort_kernel(shape, groups, cell_ref, pos_ref, *refs):
-    *refs, prefix_ref = refs
+    slots, obs = cell_ref.shape
+    refs, prefix_refs = refs[:-slots], refs[-slots:]
     rows, levels, lons = shape
-    _, obs = cell_ref.shape
     tiles, pieces = obs // LANES, obs // PIECE
     bins = rows // BIN
     bin_ids = small_ids((bins, LANES))
     square = (LANES, LANES)
     upper = (ids_of(square, 0) <= ids_of(square, 1)).astype(jnp.bfloat16)
     counting = jnp.concatenate([upper, jnp.ones((LANES, 128), jnp.bfloat16)], axis=1)
-    before = (ids_of((bins, bins), 1) < ids_of((bins, bins), 0)).astype(jnp.float32)
+    before = (ids_of((bins, bins), 1) < ids_of((bins, bins), 0)).astype(jnp.bfloat16)
+    count = functools.partial(jnp.dot, before, preferred_element_type=jnp.float32)
     wide = lambda v: jnp.concatenate([v] * (LANES // 128), axis=1)
     _, cells = quotient(cell_ref[...], rows * levels * lons)
     keys, lons_of = quotient(cells, lons)
@@ -120,13 +121,16 @@
     for slot, (group, mine) in enumerate([(g, m) for m, g in enumerate(groups) for _ in g]):
         *place_refs, bounds_ref = refs[mine * outs : (mine + 1) * outs]
         turn = slot - group[0]
+        prefix_ref = prefix_refs[slot]
         in_bin = bins_of[slot : slot + 1]
         hots = [one_hot(bin_ids, in_bin[:, at * LANES : (at + 1) * LANES]) for at in range(tiles)]
         prefix_ref[...] = jnp.dot(jnp.concatenate(hots, axis=0), counting, preferred_element_type=jnp.float32)
         total = jnp.zeros((bins, 128), jnp.float32)
         for at in range(tiles):
             total += prefix_ref[pl.ds(at * bins, bins), pl.ds(LANES, 128)]
-        carry = jnp.dot(before, total, precision=lax.Precision.HIGHEST, preferred_element_type=jnp.float32) - 1.0
+        many = jnp.floor(total * (1.0 / LANES))
+        few = total - many * LANES
+        carry = count(many.astype(jnp.bfloat16)) * LANES + count(few.astype(jnp.bfloat16)) - 1.0
         places = []
         for at in range(tiles):
             here = pl.ds(at * bins, bins)
@@ -332,7 +336,8 @@
     if len(refs) == 2:
         return refs[0][...], refs[1][...]
     last = lax.axis_index("lat") == 1
-    return jnp.where(last, refs[0][...], 0.0), jnp.where(last, 0.0, refs[0][...])
+    rows = refs[0].shape[0]
+    return jnp.where(last, refs[0][rows - HALF :], 0.0), jnp.where(last, 0.0, refs[0][:HALF])
 
 
 def summed(value, axis, turn=0):
@@ -356,7 +361,7 @@
         ordered = (len(group) * obs // PIECE, PIECE)
         kinds += [like(ordered, jnp.int32), like(ordered)] * 2
         kinds += [like((-(-3 * len(group) // 8) * 8, -(-(obs // PIECE) // 128) * 128), jnp.int32)]
-    scratch = [pltpu.VMEM((obs // LANES * shape[0] // BIN, LANES + 128), jnp.float32)]
+    scratch = [pltpu.VMEM((obs // LANES * shape[0] // BIN, LANES + 128), jnp.float32)] * slots
     pos, *outs = call(functools.partial(sort_kernel, shape, groups), kinds, scratch, COST, obs_cell)
     outs = [outs[k : k + 5] for k in range(0, len(outs), 5)]
     return pos, [(out[:2], out[2:4], out[4]) for out in outs]
@@ -402,7 +407,7 @@
     slots = obs_cell.shape[0]
     size = slots // GROUPS
     groups = [range(k, k + size) for k in range(0, slots, size)]
-    sides = edges(own)
+    sides = [lax.ppermute(own, "lat", [(0, 1), (1, 0)])] if bands == 2 else edges(own)
     pos, ordered = sort_cells(obs_cell, own.shape, groups)
     arranged = [arrange(pos, innovation, obs_weight, quality, group) for group in groups]
     local_weights, seen = None, []

time: 52.8 us -> 51.7 us (0.979)
  Pallas kernels: 21.8 us -> 20.8 us
  blocking collectives: 11.9 us -> 11.2 us
    pallas_call x9, Pallas kernels: 21.8 us -> 20.8 us  [call(): pl.pallas_call(body, out_shape=out_shape, in_specs=[vmem] * len(operands)...]
    dynamic_slice x2 -> x1, local copies, waits for them, and re-layouts: 0.97 us -> 0.02 us  [edges(): edge = lax.dynamic_slice_in_dim(field, start, HALF, 0)]
    unnamed x16, local copies, waits for them, and re-layouts: 0.05 us -> 0.95 us
    all_to_all x1, blocking collectives: 11.9 us -> 11.2 us  [local(): sums = lax.all_to_all(sums, ('mem', 'lat'), 0, 0, tiled=True)]
    ppermute x2 -> x1, waiting for transfers between devices: 1.34 us -> 1.33 us  [edges(): return [lax.ppermute(edge, 'lat', [(0, 1), (1, 0)])]]
  transfers between devices with their start and end apart: 10 -> 10, of which waited for: 2 -> 3; matrix products, arithmetic and copies ran while one was open for 0% -> 0% of each run, Pallas kernels for 27% -> 27%
where the time goes in v8:
time: 51.7 us; the launch traced here: 51.5 us
  Pallas kernels  20.8 us (40%)
  starting transfers between devices  14.6 us (28%)
  blocking collectives  11.2 us (22%)
  waiting for transfers between devices  2.99 us (6%)
  local copies, waits for them, and re-layouts  0.96 us (2%)
  between operations  0.82 us (2%)
    pallas_call x9, Pallas kernels, call(): pl.pallas_call(body, out_shape=out_shape, in_specs=[vmem] * len(operands)...  20.8 us
    ppermute x8, starting transfers between devices, summed(): lax.ppermute(value, axis, [(i, i ^ away) for i in range(count)])  14 us
    all_to_all x1, blocking collectives, local(): sums = lax.all_to_all(sums, ('mem', 'lat'), 0, 0, tiled=True)  11.2 us
    ppermute x8, waiting for transfers between devices, summed(): lax.ppermute(value, axis, [(i, i ^ away) for i in range(count)])  1.66 us
    ppermute x1, waiting for transfers between devices, edges(): return [lax.ppermute(edge, 'lat', [(0, 1), (1, 0)])]  1.33 us
  transfers between devices with their start and end apart: 10, of which 3 were waited for; matrix products, arithmetic and copies ran while one was open for 0% of the time, Pallas kernels for 27%

profile of v8, /device:TPU:0, one launch (start us, length us, event | category | flops | bytes accessed | tf_op | source)
XLA Modules:
  0.0 51.5 jit_solution(17405171375577500445)
XLA Ops:
  0.6 0.5 %collective-permute-start = (f32[32,8,512]{2,1,0:T(8,128)}, f32[32,8,512]{2,1,0:T(8,128)S(1)}, u32[]{:S(2)}, u32[]{:S(2)}) collective-permute-start(f32[32,8,512]{2,1,0:T(8,128)} %bitcast.8), channel_id=1, source_target_pairs={{0,1},{1,0},{2,3},{3,2},{4,5},{5,4},{6,7},{7,6},{8,9},{9,8},{10,11... | collective-permute-start | bytes 1572872 | tf_op jit(solution)/shard_map/ppermute | solution.py:410
  1.2 0.9 %copy-done.2 = s32[4,8192]{1,0:T(4,128)S(1)} copy-done((s32[4,8192]{1,0:T(4,128)S(1)}, s32[4,8192]{1,0:T(4,128)}, u32[]{:S(2)}) %copy-start.2) | copy-done | bytes 131096
  2.1 4.8 %shard_map.95 = (s32[4,8192]{1,0:T(4,128)S(1)}, s32[128,128]{1,0:T(8,128)S(1)}, f32[128,128]{1,0:T(8,128)S(1)}, s32[128,128]{1,0:T(8,128)S(1)}, f32[128,128]{1,0...) custom-call(s32[4,8192]{1,0:T(4,128)S(1)} %copy-done.2), custom_call_target="tpu_custom_call" | custom-call | flops 1000000000 | bytes 2097152 | tf_op jit(solution)/shard_map/pallas_call | solution.py:310
  6.9 2.8 %shard_map.96 = (f32[128,128]{1,0:T(8,128)S(1)}, f32[32,8,512]{2,1,0:T(8,128)S(1)}) custom-call(f32[32,8,512]{2,1,0:T(8,128)S(1)} %bitcast.9, bf16[512,512]{1,0:T(8,128)(2,1)S(1)} %copy-done.6, bf16[512,512]{1,0:T(8,128)(2,1)S(1)} %copy-done.7, f32[32,8,512]{2,1,0:T(8,128)S(1)} %collective-permute-done.refs_0_, bf16[4,32,8,512]{3,2,1,0:T(8,128)(2,1)S(1)} %bitcast.14, ...), custom_call_target="tpu_custom_call" | custom-call | flops 1000000000 | bytes 2097152 | tf_op jit(solution)/shard_map/pallas_call | solution.py:310
  9.6 2.7 %collective-permute-start.5 = (f32[128,128]{1,0:T(8,128)S(1)}, f32[128,128]{1,0:T(8,128)S(1)}, u32[]{:S(2)}, u32[]{:S(2)}) collective-permute-start(f32[128,128]{1,0:T(8,128)S(1)} %get-tuple-element.39), channel_id=1, source_target_pairs={{0,2},{2,0},{4,6},{6,4},{8,10},{10,8},{12,14},{14,12},{16,18},{18,... | collective-permute-start | bytes 196616 | tf_op jit(solution)/shard_map/ppermute | solution.py:349
  12.3 2.2 %shard_map.97 = f32[128,128]{1,0:T(8,128)S(1)} custom-call(f32[32,8,512]{2,1,0:T(8,128)S(1)} %get-tuple-element.30.own_ref, bf16[512,512]{1,0:T(8,128)(2,1)S(1)} %copy-done.6, bf16[512,512]{1,0:T(8,128)(2,1)S(1)} %copy-done.7, bf16[4,32,8,512]{3,2,1,0:T(8,128)(2,1)S(1)} %bitcast.15, s32[128,128]{1,0:T(8,128)S(1)} %get-tuple-element.31.refs_1_, ...), custom_call_target="tpu_custom_call" | custom-call | flops 1000000000 | bytes 2097152 | tf_op jit(solution)/shard_map/pallas_call | solution.py:310
  14.5 1.6 %collective-permute-start.1 = (f32[128,128]{1,0:T(8,128)S(1)}, f32[128,128]{1,0:T(8,128)S(1)}, u32[]{:S(2)}, u32[]{:S(2)}) collective-permute-start(f32[128,128]{1,0:T(8,128)S(1)} %shard_map.97), channel_id=1, source_target_pairs={{0,8},{2,10},{4,12},{6,14},{8,0},{10,2},{12,4},{14,6},{16,24},{18,... | collective-permute-start | bytes 196616 | tf_op jit(solution)/shard_map/ppermute | solution.py:349
  16.2 1.6 %collective-permute-start.6 = (f32[128,128]{1,0:T(8,128)S(1)}, f32[128,128]{1,0:T(8,128)S(1)}, u32[]{:S(2)}, u32[]{:S(2)}) collective-permute-start(f32[128,128]{1,0:T(8,128)S(1)} %add.31), channel_id=1, source_target_pairs={{0,4},{2,6},{4,0},{6,2},{8,12},{10,14},{12,8},{14,10},{16,20},{18,... | collective-permute-start | bytes 196616 | tf_op jit(solution)/shard_map/ppermute | solution.py:349
  17.8 1.1 %collective-permute-done.1 = f32[128,128]{1,0:T(8,128)S(1)} collective-permute-done((f32[128,128]{1,0:T(8,128)S(1)}, f32[128,128]{1,0:T(8,128)S(1)}, u32[]{:S(2)}, u32[]{:S(2)}) %collective-permute-start.1) | collective-permute-done | bytes 65568 | tf_op jit(solution)/shard_map/ppermute | solution.py:349
  18.9 2.7 %collective-permute-start.2 = (f32[128,128]{1,0:T(8,128)S(1)}, f32[128,128]{1,0:T(8,128)S(1)}, u32[]{:S(2)}, u32[]{:S(2)}) collective-permute-start(f32[128,128]{1,0:T(8,128)S(1)} %add.27), channel_id=1, source_target_pairs={{0,16},{2,18},{4,20},{6,22},{8,24},{10,26},{12,28},{14,30},{16,0},... | collective-permute-start | bytes 196616 | tf_op jit(solution)/shard_map/ppermute | solution.py:349
  21.6 1.6 %collective-permute-start.7 = (f32[128,128]{1,0:T(8,128)S(1)}, f32[128,128]{1,0:T(8,128)S(1)}, u32[]{:S(2)}, u32[]{:S(2)}) collective-permute-start(f32[128,128]{1,0:T(8,128)S(1)} %add.32), channel_id=1, source_target_pairs={{0,8},{2,10},{4,12},{6,14},{8,0},{10,2},{12,4},{14,6},{16,24},{18,... | collective-permute-start | bytes 196616 | tf_op jit(solution)/shard_map/ppermute | solution.py:349
  23.2 2.3 %shard_map.98 = (f32[128,128]{1,0:T(8,128)S(1)}, f32[128,128]{1,0:T(8,128)S(1)}) custom-call(s32[4,8192]{1,0:T(4,128)S(1)} %get-tuple-element.34.pos_ref, f32[4,8192]{1,0:T(4,128)S(1)} %copy-done.3, f32[4,8192]{1,0:T(4,128)S(1)} %copy-done.4, s32[4,8192]{1,0:T(4,128)S(1)} %copy-done.5), custom_call_target="tpu_custom_call" | custom-call | flops 1000000000 | bytes 2097152 | tf_op jit(solution)/shard_map/pallas_call | solution.py:310
  25.6 0.6 %collective-permute-start.3 = (f32[128,128]{1,0:T(8,128)S(1)}, f32[128,128]{1,0:T(8,128)S(1)}, u32[]{:S(2)}, u32[]{:S(2)}) collective-permute-start(f32[128,128]{1,0:T(8,128)S(1)} %add.28), channel_id=1, source_target_pairs={{0,2},{2,0},{4,6},{6,4},{8,10},{10,8},{12,14},{14,12},{16,18},{18,... | collective-permute-start | bytes 196616 | tf_op jit(solution)/shard_map/ppermute | solution.py:349
  26.2 1.7 %collective-permute-start.8 = (f32[128,128]{1,0:T(8,128)S(1)}, f32[128,128]{1,0:T(8,128)S(1)}, u32[]{:S(2)}, u32[]{:S(2)}) collective-permute-start(f32[128,128]{1,0:T(8,128)S(1)} %add.33), channel_id=1, source_target_pairs={{0,16},{2,18},{4,20},{6,22},{8,24},{10,26},{12,28},{14,30},{16,0},... | collective-permute-start | bytes 196616 | tf_op jit(solution)/shard_map/ppermute | solution.py:349
  27.8 2.3 %shard_map.99 = (f32[128,128]{1,0:T(8,128)S(1)}, f32[128,128]{1,0:T(8,128)S(1)}) custom-call(s32[4,8192]{1,0:T(4,128)S(1)} %get-tuple-element.34.pos_ref, f32[4,8192]{1,0:T(4,128)S(1)} %copy-done.3, f32[4,8192]{1,0:T(4,128)S(1)} %copy-done.4, s32[4,8192]{1,0:T(4,128)S(1)} %copy-done.5), custom_call_target="tpu_custom_call" | custom-call | flops 1000000000 | bytes 2097152 | tf_op jit(solution)/shard_map/pallas_call | solution.py:310
  30.2 1.6 %collective-permute-start.4 = (f32[128,128]{1,0:T(8,128)S(1)}, f32[128,128]{1,0:T(8,128)S(1)}, u32[]{:S(2)}, u32[]{:S(2)}) collective-permute-start(f32[128,128]{1,0:T(8,128)S(1)} %add.29), channel_id=1, source_target_pairs={{0,4},{2,6},{4,0},{6,2},{8,12},{10,14},{12,8},{14,10},{16,20},{18,... | collective-permute-start | bytes 196616 | tf_op jit(solution)/shard_map/ppermute | solution.py:349
  31.8 2.2 %shard_map.100 = (f32[32,8,512]{2,1,0:T(8,128)S(1)}, f32[8,128]{1,0:T(8,128)S(1)}) custom-call(f32[128,128]{1,0:T(8,128)S(1)} %add.34.seen_ref, f32[128,128]{1,0:T(8,128)S(1)} %get-tuple-element.40.want_ref, f32[128,128]{1,0:T(8,128)S(1)} %get-tuple-element.41.keep_ref, s32[128,128]{1,0:T(8,128)S(1)} %get-tuple-element.42.place_ref, ...), custom_call_target="tpu_custom_call" | custom-call | flops 1000000000 | bytes 2097152 | tf_op jit(solution)/shard_map/pallas_call | solution.py:310
  34.0 0.5 %collective-permute-done.4 = f32[128,128]{1,0:T(8,128)S(1)} collective-permute-done((f32[128,128]{1,0:T(8,128)S(1)}, f32[128,128]{1,0:T(8,128)S(1)}, u32[]{:S(2)}, u32[]{:S(2)}) %collective-permute-start.4) | collective-permute-done | bytes 65568 | tf_op jit(solution)/shard_map/ppermute | solution.py:349
  34.5 2.3 %shard_map.101 = (f32[32,8,512]{2,1,0:T(8,128)S(1)}, f32[8,128]{1,0:T(8,128)S(1)}) custom-call(f32[128,128]{1,0:T(8,128)S(1)} %add.30.seen_ref, f32[128,128]{1,0:T(8,128)S(1)} %get-tuple-element.35.want_ref, f32[128,128]{1,0:T(8,128)S(1)} %get-tuple-element.36.keep_ref, s32[128,128]{1,0:T(8,128)S(1)} %get-tuple-element.37.place_ref, ...), custom_call_target="tpu_custom_call" | custom-call | flops 1000000000 | bytes 2097152 | tf_op jit(solution)/shard_map/pallas_call | solution.py:310
  36.8 0.1 collective-permute-start.9
  36.9 1.3 %collective-permute-done.9.refs_0_ = f32[8,8,512]{2,1,0:T(8,128)S(1)} collective-permute-done((f32[8,8,512]{2,1,0:T(8,128)S(1)}, f32[8,8,512]{2,1,0:T(8,128)S(1)}, u32[]{:S(2)}, u32[]{:S(2)}) %collective-permute-start.9) | collective-permute-done | bytes 131104 | tf_op jit(solution)/shard_map/ppermute | solution.py:327
  38.2 1.1 %shard_map.102 = (f32[32,8,512]{2,1,0:T(8,128)S(1)}, f32[32,128]{1,0:T(8,128)S(1)}) custom-call(f32[8,8,512]{2,1,0:T(8,128)S(1)} %collective-permute-done.9.refs_0_, f32[32,8,512]{2,1,0:T(8,128)S(1)} %get-tuple-element.46.refs_1_, bf16[512,512]{1,0:T(8,128)(2,1)S(1)} %copy-done.6, bf16[512,512]{1,0:T(8,128)(2,1)S(1)} %copy-done.7, ...), custom_call_target="tpu_custom_call" | custom-call | flops 1000000000 | bytes 2097152 | tf_op jit(solution)/shard_map/pallas_call | solution.py:310
  39.3 11.2 %all_to_all.11 = f32[32,1,128]{2,1,0:T(1,128)S(1)} all-to-all(f32[32,1,128]{2,1,0:T(1,128)S(1)} %bitcast.13), channel_id=1, replica_groups=mesh['mem'=16,'lat'=2] {'mem','lat'}, dimensions={0} | all-to-all | bytes 32768 | tf_op jit(solution)/shard_map/all_to_all | solution.py:425
  50.6 1.0 %shard_map.103 = (f32[32,8,512]{2,1,0:T(8,128)}, f32[1,1]{1,0:T(1,128)}) custom-call(f32[32,128]{1,0:T(8,128)S(1)} %bitcast.12, f32[32,8,512]{2,1,0:T(8,128)S(1)} %bitcast.11, f32[32,8,512]{2,1,0:T(8,128)S(1)} %get-tuple-element.49.grad_ref), custom_call_target="tpu_custom_call" | custom-call | flops 100000000 | bytes 2097152 | tf_op jit(solution)/shard_map/pallas_call | solution.py:310
  (31 shorter events, 0.2 us)
Async XLA Ops:
  0.6 6.2 %copy-start = (f32[1,32,8,512]{3,2,1,0:T(8,128)S(1)}, f32[1,32,8,512]{3,2,1,0:T(8,128)}, u32[]{:S(2)}) copy-start(f32[1,32,8,512]{3,2,1,0:T(8,128)} %param.9) | copy-start | bytes 1572868
  0.6 6.2 %copy-start.1 = (bf16[1,4,32,8,512]{4,3,2,1,0:T(8,128)(2,1)S(1)}, bf16[1,4,32,8,512]{4,3,2,1,0:T(8,128)(2,1)}, u32[]{:S(2)}) copy-start(bf16[1,4,32,8,512]{4,3,2,1,0:T(8,128)(2,1)} %param.8) | copy-start | bytes 3145732
  0.6 6.2 %collective-permute-start = (f32[32,8,512]{2,1,0:T(8,128)}, f32[32,8,512]{2,1,0:T(8,128)S(1)}, u32[]{:S(2)}, u32[]{:S(2)}) collective-permute-start(f32[32,8,512]{2,1,0:T(8,128)} %bitcast.8), channel_id=1, source_target_pairs={{0,1},{1,0},{2,3},{3,2},{4,5},{5,4},{6,7},{7,6},{8,9},{9,8},{10,11... | collective-permute-start | bytes 1572872 | tf_op jit(solution)/shard_map/ppermute | solution.py:410
  1.2 0.9 %copy-start.2 = (s32[4,8192]{1,0:T(4,128)S(1)}, s32[4,8192]{1,0:T(4,128)}, u32[]{:S(2)}) copy-start(s32[4,8192]{1,0:T(4,128)} %cell_ref.1) | copy-start | bytes 393220
  2.1 4.8 %copy-start.6 = (bf16[512,512]{1,0:T(8,128)(2,1)S(1)}, bf16[512,512]{1,0:T(8,128)(2,1)}, u32[]{:S(2)}) copy-start(bf16[512,512]{1,0:T(8,128)(2,1)} %constant.16.clone.circ_high_ref.refs_2_) | copy-start | bytes 1572868
  2.1 4.8 %copy-start.7 = (bf16[512,512]{1,0:T(8,128)(2,1)S(1)}, bf16[512,512]{1,0:T(8,128)(2,1)}, u32[]{:S(2)}) copy-start(bf16[512,512]{1,0:T(8,128)(2,1)} %constant.17.clone.circ_low_ref.refs_3_) | copy-start | bytes 1572868
  9.6 6.5 %collective-permute-start.5 = (f32[128,128]{1,0:T(8,128)S(1)}, f32[128,128]{1,0:T(8,128)S(1)}, u32[]{:S(2)}, u32[]{:S(2)}) collective-permute-start(f32[128,128]{1,0:T(8,128)S(1)} %get-tuple-element.39), channel_id=1, source_target_pairs={{0,2},{2,0},{4,6},{6,4},{8,10},{10,8},{12,14},{14,12},{16,18},{18,... | collective-permute-start | bytes 196616 | tf_op jit(solution)/shard_map/ppermute | solution.py:349
  14.5 4.3 %collective-permute-start.1 = (f32[128,128]{1,0:T(8,128)S(1)}, f32[128,128]{1,0:T(8,128)S(1)}, u32[]{:S(2)}, u32[]{:S(2)}) collective-permute-start(f32[128,128]{1,0:T(8,128)S(1)} %shard_map.97), channel_id=1, source_target_pairs={{0,8},{2,10},{4,12},{6,14},{8,0},{10,2},{12,4},{14,6},{16,24},{18,... | collective-permute-start | bytes 196616 | tf_op jit(solution)/shard_map/ppermute | solution.py:349
  16.2 5.4 %collective-permute-start.6 = (f32[128,128]{1,0:T(8,128)S(1)}, f32[128,128]{1,0:T(8,128)S(1)}, u32[]{:S(2)}, u32[]{:S(2)}) collective-permute-start(f32[128,128]{1,0:T(8,128)S(1)} %add.31), channel_id=1, source_target_pairs={{0,4},{2,6},{4,0},{6,2},{8,12},{10,14},{12,8},{14,10},{16,20},{18,... | collective-permute-start | bytes 196616 | tf_op jit(solution)/shard_map/ppermute | solution.py:349
  18.8 4.4 %copy-start.4 = (f32[4,8192]{1,0:T(4,128)S(1)}, f32[4,8192]{1,0:T(4,128)}, u32[]{:S(2)}) copy-start(f32[4,8192]{1,0:T(4,128)} %weight_ref.3) | copy-start | bytes 393220
  18.8 4.4 %copy-start.5 = (s32[4,8192]{1,0:T(4,128)S(1)}, s32[4,8192]{1,0:T(4,128)}, u32[]{:S(2)}) copy-start(s32[4,8192]{1,0:T(4,128)} %quality_ref.3) | copy-start | bytes 393220
  18.9 4.4 %copy-start.3 = (f32[4,8192]{1,0:T(4,128)S(1)}, f32[4,8192]{1,0:T(4,128)}, u32[]{:S(2)}) copy-start(f32[4,8192]{1,0:T(4,128)} %innov_ref.3) | copy-start | bytes 393220
  18.9 6.7 %collective-permute-start.2 = (f32[128,128]{1,0:T(8,128)S(1)}, f32[128,128]{1,0:T(8,128)S(1)}, u32[]{:S(2)}, u32[]{:S(2)}) collective-permute-start(f32[128,128]{1,0:T(8,128)S(1)} %add.27), channel_id=1, source_target_pairs={{0,16},{2,18},{4,20},{6,22},{8,24},{10,26},{12,28},{14,30},{16,0},... | collective-permute-start | bytes 196616 | tf_op jit(solution)/shard_map/ppermute | solution.py:349
  21.6 4.6 %collective-permute-start.7 = (f32[128,128]{1,0:T(8,128)S(1)}, f32[128,128]{1,0:T(8,128)S(1)}, u32[]{:S(2)}, u32[]{:S(2)}) collective-permute-start(f32[128,128]{1,0:T(8,128)S(1)} %add.32), channel_id=1, source_target_pairs={{0,8},{2,10},{4,12},{6,14},{8,0},{10,2},{12,4},{14,6},{16,24},{18,... | collective-permute-start | bytes 196616 | tf_op jit(solution)/shard_map/ppermute | solution.py:349
  25.6 4.6 %collective-permute-start.3 = (f32[128,128]{1,0:T(8,128)S(1)}, f32[128,128]{1,0:T(8,128)S(1)}, u32[]{:S(2)}, u32[]{:S(2)}) collective-permute-start(f32[128,128]{1,0:T(8,128)S(1)} %add.28), channel_id=1, source_target_pairs={{0,2},{2,0},{4,6},{6,4},{8,10},{10,8},{12,14},{14,12},{16,18},{18,... | collective-permute-start | bytes 196616 | tf_op jit(solution)/shard_map/ppermute | solution.py:349
  26.2 5.6 %collective-permute-start.8 = (f32[128,128]{1,0:T(8,128)S(1)}, f32[128,128]{1,0:T(8,128)S(1)}, u32[]{:S(2)}, u32[]{:S(2)}) collective-permute-start(f32[128,128]{1,0:T(8,128)S(1)} %add.33), channel_id=1, source_target_pairs={{0,16},{2,18},{4,20},{6,22},{8,24},{10,26},{12,28},{14,30},{16,0},... | collective-permute-start | bytes 196616 | tf_op jit(solution)/shard_map/ppermute | solution.py:349
  30.2 4.3 %collective-permute-start.4 = (f32[128,128]{1,0:T(8,128)S(1)}, f32[128,128]{1,0:T(8,128)S(1)}, u32[]{:S(2)}, u32[]{:S(2)}) collective-permute-start(f32[128,128]{1,0:T(8,128)S(1)} %add.29), channel_id=1, source_target_pairs={{0,4},{2,6},{4,0},{6,2},{8,12},{10,14},{12,8},{14,10},{16,20},{18,... | collective-permute-start | bytes 196616 | tf_op jit(solution)/shard_map/ppermute | solution.py:349
  36.8 1.4 %collective-permute-start.9 = (f32[8,8,512]{2,1,0:T(8,128)S(1)}, f32[8,8,512]{2,1,0:T(8,128)S(1)}, u32[]{:S(2)}, u32[]{:S(2)}) collective-permute-start(f32[8,8,512]{2,1,0:T(8,128)S(1)} %constant_dynamic-slice_fusion), channel_id=1, source_target_pairs={{0,1},{1,0},{2,3},{3,2},{4,5},{5,4},{6,7},{7,6},{8,9},{9,8},{10,11... | collective-permute-start | bytes 393224 | tf_op jit(solution)/shard_map/ppermute | solution.py:327

commit v9 on v8

--- a/solution.py
+++ b/solution.py
@@ -107,7 +107,7 @@
     bin_ids = small_ids((bins, LANES))
     square = (LANES, LANES)
     upper = (ids_of(square, 0) <= ids_of(square, 1)).astype(jnp.bfloat16)
-    counting = jnp.concatenate([upper, jnp.ones((LANES, 128), jnp.bfloat16)], axis=1)
+    ones = jnp.ones((LANES, 128), jnp.bfloat16)
     before = (ids_of((bins, bins), 1) < ids_of((bins, bins), 0)).astype(jnp.bfloat16)
     count = functools.partial(jnp.dot, before, preferred_element_type=jnp.float32)
     wide = lambda v: jnp.concatenate([v] * (LANES // 128), axis=1)
@@ -124,10 +124,8 @@
         prefix_ref = prefix_refs[slot]
         in_bin = bins_of[slot : slot + 1]
         hots = [one_hot(bin_ids, in_bin[:, at * LANES : (at + 1) * LANES]) for at in range(tiles)]
-        prefix_ref[...] = jnp.dot(jnp.concatenate(hots, axis=0), counting, preferred_element_type=jnp.float32)
-        total = jnp.zeros((bins, 128), jnp.float32)
-        for at in range(tiles):
-            total += prefix_ref[pl.ds(at * bins, bins), pl.ds(LANES, 128)]
+        prefix_ref[...] = jnp.dot(jnp.concatenate(hots, axis=0), upper, preferred_element_type=jnp.float32)
+        total = jnp.dot(sum(hots[1:], hots[0]), ones, preferred_element_type=jnp.float32)
         many = jnp.floor(total * (1.0 / LANES))
         few = total - many * LANES
         carry = count(many.astype(jnp.bfloat16)) * LANES + count(few.astype(jnp.bfloat16)) - 1.0
@@ -136,7 +134,7 @@
             here = pl.ds(at * bins, bins)
             place = (prefix_ref[here, pl.ds(0, LANES)] + wide(carry)) * hots[at].astype(jnp.float32)
             places.append(jnp.sum(place, axis=0, keepdims=True))
-            carry += prefix_ref[here, pl.ds(LANES, 128)]
+            carry += prefix_ref[here, pl.ds(LANES - 1, 1)]
         pos = jnp.concatenate(places, axis=1).astype(jnp.int32)
         pos_ref[pl.ds(slot, 1), :] = pos
         key, lane = permute(pos, [keys[slot : slot + 1], signed[slot : slot + 1]], pieces)
@@ -361,7 +359,7 @@
         ordered = (len(group) * obs // PIECE, PIECE)
         kinds += [like(ordered, jnp.int32), like(ordered)] * 2
         kinds += [like((-(-3 * len(group) // 8) * 8, -(-(obs // PIECE) // 128) * 128), jnp.int32)]
-    scratch = [pltpu.VMEM((obs // LANES * shape[0] // BIN, LANES + 128), jnp.float32)] * slots
+    scratch = [pltpu.VMEM((obs // LANES * shape[0] // BIN, LANES), jnp.float32)] * slots
     pos, *outs = call(functools.partial(sort_kernel, shape, groups), kinds, scratch, COST, obs_cell)
     outs = [outs[k : k + 5] for k in range(0, len(outs), 5)]
     return pos, [(out[:2], out[2:4], out[4]) for out in outs]

time: 51.7 us -> 51.2 us (level)
  transfers between devices with their start and end apart: 10 -> 10, of which waited for: 3 -> 3; matrix products, arithmetic and copies ran while one was open for 0% -> 0% of each run, Pallas kernels for 27% -> 26%
where the time goes in v9:
time: 51.2 us; the launch traced here: 51 us
  Pallas kernels  20.3 us (40%)
  starting transfers between devices  14.6 us (29%)
  blocking collectives  11.2 us (22%)
  waiting for transfers between devices  3.02 us (6%)
  local copies, waits for them, and re-layouts  0.96 us (2%)
  between operations  0.82 us (2%)
    pallas_call x9, Pallas kernels, call(): pl.pallas_call(body, out_shape=out_shape, in_specs=[vmem] * len(operands)...  20.3 us
    ppermute x8, starting transfers between devices, summed(): lax.ppermute(value, axis, [(i, i ^ away) for i in range(count)])  14 us
    all_to_all x1, blocking collectives, local(): sums = lax.all_to_all(sums, ('mem', 'lat'), 0, 0, tiled=True)  11.2 us
    ppermute x8, waiting for transfers between devices, summed(): lax.ppermute(value, axis, [(i, i ^ away) for i in range(count)])  1.68 us
    ppermute x1, waiting for transfers between devices, edges(): return [lax.ppermute(edge, 'lat', [(0, 1), (1, 0)])]  1.33 us
  transfers between devices with their start and end apart: 10, of which 3 were waited for; matrix products, arithmetic and copies ran while one was open for 0% of the time, Pallas kernels for 26%

profile of v9, /device:TPU:0, one launch (start us, length us, event | category | flops | bytes accessed | tf_op | source)
XLA Modules:
  0.0 51.0 jit_solution(3300066513761142115)
XLA Ops:
  0.6 0.5 %collective-permute-start = (f32[32,8,512]{2,1,0:T(8,128)}, f32[32,8,512]{2,1,0:T(8,128)S(1)}, u32[]{:S(2)}, u32[]{:S(2)}) collective-permute-start(f32[32,8,512]{2,1,0:T(8,128)} %bitcast.8), channel_id=1, source_target_pairs={{0,1},{1,0},{2,3},{3,2},{4,5},{5,4},{6,7},{7,6},{8,9},{9,8},{10,11... | collective-permute-start | bytes 1572872 | tf_op jit(solution)/shard_map/ppermute | solution.py:408
  1.2 0.9 %copy-done.2 = s32[4,8192]{1,0:T(4,128)S(1)} copy-done((s32[4,8192]{1,0:T(4,128)S(1)}, s32[4,8192]{1,0:T(4,128)}, u32[]{:S(2)}) %copy-start.2) | copy-done | bytes 131096
  2.1 4.2 %shard_map.95 = (s32[4,8192]{1,0:T(4,128)S(1)}, s32[128,128]{1,0:T(8,128)S(1)}, f32[128,128]{1,0:T(8,128)S(1)}, s32[128,128]{1,0:T(8,128)S(1)}, f32[128,128]{1,0...) custom-call(s32[4,8192]{1,0:T(4,128)S(1)} %copy-done.2), custom_call_target="tpu_custom_call" | custom-call | flops 1000000000 | bytes 2097152 | tf_op jit(solution)/shard_map/pallas_call | solution.py:308
  6.4 2.8 %shard_map.96 = (f32[128,128]{1,0:T(8,128)S(1)}, f32[32,8,512]{2,1,0:T(8,128)S(1)}) custom-call(f32[32,8,512]{2,1,0:T(8,128)S(1)} %bitcast.9, bf16[512,512]{1,0:T(8,128)(2,1)S(1)} %copy-done.6, bf16[512,512]{1,0:T(8,128)(2,1)S(1)} %copy-done.7, f32[32,8,512]{2,1,0:T(8,128)S(1)} %collective-permute-done.refs_0_, bf16[4,32,8,512]{3,2,1,0:T(8,128)(2,1)S(1)} %bitcast.14, ...), custom_call_target="tpu_custom_call" | custom-call | flops 1000000000 | bytes 2097152 | tf_op jit(solution)/shard_map/pallas_call | solution.py:308
  9.1 2.6 %collective-permute-start.5 = (f32[128,128]{1,0:T(8,128)S(1)}, f32[128,128]{1,0:T(8,128)S(1)}, u32[]{:S(2)}, u32[]{:S(2)}) collective-permute-start(f32[128,128]{1,0:T(8,128)S(1)} %get-tuple-element.39), channel_id=1, source_target_pairs={{0,2},{2,0},{4,6},{6,4},{8,10},{10,8},{12,14},{14,12},{16,18},{18,... | collective-permute-start | bytes 196616 | tf_op jit(solution)/shard_map/ppermute | solution.py:347
  11.8 2.2 %shard_map.97 = f32[128,128]{1,0:T(8,128)S(1)} custom-call(f32[32,8,512]{2,1,0:T(8,128)S(1)} %get-tuple-element.30.own_ref, bf16[512,512]{1,0:T(8,128)(2,1)S(1)} %copy-done.6, bf16[512,512]{1,0:T(8,128)(2,1)S(1)} %copy-done.7, bf16[4,32,8,512]{3,2,1,0:T(8,128)(2,1)S(1)} %bitcast.15, s32[128,128]{1,0:T(8,128)S(1)} %get-tuple-element.31.refs_1_, ...), custom_call_target="tpu_custom_call" | custom-call | flops 1000000000 | bytes 2097152 | tf_op jit(solution)/shard_map/pallas_call | solution.py:308
  14.0 1.6 %collective-permute-start.1 = (f32[128,128]{1,0:T(8,128)S(1)}, f32[128,128]{1,0:T(8,128)S(1)}, u32[]{:S(2)}, u32[]{:S(2)}) collective-permute-start(f32[128,128]{1,0:T(8,128)S(1)} %shard_map.97), channel_id=1, source_target_pairs={{0,8},{2,10},{4,12},{6,14},{8,0},{10,2},{12,4},{14,6},{16,24},{18,... | collective-permute-start | bytes 196616 | tf_op jit(solution)/shard_map/ppermute | solution.py:347
  15.6 1.6 %collective-permute-start.6 = (f32[128,128]{1,0:T(8,128)S(1)}, f32[128,128]{1,0:T(8,128)S(1)}, u32[]{:S(2)}, u32[]{:S(2)}) collective-permute-start(f32[128,128]{1,0:T(8,128)S(1)} %add.31), channel_id=1, source_target_pairs={{0,4},{2,6},{4,0},{6,2},{8,12},{10,14},{12,8},{14,10},{16,20},{18,... | collective-permute-start | bytes 196616 | tf_op jit(solution)/shard_map/ppermute | solution.py:347
  17.2 1.1 %collective-permute-done.1 = f32[128,128]{1,0:T(8,128)S(1)} collective-permute-done((f32[128,128]{1,0:T(8,128)S(1)}, f32[128,128]{1,0:T(8,128)S(1)}, u32[]{:S(2)}, u32[]{:S(2)}) %collective-permute-start.1) | collective-permute-done | bytes 65568 | tf_op jit(solution)/shard_map/ppermute | solution.py:347
  18.3 2.7 %collective-permute-start.2 = (f32[128,128]{1,0:T(8,128)S(1)}, f32[128,128]{1,0:T(8,128)S(1)}, u32[]{:S(2)}, u32[]{:S(2)}) collective-permute-start(f32[128,128]{1,0:T(8,128)S(1)} %add.27), channel_id=1, source_target_pairs={{0,16},{2,18},{4,20},{6,22},{8,24},{10,26},{12,28},{14,30},{16,0},... | collective-permute-start | bytes 196616 | tf_op jit(solution)/shard_map/ppermute | solution.py:347
  21.1 1.6 %collective-permute-start.7 = (f32[128,128]{1,0:T(8,128)S(1)}, f32[128,128]{1,0:T(8,128)S(1)}, u32[]{:S(2)}, u32[]{:S(2)}) collective-permute-start(f32[128,128]{1,0:T(8,128)S(1)} %add.32), channel_id=1, source_target_pairs={{0,8},{2,10},{4,12},{6,14},{8,0},{10,2},{12,4},{14,6},{16,24},{18,... | collective-permute-start | bytes 196616 | tf_op jit(solution)/shard_map/ppermute | solution.py:347
  22.7 2.3 %shard_map.98 = (f32[128,128]{1,0:T(8,128)S(1)}, f32[128,128]{1,0:T(8,128)S(1)}) custom-call(s32[4,8192]{1,0:T(4,128)S(1)} %get-tuple-element.34.pos_ref, f32[4,8192]{1,0:T(4,128)S(1)} %copy-done.3, f32[4,8192]{1,0:T(4,128)S(1)} %copy-done.4, s32[4,8192]{1,0:T(4,128)S(1)} %copy-done.5), custom_call_target="tpu_custom_call" | custom-call | flops 1000000000 | bytes 2097152 | tf_op jit(solution)/shard_map/pallas_call | solution.py:308
  25.0 0.6 %collective-permute-start.3 = (f32[128,128]{1,0:T(8,128)S(1)}, f32[128,128]{1,0:T(8,128)S(1)}, u32[]{:S(2)}, u32[]{:S(2)}) collective-permute-start(f32[128,128]{1,0:T(8,128)S(1)} %add.28), channel_id=1, source_target_pairs={{0,2},{2,0},{4,6},{6,4},{8,10},{10,8},{12,14},{14,12},{16,18},{18,... | collective-permute-start | bytes 196616 | tf_op jit(solution)/shard_map/ppermute | solution.py:347
  25.7 1.6 %collective-permute-start.8 = (f32[128,128]{1,0:T(8,128)S(1)}, f32[128,128]{1,0:T(8,128)S(1)}, u32[]{:S(2)}, u32[]{:S(2)}) collective-permute-start(f32[128,128]{1,0:T(8,128)S(1)} %add.33), channel_id=1, source_target_pairs={{0,16},{2,18},{4,20},{6,22},{8,24},{10,26},{12,28},{14,30},{16,0},... | collective-permute-start | bytes 196616 | tf_op jit(solution)/shard_map/ppermute | solution.py:347
  27.3 2.3 %shard_map.99 = (f32[128,128]{1,0:T(8,128)S(1)}, f32[128,128]{1,0:T(8,128)S(1)}) custom-call(s32[4,8192]{1,0:T(4,128)S(1)} %get-tuple-element.34.pos_ref, f32[4,8192]{1,0:T(4,128)S(1)} %copy-done.3, f32[4,8192]{1,0:T(4,128)S(1)} %copy-done.4, s32[4,8192]{1,0:T(4,128)S(1)} %copy-done.5), custom_call_target="tpu_custom_call" | custom-call | flops 1000000000 | bytes 2097152 | tf_op jit(solution)/shard_map/pallas_call | solution.py:308
  29.7 1.6 %collective-permute-start.4 = (f32[128,128]{1,0:T(8,128)S(1)}, f32[128,128]{1,0:T(8,128)S(1)}, u32[]{:S(2)}, u32[]{:S(2)}) collective-permute-start(f32[128,128]{1,0:T(8,128)S(1)} %add.29), channel_id=1, source_target_pairs={{0,4},{2,6},{4,0},{6,2},{8,12},{10,14},{12,8},{14,10},{16,20},{18,... | collective-permute-start | bytes 196616 | tf_op jit(solution)/shard_map/ppermute | solution.py:347
  31.2 2.2 %shard_map.100 = (f32[32,8,512]{2,1,0:T(8,128)S(1)}, f32[8,128]{1,0:T(8,128)S(1)}) custom-call(f32[128,128]{1,0:T(8,128)S(1)} %add.34.seen_ref, f32[128,128]{1,0:T(8,128)S(1)} %get-tuple-element.40.want_ref, f32[128,128]{1,0:T(8,128)S(1)} %get-tuple-element.41.keep_ref, s32[128,128]{1,0:T(8,128)S(1)} %get-tuple-element.42.place_ref, ...), custom_call_target="tpu_custom_call" | custom-call | flops 1000000000 | bytes 2097152 | tf_op jit(solution)/shard_map/pallas_call | solution.py:308
  33.4 0.5 %collective-permute-done.4 = f32[128,128]{1,0:T(8,128)S(1)} collective-permute-done((f32[128,128]{1,0:T(8,128)S(1)}, f32[128,128]{1,0:T(8,128)S(1)}, u32[]{:S(2)}, u32[]{:S(2)}) %collective-permute-start.4) | collective-permute-done | bytes 65568 | tf_op jit(solution)/shard_map/ppermute | solution.py:347
  34.0 2.3 %shard_map.101 = (f32[32,8,512]{2,1,0:T(8,128)S(1)}, f32[8,128]{1,0:T(8,128)S(1)}) custom-call(f32[128,128]{1,0:T(8,128)S(1)} %add.30.seen_ref, f32[128,128]{1,0:T(8,128)S(1)} %get-tuple-element.35.want_ref, f32[128,128]{1,0:T(8,128)S(1)} %get-tuple-element.36.keep_ref, s32[128,128]{1,0:T(8,128)S(1)} %get-tuple-element.37.place_ref, ...), custom_call_target="tpu_custom_call" | custom-call | flops 1000000000 | bytes 2097152 | tf_op jit(solution)/shard_map/pallas_call | solution.py:308
  36.3 0.1 collective-permute-start.9
  36.4 1.3 %collective-permute-done.9.refs_0_ = f32[8,8,512]{2,1,0:T(8,128)S(1)} collective-permute-done((f32[8,8,512]{2,1,0:T(8,128)S(1)}, f32[8,8,512]{2,1,0:T(8,128)S(1)}, u32[]{:S(2)}, u32[]{:S(2)}) %collective-permute-start.9) | collective-permute-done | bytes 131104 | tf_op jit(solution)/shard_map/ppermute | solution.py:325
  37.7 1.1 %shard_map.102 = (f32[32,8,512]{2,1,0:T(8,128)S(1)}, f32[32,128]{1,0:T(8,128)S(1)}) custom-call(f32[8,8,512]{2,1,0:T(8,128)S(1)} %collective-permute-done.9.refs_0_, f32[32,8,512]{2,1,0:T(8,128)S(1)} %get-tuple-element.46.refs_1_, bf16[512,512]{1,0:T(8,128)(2,1)S(1)} %copy-done.6, bf16[512,512]{1,0:T(8,128)(2,1)S(1)} %copy-done.7, ...), custom_call_target="tpu_custom_call" | custom-call | flops 1000000000 | bytes 2097152 | tf_op jit(solution)/shard_map/pallas_call | solution.py:308
  38.8 11.2 %all_to_all.11 = f32[32,1,128]{2,1,0:T(1,128)S(1)} all-to-all(f32[32,1,128]{2,1,0:T(1,128)S(1)} %bitcast.13), channel_id=1, replica_groups=mesh['mem'=16,'lat'=2] {'mem','lat'}, dimensions={0} | all-to-all | bytes 32768 | tf_op jit(solution)/shard_map/all_to_all | solution.py:423
  50.0 1.0 %shard_map.103 = (f32[32,8,512]{2,1,0:T(8,128)}, f32[1,1]{1,0:T(1,128)}) custom-call(f32[32,128]{1,0:T(8,128)S(1)} %bitcast.12, f32[32,8,512]{2,1,0:T(8,128)S(1)} %bitcast.11, f32[32,8,512]{2,1,0:T(8,128)S(1)} %get-tuple-element.49.grad_ref), custom_call_target="tpu_custom_call" | custom-call | flops 100000000 | bytes 2097152 | tf_op jit(solution)/shard_map/pallas_call | solution.py:308
  (31 shorter events, 0.2 us)
Async XLA Ops:
  0.6 5.7 %copy-start = (f32[1,32,8,512]{3,2,1,0:T(8,128)S(1)}, f32[1,32,8,512]{3,2,1,0:T(8,128)}, u32[]{:S(2)}) copy-start(f32[1,32,8,512]{3,2,1,0:T(8,128)} %param.9) | copy-start | bytes 1572868
  0.6 5.7 %copy-start.1 = (bf16[1,4,32,8,512]{4,3,2,1,0:T(8,128)(2,1)S(1)}, bf16[1,4,32,8,512]{4,3,2,1,0:T(8,128)(2,1)}, u32[]{:S(2)}) copy-start(bf16[1,4,32,8,512]{4,3,2,1,0:T(8,128)(2,1)} %param.8) | copy-start | bytes 3145732
  0.6 5.7 %collective-permute-start = (f32[32,8,512]{2,1,0:T(8,128)}, f32[32,8,512]{2,1,0:T(8,128)S(1)}, u32[]{:S(2)}, u32[]{:S(2)}) collective-permute-start(f32[32,8,512]{2,1,0:T(8,128)} %bitcast.8), channel_id=1, source_target_pairs={{0,1},{1,0},{2,3},{3,2},{4,5},{5,4},{6,7},{7,6},{8,9},{9,8},{10,11... | collective-permute-start | bytes 1572872 | tf_op jit(solution)/shard_map/ppermute | solution.py:408
  1.2 0.9 %copy-start.2 = (s32[4,8192]{1,0:T(4,128)S(1)}, s32[4,8192]{1,0:T(4,128)}, u32[]{:S(2)}) copy-start(s32[4,8192]{1,0:T(4,128)} %cell_ref.1) | copy-start | bytes 393220
  2.1 4.3 %copy-start.6 = (bf16[512,512]{1,0:T(8,128)(2,1)S(1)}, bf16[512,512]{1,0:T(8,128)(2,1)}, u32[]{:S(2)}) copy-start(bf16[512,512]{1,0:T(8,128)(2,1)} %constant.16.clone.circ_high_ref.refs_2_) | copy-start | bytes 1572868
  2.1 4.3 %copy-start.7 = (bf16[512,512]{1,0:T(8,128)(2,1)S(1)}, bf16[512,512]{1,0:T(8,128)(2,1)}, u32[]{:S(2)}) copy-start(bf16[512,512]{1,0:T(8,128)(2,1)} %constant.17.clone.circ_low_ref.refs_3_) | copy-start | bytes 1572868
  9.1 6.5 %collective-permute-start.5 = (f32[128,128]{1,0:T(8,128)S(1)}, f32[128,128]{1,0:T(8,128)S(1)}, u32[]{:S(2)}, u32[]{:S(2)}) collective-permute-start(f32[128,128]{1,0:T(8,128)S(1)} %get-tuple-element.39), channel_id=1, source_target_pairs={{0,2},{2,0},{4,6},{6,4},{8,10},{10,8},{12,14},{14,12},{16,18},{18,... | collective-permute-start | bytes 196616 | tf_op jit(solution)/shard_map/ppermute | solution.py:347
  14.0 4.3 %collective-permute-start.1 = (f32[128,128]{1,0:T(8,128)S(1)}, f32[128,128]{1,0:T(8,128)S(1)}, u32[]{:S(2)}, u32[]{:S(2)}) collective-permute-start(f32[128,128]{1,0:T(8,128)S(1)} %shard_map.97), channel_id=1, source_target_pairs={{0,8},{2,10},{4,12},{6,14},{8,0},{10,2},{12,4},{14,6},{16,24},{18,... | collective-permute-start | bytes 196616 | tf_op jit(solution)/shard_map/ppermute | solution.py:347
  15.6 5.4 %collective-permute-start.6 = (f32[128,128]{1,0:T(8,128)S(1)}, f32[128,128]{1,0:T(8,128)S(1)}, u32[]{:S(2)}, u32[]{:S(2)}) collective-permute-start(f32[128,128]{1,0:T(8,128)S(1)} %add.31), channel_id=1, source_target_pairs={{0,4},{2,6},{4,0},{6,2},{8,12},{10,14},{12,8},{14,10},{16,20},{18,... | collective-permute-start | bytes 196616 | tf_op jit(solution)/shard_map/ppermute | solution.py:347
  18.3 4.4 %copy-start.4 = (f32[4,8192]{1,0:T(4,128)S(1)}, f32[4,8192]{1,0:T(4,128)}, u32[]{:S(2)}) copy-start(f32[4,8192]{1,0:T(4,128)} %weight_ref.3) | copy-start | bytes 393220
  18.3 4.4 %copy-start.5 = (s32[4,8192]{1,0:T(4,128)S(1)}, s32[4,8192]{1,0:T(4,128)}, u32[]{:S(2)}) copy-start(s32[4,8192]{1,0:T(4,128)} %quality_ref.3) | copy-start | bytes 393220
  18.3 4.3 %copy-start.3 = (f32[4,8192]{1,0:T(4,128)S(1)}, f32[4,8192]{1,0:T(4,128)}, u32[]{:S(2)}) copy-start(f32[4,8192]{1,0:T(4,128)} %innov_ref.3) | copy-start | bytes 393220
  18.3 6.7 %collective-permute-start.2 = (f32[128,128]{1,0:T(8,128)S(1)}, f32[128,128]{1,0:T(8,128)S(1)}, u32[]{:S(2)}, u32[]{:S(2)}) collective-permute-start(f32[128,128]{1,0:T(8,128)S(1)} %add.27), channel_id=1, source_target_pairs={{0,16},{2,18},{4,20},{6,22},{8,24},{10,26},{12,28},{14,30},{16,0},... | collective-permute-start | bytes 196616 | tf_op jit(solution)/shard_map/ppermute | solution.py:347
  21.1 4.6 %collective-permute-start.7 = (f32[128,128]{1,0:T(8,128)S(1)}, f32[128,128]{1,0:T(8,128)S(1)}, u32[]{:S(2)}, u32[]{:S(2)}) collective-permute-start(f32[128,128]{1,0:T(8,128)S(1)} %add.32), channel_id=1, source_target_pairs={{0,8},{2,10},{4,12},{6,14},{8,0},{10,2},{12,4},{14,6},{16,24},{18,... | collective-permute-start | bytes 196616 | tf_op jit(solution)/shard_map/ppermute | solution.py:347
  25.0 4.6 %collective-permute-start.3 = (f32[128,128]{1,0:T(8,128)S(1)}, f32[128,128]{1,0:T(8,128)S(1)}, u32[]{:S(2)}, u32[]{:S(2)}) collective-permute-start(f32[128,128]{1,0:T(8,128)S(1)} %add.28), channel_id=1, source_target_pairs={{0,2},{2,0},{4,6},{6,4},{8,10},{10,8},{12,14},{14,12},{16,18},{18,... | collective-permute-start | bytes 196616 | tf_op jit(solution)/shard_map/ppermute | solution.py:347
  25.7 5.5 %collective-permute-start.8 = (f32[128,128]{1,0:T(8,128)S(1)}, f32[128,128]{1,0:T(8,128)S(1)}, u32[]{:S(2)}, u32[]{:S(2)}) collective-permute-start(f32[128,128]{1,0:T(8,128)S(1)} %add.33), channel_id=1, source_target_pairs={{0,16},{2,18},{4,20},{6,22},{8,24},{10,26},{12,28},{14,30},{16,0},... | collective-permute-start | bytes 196616 | tf_op jit(solution)/shard_map/ppermute | solution.py:347
  29.7 4.3 %collective-permute-start.4 = (f32[128,128]{1,0:T(8,128)S(1)}, f32[128,128]{1,0:T(8,128)S(1)}, u32[]{:S(2)}, u32[]{:S(2)}) collective-permute-start(f32[128,128]{1,0:T(8,128)S(1)} %add.29), channel_id=1, source_target_pairs={{0,4},{2,6},{4,0},{6,2},{8,12},{10,14},{12,8},{14,10},{16,20},{18,... | collective-permute-start | bytes 196616 | tf_op jit(solution)/shard_map/ppermute | solution.py:347
  36.3 1.4 %collective-permute-start.9 = (f32[8,8,512]{2,1,0:T(8,128)S(1)}, f32[8,8,512]{2,1,0:T(8,128)S(1)}, u32[]{:S(2)}, u32[]{:S(2)}) collective-permute-start(f32[8,8,512]{2,1,0:T(8,128)S(1)} %constant_dynamic-slice_fusion), channel_id=1, source_target_pairs={{0,1},{1,0},{2,3},{3,2},{4,5},{5,4},{6,7},{7,6},{8,9},{9,8},{10,11... | collective-permute-start | bytes 393224 | tf_op jit(solution)/shard_map/ppermute | solution.py:325

commit v10 on v9

--- a/solution.py
+++ b/solution.py
@@ -296,20 +296,31 @@
     sums_ref[...] = jnp.where(lane == 0, square, jnp.where(lane == 1, prior, jnp.where(lane == 2, obs_cost, 0.0)))
 
 
-def update_kernel(members, entries, sums_ref, own_ref, grad_ref, new_ref, cost_ref):
+def update_kernel(members, entries, sums_ref, own_ref, grad_ref, new_ref, cost_ref, ready_ref, sems):
     totals = jnp.sum(sums_ref[...], axis=0, keepdims=True)
     length = jnp.sqrt(totals[:, :1] / entries + EPSILON)
-    new_ref[...] = own_ref[...] - grad_ref[...] * (STEP_LENGTH / length)[None]
+    scale = (STEP_LENGTH / length)[None]
+    rows = own_ref.shape[0]
+    copies = []
+    for k, begin in enumerate(range(0, rows, HALF)):
+        here = pl.ds(begin, HALF)
+        ready_ref[here] = own_ref[here] - grad_ref[here] * scale
+        copies.append(pltpu.make_async_copy(ready_ref.at[here], new_ref.at[here], sems.at[k]))
+        copies[-1].start()
     cost_ref[...] = (0.5 * totals[:, 1:2] + 0.5 * totals[:, 2:3] / members) / entries
-
-
-def call(body, out_shape, scratch, flops, *operands):
+    for copy in copies:
+        copy.wait()
+
+
+def call(body, out_shape, scratch, flops, *operands, unplaced=0):
     vmem = pl.BlockSpec(memory_space=pltpu.VMEM)
     return pl.pallas_call(
         body,
         out_shape=out_shape,
         in_specs=[vmem] * len(operands),
-        out_specs=jax.tree.map(lambda _: vmem, out_shape),
+        out_specs=[pl.BlockSpec(memory_space=pl.ANY)] * unplaced + [vmem] * (len(out_shape) - unplaced)
+        if unplaced
+        else jax.tree.map(lambda _: vmem, out_shape),
         scratch_shapes=scratch,
         compiler_params=pltpu.CompilerParams(vmem_limit_bytes=48 * MIB),
         cost_estimate=pl.CostEstimate(flops=flops, bytes_accessed=2 * MIB, transcendentals=0),
@@ -422,7 +433,8 @@
     grad, sums = gradient(edges(back), back, circ, own, obs_cost, members * bands)
     sums = lax.all_to_all(sums, ("mem", "lat"), 0, 0, tiled=True)
     body = functools.partial(update_kernel, members, float(members * bands * rows * levels * lons))
-    new_weights, cost = call(body, [like(own.shape), like((1, 1))], [], 10**8, sums, own, grad)
+    scratch = [pltpu.VMEM(own.shape, jnp.float32), pltpu.SemaphoreType.DMA((rows // HALF,))]
+    new_weights, cost = call(body, [like(own.shape), like((1, 1))], scratch, COST, sums, own, grad, unplaced=1)
     return new_weights[None], cost[0, 0]
 
 

time: 51.2 us -> 51.8 us (1.012)
  no operation moved by 1% of the time
where the time goes in v10:
time: 51.8 us; the launch traced here: 51.6 us
  Pallas kernels  20.8 us (40%)
  starting transfers between devices  14.6 us (28%)
  blocking collectives  11.2 us (22%)
  waiting for transfers between devices  3.02 us (6%)
  between operations  0.98 us (2%)
  local copies, waits for them, and re-layouts  0.96 us (2%)
    pallas_call x9, Pallas kernels, call(): pl.pallas_call(body, out_shape=out_shape, in_specs=[vmem] * len(operands)...  20.8 us
    ppermute x8, starting transfers between devices, summed(): lax.ppermute(value, axis, [(i, i ^ away) for i in range(count)])  14 us
    all_to_all x1, blocking collectives, local(): sums = lax.all_to_all(sums, ('mem', 'lat'), 0, 0, tiled=True)  11.2 us
    ppermute x8, waiting for transfers between devices, summed(): lax.ppermute(value, axis, [(i, i ^ away) for i in range(count)])  1.68 us
    ppermute x1, waiting for transfers between devices, edges(): return [lax.ppermute(edge, 'lat', [(0, 1), (1, 0)])]  1.33 us
  transfers between devices with their start and end apart: 10, of which 3 were waited for; matrix products, arithmetic and copies ran while one was open for 0% of the time, Pallas kernels for 26%

profile of v10, /device:TPU:0, one launch (start us, length us, event | category | flops | bytes accessed | tf_op | source)
XLA Modules:
  0.0 51.6 jit_solution(4095406384225334327)
XLA Ops:
  0.6 0.5 %collective-permute-start = (f32[32,8,512]{2,1,0:T(8,128)}, f32[32,8,512]{2,1,0:T(8,128)S(1)}, u32[]{:S(2)}, u32[]{:S(2)}) collective-permute-start(f32[32,8,512]{2,1,0:T(8,128)} %bitcast.14), channel_id=1, source_target_pairs={{0,1},{1,0},{2,3},{3,2},{4,5},{5,4},{6,7},{7,6},{8,9},{9,8},{10,11... | collective-permute-start | bytes 1572872 | tf_op jit(solution)/shard_map/ppermute | solution.py:419
  1.2 0.9 %copy-done.2 = s32[4,8192]{1,0:T(4,128)S(1)} copy-done((s32[4,8192]{1,0:T(4,128)S(1)}, s32[4,8192]{1,0:T(4,128)}, u32[]{:S(2)}) %copy-start.2) | copy-done | bytes 131096
  2.1 4.2 %shard_map.95 = (s32[4,8192]{1,0:T(4,128)S(1)}, s32[128,128]{1,0:T(8,128)S(1)}, f32[128,128]{1,0:T(8,128)S(1)}, s32[128,128]{1,0:T(8,128)S(1)}, f32[128,128]{1,0...) custom-call(s32[4,8192]{1,0:T(4,128)S(1)} %copy-done.2), custom_call_target="tpu_custom_call" | custom-call | flops 1000000000 | bytes 2097152 | tf_op jit(solution)/shard_map/pallas_call | solution.py:317
  6.4 2.8 %shard_map.96 = (f32[128,128]{1,0:T(8,128)S(1)}, f32[32,8,512]{2,1,0:T(8,128)S(1)}) custom-call(f32[32,8,512]{2,1,0:T(8,128)S(1)} %bitcast.15, bf16[512,512]{1,0:T(8,128)(2,1)S(1)} %copy-done.6, bf16[512,512]{1,0:T(8,128)(2,1)S(1)} %copy-done.7, f32[32,8,512]{2,1,0:T(8,128)S(1)} %collective-permute-done.refs_0_, bf16[4,32,8,512]{3,2,1,0:T(8,128)(2,1)S(1)} %bitcast.10, ...), custom_call_target="tpu_custom_call" | custom-call | flops 1000000000 | bytes 2097152 | tf_op jit(solution)/shard_map/pallas_call | solution.py:317
  9.1 2.6 %collective-permute-start.5 = (f32[128,128]{1,0:T(8,128)S(1)}, f32[128,128]{1,0:T(8,128)S(1)}, u32[]{:S(2)}, u32[]{:S(2)}) collective-permute-start(f32[128,128]{1,0:T(8,128)S(1)} %get-tuple-element.39), channel_id=1, source_target_pairs={{0,2},{2,0},{4,6},{6,4},{8,10},{10,8},{12,14},{14,12},{16,18},{18,... | collective-permute-start | bytes 196616 | tf_op jit(solution)/shard_map/ppermute | solution.py:358
  11.8 2.2 %shard_map.97 = f32[128,128]{1,0:T(8,128)S(1)} custom-call(f32[32,8,512]{2,1,0:T(8,128)S(1)} %get-tuple-element.30.own_ref, bf16[512,512]{1,0:T(8,128)(2,1)S(1)} %copy-done.6, bf16[512,512]{1,0:T(8,128)(2,1)S(1)} %copy-done.7, bf16[4,32,8,512]{3,2,1,0:T(8,128)(2,1)S(1)} %bitcast.11, s32[128,128]{1,0:T(8,128)S(1)} %get-tuple-element.31.refs_1_, ...), custom_call_target="tpu_custom_call" | custom-call | flops 1000000000 | bytes 2097152 | tf_op jit(solution)/shard_map/pallas_call | solution.py:317
  14.0 1.6 %collective-permute-start.1 = (f32[128,128]{1,0:T(8,128)S(1)}, f32[128,128]{1,0:T(8,128)S(1)}, u32[]{:S(2)}, u32[]{:S(2)}) collective-permute-start(f32[128,128]{1,0:T(8,128)S(1)} %shard_map.97), channel_id=1, source_target_pairs={{0,8},{2,10},{4,12},{6,14},{8,0},{10,2},{12,4},{14,6},{16,24},{18,... | collective-permute-start | bytes 196616 | tf_op jit(solution)/shard_map/ppermute | solution.py:358
  15.6 1.6 %collective-permute-start.6 = (f32[128,128]{1,0:T(8,128)S(1)}, f32[128,128]{1,0:T(8,128)S(1)}, u32[]{:S(2)}, u32[]{:S(2)}) collective-permute-start(f32[128,128]{1,0:T(8,128)S(1)} %add.31), channel_id=1, source_target_pairs={{0,4},{2,6},{4,0},{6,2},{8,12},{10,14},{12,8},{14,10},{16,20},{18,... | collective-permute-start | bytes 196616 | tf_op jit(solution)/shard_map/ppermute | solution.py:358
  17.2 1.1 %collective-permute-done.1 = f32[128,128]{1,0:T(8,128)S(1)} collective-permute-done((f32[128,128]{1,0:T(8,128)S(1)}, f32[128,128]{1,0:T(8,128)S(1)}, u32[]{:S(2)}, u32[]{:S(2)}) %collective-permute-start.1) | collective-permute-done | bytes 65568 | tf_op jit(solution)/shard_map/ppermute | solution.py:358
  18.3 2.7 %collective-permute-start.2 = (f32[128,128]{1,0:T(8,128)S(1)}, f32[128,128]{1,0:T(8,128)S(1)}, u32[]{:S(2)}, u32[]{:S(2)}) collective-permute-start(f32[128,128]{1,0:T(8,128)S(1)} %add.27), channel_id=1, source_target_pairs={{0,16},{2,18},{4,20},{6,22},{8,24},{10,26},{12,28},{14,30},{16,0},... | collective-permute-start | bytes 196616 | tf_op jit(solution)/shard_map/ppermute | solution.py:358
  21.1 1.6 %collective-permute-start.7 = (f32[128,128]{1,0:T(8,128)S(1)}, f32[128,128]{1,0:T(8,128)S(1)}, u32[]{:S(2)}, u32[]{:S(2)}) collective-permute-start(f32[128,128]{1,0:T(8,128)S(1)} %add.32), channel_id=1, source_target_pairs={{0,8},{2,10},{4,12},{6,14},{8,0},{10,2},{12,4},{14,6},{16,24},{18,... | collective-permute-start | bytes 196616 | tf_op jit(solution)/shard_map/ppermute | solution.py:358
  22.7 2.3 %shard_map.98 = (f32[128,128]{1,0:T(8,128)S(1)}, f32[128,128]{1,0:T(8,128)S(1)}) custom-call(s32[4,8192]{1,0:T(4,128)S(1)} %get-tuple-element.34.pos_ref, f32[4,8192]{1,0:T(4,128)S(1)} %copy-done.3, f32[4,8192]{1,0:T(4,128)S(1)} %copy-done.4, s32[4,8192]{1,0:T(4,128)S(1)} %copy-done.5), custom_call_target="tpu_custom_call" | custom-call | flops 1000000000 | bytes 2097152 | tf_op jit(solution)/shard_map/pallas_call | solution.py:317
  25.0 0.6 %collective-permute-start.3 = (f32[128,128]{1,0:T(8,128)S(1)}, f32[128,128]{1,0:T(8,128)S(1)}, u32[]{:S(2)}, u32[]{:S(2)}) collective-permute-start(f32[128,128]{1,0:T(8,128)S(1)} %add.28), channel_id=1, source_target_pairs={{0,2},{2,0},{4,6},{6,4},{8,10},{10,8},{12,14},{14,12},{16,18},{18,... | collective-permute-start | bytes 196616 | tf_op jit(solution)/shard_map/ppermute | solution.py:358
  25.7 1.6 %collective-permute-start.8 = (f32[128,128]{1,0:T(8,128)S(1)}, f32[128,128]{1,0:T(8,128)S(1)}, u32[]{:S(2)}, u32[]{:S(2)}) collective-permute-start(f32[128,128]{1,0:T(8,128)S(1)} %add.33), channel_id=1, source_target_pairs={{0,16},{2,18},{4,20},{6,22},{8,24},{10,26},{12,28},{14,30},{16,0},... | collective-permute-start | bytes 196616 | tf_op jit(solution)/shard_map/ppermute | solution.py:358
  27.3 2.3 %shard_map.99 = (f32[128,128]{1,0:T(8,128)S(1)}, f32[128,128]{1,0:T(8,128)S(1)}) custom-call(s32[4,8192]{1,0:T(4,128)S(1)} %get-tuple-element.34.pos_ref, f32[4,8192]{1,0:T(4,128)S(1)} %copy-done.3, f32[4,8192]{1,0:T(4,128)S(1)} %copy-done.4, s32[4,8192]{1,0:T(4,128)S(1)} %copy-done.5), custom_call_target="tpu_custom_call" | custom-call | flops 1000000000 | bytes 2097152 | tf_op jit(solution)/shard_map/pallas_call | solution.py:317
  29.7 1.6 %collective-permute-start.4 = (f32[128,128]{1,0:T(8,128)S(1)}, f32[128,128]{1,0:T(8,128)S(1)}, u32[]{:S(2)}, u32[]{:S(2)}) collective-permute-start(f32[128,128]{1,0:T(8,128)S(1)} %add.29), channel_id=1, source_target_pairs={{0,4},{2,6},{4,0},{6,2},{8,12},{10,14},{12,8},{14,10},{16,20},{18,... | collective-permute-start | bytes 196616 | tf_op jit(solution)/shard_map/ppermute | solution.py:358
  31.2 2.2 %shard_map.100 = (f32[32,8,512]{2,1,0:T(8,128)S(1)}, f32[8,128]{1,0:T(8,128)S(1)}) custom-call(f32[128,128]{1,0:T(8,128)S(1)} %add.34.seen_ref, f32[128,128]{1,0:T(8,128)S(1)} %get-tuple-element.40.want_ref, f32[128,128]{1,0:T(8,128)S(1)} %get-tuple-element.41.keep_ref, s32[128,128]{1,0:T(8,128)S(1)} %get-tuple-element.42.place_ref, ...), custom_call_target="tpu_custom_call" | custom-call | flops 1000000000 | bytes 2097152 | tf_op jit(solution)/shard_map/pallas_call | solution.py:317
  33.4 0.5 %collective-permute-done.4 = f32[128,128]{1,0:T(8,128)S(1)} collective-permute-done((f32[128,128]{1,0:T(8,128)S(1)}, f32[128,128]{1,0:T(8,128)S(1)}, u32[]{:S(2)}, u32[]{:S(2)}) %collective-permute-start.4) | collective-permute-done | bytes 65568 | tf_op jit(solution)/shard_map/ppermute | solution.py:358
  34.0 2.3 %shard_map.101 = (f32[32,8,512]{2,1,0:T(8,128)S(1)}, f32[8,128]{1,0:T(8,128)S(1)}) custom-call(f32[128,128]{1,0:T(8,128)S(1)} %add.30.seen_ref, f32[128,128]{1,0:T(8,128)S(1)} %get-tuple-element.35.want_ref, f32[128,128]{1,0:T(8,128)S(1)} %get-tuple-element.36.keep_ref, s32[128,128]{1,0:T(8,128)S(1)} %get-tuple-element.37.place_ref, ...), custom_call_target="tpu_custom_call" | custom-call | flops 1000000000 | bytes 2097152 | tf_op jit(solution)/shard_map/pallas_call | solution.py:317
  36.3 0.1 collective-permute-start.9
  36.4 1.3 %collective-permute-done.9.refs_0_ = f32[8,8,512]{2,1,0:T(8,128)S(1)} collective-permute-done((f32[8,8,512]{2,1,0:T(8,128)S(1)}, f32[8,8,512]{2,1,0:T(8,128)S(1)}, u32[]{:S(2)}, u32[]{:S(2)}) %collective-permute-start.9) | collective-permute-done | bytes 131104 | tf_op jit(solution)/shard_map/ppermute | solution.py:336
  37.7 1.1 %shard_map.102 = (f32[32,8,512]{2,1,0:T(8,128)S(1)}, f32[32,128]{1,0:T(8,128)S(1)}) custom-call(f32[8,8,512]{2,1,0:T(8,128)S(1)} %collective-permute-done.9.refs_0_, f32[32,8,512]{2,1,0:T(8,128)S(1)} %get-tuple-element.46.refs_1_, bf16[512,512]{1,0:T(8,128)(2,1)S(1)} %copy-done.6, bf16[512,512]{1,0:T(8,128)(2,1)S(1)} %copy-done.7, ...), custom_call_target="tpu_custom_call" | custom-call | flops 1000000000 | bytes 2097152 | tf_op jit(solution)/shard_map/pallas_call | solution.py:317
  38.8 11.2 %all_to_all.11 = f32[32,1,128]{2,1,0:T(1,128)S(1)} all-to-all(f32[32,1,128]{2,1,0:T(1,128)S(1)} %bitcast.8), channel_id=1, replica_groups=mesh['mem'=16,'lat'=2] {'mem','lat'}, dimensions={0} | all-to-all | bytes 32768 | tf_op jit(solution)/shard_map/all_to_all | solution.py:434
  50.0 1.4 %shard_map.103 = (f32[32,8,512]{2,1,0:T(8,128)}, f32[1,1]{1,0:T(1,128)}) custom-call(f32[32,128]{1,0:T(8,128)S(1)} %bitcast.9, f32[32,8,512]{2,1,0:T(8,128)S(1)} %bitcast.17, f32[32,8,512]{2,1,0:T(8,128)S(1)} %get-tuple-element.49.grad_ref), custom_call_target="tpu_custom_call" | custom-call | flops 1000000000 | bytes 2097152 | tf_op jit(solution)/shard_map/pallas_call | solution.py:317
  (31 shorter events, 0.2 us)
Async XLA Ops:
  0.6 5.7 %copy-start = (bf16[1,4,32,8,512]{4,3,2,1,0:T(8,128)(2,1)S(1)}, bf16[1,4,32,8,512]{4,3,2,1,0:T(8,128)(2,1)}, u32[]{:S(2)}) copy-start(bf16[1,4,32,8,512]{4,3,2,1,0:T(8,128)(2,1)} %param.8) | copy-start | bytes 3145732
  0.6 5.7 %copy-start.1 = (f32[1,32,8,512]{3,2,1,0:T(8,128)S(1)}, f32[1,32,8,512]{3,2,1,0:T(8,128)}, u32[]{:S(2)}) copy-start(f32[1,32,8,512]{3,2,1,0:T(8,128)} %param.9) | copy-start | bytes 1572868
  0.6 5.7 %collective-permute-start = (f32[32,8,512]{2,1,0:T(8,128)}, f32[32,8,512]{2,1,0:T(8,128)S(1)}, u32[]{:S(2)}, u32[]{:S(2)}) collective-permute-start(f32[32,8,512]{2,1,0:T(8,128)} %bitcast.14), channel_id=1, source_target_pairs={{0,1},{1,0},{2,3},{3,2},{4,5},{5,4},{6,7},{7,6},{8,9},{9,8},{10,11... | collective-permute-start | bytes 1572872 | tf_op jit(solution)/shard_map/ppermute | solution.py:419
  1.2 0.9 %copy-start.2 = (s32[4,8192]{1,0:T(4,128)S(1)}, s32[4,8192]{1,0:T(4,128)}, u32[]{:S(2)}) copy-start(s32[4,8192]{1,0:T(4,128)} %cell_ref.1) | copy-start | bytes 393220
  2.1 4.3 %copy-start.6 = (bf16[512,512]{1,0:T(8,128)(2,1)S(1)}, bf16[512,512]{1,0:T(8,128)(2,1)}, u32[]{:S(2)}) copy-start(bf16[512,512]{1,0:T(8,128)(2,1)} %constant.16.clone.circ_high_ref.refs_2_) | copy-start | bytes 1572868
  2.1 4.3 %copy-start.7 = (bf16[512,512]{1,0:T(8,128)(2,1)S(1)}, bf16[512,512]{1,0:T(8,128)(2,1)}, u32[]{:S(2)}) copy-start(bf16[512,512]{1,0:T(8,128)(2,1)} %constant.17.clone.circ_low_ref.refs_3_) | copy-start | bytes 1572868
  9.1 6.5 %collective-permute-start.5 = (f32[128,128]{1,0:T(8,128)S(1)}, f32[128,128]{1,0:T(8,128)S(1)}, u32[]{:S(2)}, u32[]{:S(2)}) collective-permute-start(f32[128,128]{1,0:T(8,128)S(1)} %get-tuple-element.39), channel_id=1, source_target_pairs={{0,2},{2,0},{4,6},{6,4},{8,10},{10,8},{12,14},{14,12},{16,18},{18,... | collective-permute-start | bytes 196616 | tf_op jit(solution)/shard_map/ppermute | solution.py:358
  14.0 4.3 %collective-permute-start.1 = (f32[128,128]{1,0:T(8,128)S(1)}, f32[128,128]{1,0:T(8,128)S(1)}, u32[]{:S(2)}, u32[]{:S(2)}) collective-permute-start(f32[128,128]{1,0:T(8,128)S(1)} %shard_map.97), channel_id=1, source_target_pairs={{0,8},{2,10},{4,12},{6,14},{8,0},{10,2},{12,4},{14,6},{16,24},{18,... | collective-permute-start | bytes 196616 | tf_op jit(solution)/shard_map/ppermute | solution.py:358
  15.6 5.4 %collective-permute-start.6 = (f32[128,128]{1,0:T(8,128)S(1)}, f32[128,128]{1,0:T(8,128)S(1)}, u32[]{:S(2)}, u32[]{:S(2)}) collective-permute-start(f32[128,128]{1,0:T(8,128)S(1)} %add.31), channel_id=1, source_target_pairs={{0,4},{2,6},{4,0},{6,2},{8,12},{10,14},{12,8},{14,10},{16,20},{18,... | collective-permute-start | bytes 196616 | tf_op jit(solution)/shard_map/ppermute | solution.py:358
  18.3 4.4 %copy-start.4 = (f32[4,8192]{1,0:T(4,128)S(1)}, f32[4,8192]{1,0:T(4,128)}, u32[]{:S(2)}) copy-start(f32[4,8192]{1,0:T(4,128)} %weight_ref.3) | copy-start | bytes 393220
  18.3 4.4 %copy-start.5 = (s32[4,8192]{1,0:T(4,128)S(1)}, s32[4,8192]{1,0:T(4,128)}, u32[]{:S(2)}) copy-start(s32[4,8192]{1,0:T(4,128)} %quality_ref.3) | copy-start | bytes 393220
  18.3 4.3 %copy-start.3 = (f32[4,8192]{1,0:T(4,128)S(1)}, f32[4,8192]{1,0:T(4,128)}, u32[]{:S(2)}) copy-start(f32[4,8192]{1,0:T(4,128)} %innov_ref.3) | copy-start | bytes 393220
  18.3 6.7 %collective-permute-start.2 = (f32[128,128]{1,0:T(8,128)S(1)}, f32[128,128]{1,0:T(8,128)S(1)}, u32[]{:S(2)}, u32[]{:S(2)}) collective-permute-start(f32[128,128]{1,0:T(8,128)S(1)} %add.27), channel_id=1, source_target_pairs={{0,16},{2,18},{4,20},{6,22},{8,24},{10,26},{12,28},{14,30},{16,0},... | collective-permute-start | bytes 196616 | tf_op jit(solution)/shard_map/ppermute | solution.py:358
  21.1 4.6 %collective-permute-start.7 = (f32[128,128]{1,0:T(8,128)S(1)}, f32[128,128]{1,0:T(8,128)S(1)}, u32[]{:S(2)}, u32[]{:S(2)}) collective-permute-start(f32[128,128]{1,0:T(8,128)S(1)} %add.32), channel_id=1, source_target_pairs={{0,8},{2,10},{4,12},{6,14},{8,0},{10,2},{12,4},{14,6},{16,24},{18,... | collective-permute-start | bytes 196616 | tf_op jit(solution)/shard_map/ppermute | solution.py:358
  25.0 4.6 %collective-permute-start.3 = (f32[128,128]{1,0:T(8,128)S(1)}, f32[128,128]{1,0:T(8,128)S(1)}, u32[]{:S(2)}, u32[]{:S(2)}) collective-permute-start(f32[128,128]{1,0:T(8,128)S(1)} %add.28), channel_id=1, source_target_pairs={{0,2},{2,0},{4,6},{6,4},{8,10},{10,8},{12,14},{14,12},{16,18},{18,... | collective-permute-start | bytes 196616 | tf_op jit(solution)/shard_map/ppermute | solution.py:358
  25.7 5.5 %collective-permute-start.8 = (f32[128,128]{1,0:T(8,128)S(1)}, f32[128,128]{1,0:T(8,128)S(1)}, u32[]{:S(2)}, u32[]{:S(2)}) collective-permute-start(f32[128,128]{1,0:T(8,128)S(1)} %add.33), channel_id=1, source_target_pairs={{0,16},{2,18},{4,20},{6,22},{8,24},{10,26},{12,28},{14,30},{16,0},... | collective-permute-start | bytes 196616 | tf_op jit(solution)/shard_map/ppermute | solution.py:358
  29.7 4.3 %collective-permute-start.4 = (f32[128,128]{1,0:T(8,128)S(1)}, f32[128,128]{1,0:T(8,128)S(1)}, u32[]{:S(2)}, u32[]{:S(2)}) collective-permute-start(f32[128,128]{1,0:T(8,128)S(1)} %add.29), channel_id=1, source_target_pairs={{0,4},{2,6},{4,0},{6,2},{8,12},{10,14},{12,8},{14,10},{16,20},{18,... | collective-permute-start | bytes 196616 | tf_op jit(solution)/shard_map/ppermute | solution.py:358
  36.3 1.4 %collective-permute-start.9 = (f32[8,8,512]{2,1,0:T(8,128)S(1)}, f32[8,8,512]{2,1,0:T(8,128)S(1)}, u32[]{:S(2)}, u32[]{:S(2)}) collective-permute-start(f32[8,8,512]{2,1,0:T(8,128)S(1)} %constant_dynamic-slice_fusion), channel_id=1, source_target_pairs={{0,1},{1,0},{2,3},{3,2},{4,5},{5,4},{6,7},{7,6},{8,9},{9,8},{10,11... | collective-permute-start | bytes 393224 | tf_op jit(solution)/shard_map/ppermute | solution.py:336
